TPU v7x, 32 devices: a whole 2x2x4 slice. The times are simulated.
32 devices in a mesh: expert: 16 (over z, y, x), tensor: 2 (over core).
Axes of the slice: x: 2, y: 2, z: 4, core: 2. Of those that a mesh axis runs over, the one named last changes fastest.
Arguments:
- first_half: bfloat16 [2048, 2048], P('expert', 'tensor'), may hold values from -6 to 6
- second_half: bfloat16 [2048, 2048], P('expert', 'tensor'), may hold values from -1.5 to 1.5
- first_grad: bfloat16 [2048, 2048], P('expert', 'tensor'), may hold values from -1.5 to 1.5
- second_grad: bfloat16 [2048, 2048], P('expert', 'tensor'), may hold values from -6 to 6
- expert_ids: int32 [2048, 6], P('expert'), may hold values from 0 to 15, as said below
- gate_weights: bfloat16 [2048, 6], P('expert'), may hold values from 0.049804688 to 0.5
- expert_in: bfloat16 [16, 2, 1408, 2048], P('expert', None, 'tensor'), may hold values from -0.125 to 0.125
- expert_out: bfloat16 [16, 1408, 2048], P('expert', 'tensor'), may hold values from -0.15625 to 0.15625
Outputs:
- restored: bfloat16 [2048, 2048], P('expert', 'tensor')
- carried_grad: bfloat16 [2048, 2048], P('expert', 'tensor')
- gate_grad: float32 [2048, 6], P('expert')
- grad_in: bfloat16 [16, 2, 1408, 2048], P('expert', None, 'tensor')
- grad_out: bfloat16 [16, 1408, 2048], P('expert', 'tensor')
Inputs may be any that keep to these rules, and one draw needn't show every extreme that they name: `expert_ids`: each token names 6 different experts. In the rows of one index of expert (128 tokens) each expert is named by at least 40 and at most 56 tokens, and one expert is named by exactly 56 tokens of every index of expert.
All inputs are finite; a program needn't handle non-finite values.
Results may differ from a plain program's by a relative error of at most 0.02.
Values may be sent and summed in bfloat16 or wider, within the bound.
No kernel may reach another device: no remote copies, remote signals or barrier semaphores. Data moves between devices by JAX's collectives and lax.ppermute only.
A program may use at most 128 MiB of HBM per device.

v0:
```python
import functools

import jax
import jax.numpy as jnp
from jax import lax
from jax.experimental import pallas as pl
from jax.experimental.pallas import tpu as pltpu
from jax.sharding import PartitionSpec as P

PLANE = 4
CHUNKS = 1
RETURNS = 2
TAIL = 16
VMEM_LIMIT = 56 * 1024 * 1024
F32 = jnp.float32
BF16 = jnp.bfloat16


def dot_nn(a, b):
    return lax.dot_general(a, b, (((1,), (0,)), ((), ())), preferred_element_type=F32)


def dot_nt(a, b):
    return lax.dot_general(a, b, (((1,), (1,)), ((), ())), preferred_element_type=F32)


def dot_tn(a, b):
    return lax.dot_general(a, b, (((0,), (0,)), ((), ())), preferred_element_type=F32)


def iota(shape, axis):
    return lax.broadcasted_iota(jnp.int32, shape, axis)


SMEM = pl.BlockSpec(memory_space=pltpu.SMEM)
VMEM = pl.BlockSpec(memory_space=pltpu.VMEM)
HBM = pl.BlockSpec(memory_space=pl.ANY)


def call(kernel, outs, args, specs, out_specs=None, scratch=(), name=None):
    return pl.pallas_call(
        kernel,
        out_shape=outs,
        in_specs=specs,
        out_specs=out_specs if out_specs is not None else [VMEM] * len(outs),
        scratch_shapes=list(scratch),
        compiler_params=pltpu.CompilerParams(vmem_limit_bytes=VMEM_LIMIT),
        cost_estimate=pl.CostEstimate(flops=1024, bytes_accessed=1024, transcendentals=0),
        name=name,
    )(*args)


def shape(*dims, dtype=BF16):
    return jax.ShapeDtypeStruct(dims, dtype)


def outer_meta(info, meta, s, zn):
    return meta[lax.rem(info[3] - s + zn, zn)]


def select(info, meta, sels, zn, pn, tokens, picks, rows):
    zc = zn // CHUNKS
    cap = rows // zc
    partner = iota((8, 1), 0)
    experts = jnp.where(partner < pn, info[0] + (partner ^ info[1]), -2).astype(F32)
    before = (iota((tokens, tokens), 0) < iota((tokens, tokens), 1)).astype(F32).astype(BF16)
    slot = iota((rows, tokens), 0).astype(F32)
    for s in range(zn):
        g, local = divmod(s, zc)
        ids = outer_meta(info, meta, s, zn)
        named = jnp.zeros((8, tokens), F32)
        for k in range(picks):
            named += (ids[k : k + 1, :] == experts).astype(F32)
        dest = dot_nn(named.astype(BF16), before) + local * cap
        dest = jnp.where(named > 0, dest, -1.0)
        for q in range(pn):
            sels[g][q * rows : (q + 1) * rows, local * tokens : (local + 1) * tokens] = (
                (slot == dest[q : q + 1, :]).astype(F32).astype(BF16)
            )


def route_kernel(info, meta, *chosen, zn, pn, tokens, picks, cap):
    zr = zn // RETURNS
    rows = zr * cap
    partner = iota((1, 8), 1)
    experts = jnp.where(partner < pn, info[0] + (partner ^ info[1]), -2).astype(F32)
    after = (iota((tokens, tokens), 1) < iota((tokens, tokens), 0)).astype(F32).astype(BF16)
    eye = (iota((16, 16), 0) == iota((16, 16), 1)).astype(F32).astype(BF16)
    lane = iota((tokens, pn * rows), 1).astype(F32)
    for s in range(zn):
        g, local = divmod(s, zr)
        columned = dot_tn(outer_meta(info, meta, s, zn).astype(BF16), eye)
        named = jnp.zeros((tokens, 8), F32)
        for k in range(picks):
            named += (columned[:, k : k + 1] == experts).astype(F32)
        dest = dot_nn(after, named.astype(BF16)) + local * cap
        dest = jnp.where(named > 0, dest + rows * partner.astype(F32), -1.0)
        picked = jnp.zeros((tokens, pn * rows), F32)
        for q in range(pn):
            picked += (lane == dest[:, q : q + 1]).astype(F32)
        chosen[g][local * tokens : (local + 1) * tokens, :] = picked.astype(BF16)


def tail_lanes(rows):
    return -(-rows // 128) * 128


class Loads:
    def __init__(self, sems):
        self.sems, self.copies, self.waited = sems, {}, set()

    def add(self, key, source, target):
        assert key not in self.copies
        self.copies[key] = pltpu.make_async_copy(source, target, self.sems.at[len(self.copies)])
        self.copies[key].start()

    def need(self, *keys):
        for key in keys:
            if key not in self.waited:
                self.waited.add(key)
                self.copies[key].wait()

    def finish(self):
        self.need(*self.copies)


def pack_kernel(info, sel, source, *refs, zn, pn, tokens, rows):
    outs, whole, sems = refs[:pn], refs[-2], refs[-1]
    loads = Loads(sems)
    for s in range(zn):
        place = lax.rem(info[3] - s + zn, zn)
        loads.add(s, source.at[place], whole.at[pl.ds(s * tokens, tokens)])
    loads.finish()
    for q in range(pn):
        outs[q][...] = dot_nn(sel[q * rows : (q + 1) * rows, :], whole[...]).astype(BF16)


def pack_gates_kernel(info, meta, *refs, zn, pn, tokens, picks, rows):
    zc = zn // CHUNKS
    sources, outs, refs = refs[:zc], refs[zc : zc + pn], refs[zc + pn :]
    sels, (whole, sems) = refs[:CHUNKS], refs[CHUNKS:]
    loads = Loads(sems)
    for s in range(zc):
        loads.add(s, sources[s], whole.at[pl.ds(s * tokens, tokens)])
    select(info, meta, sels, zn, pn, tokens, picks, rows)
    for q in range(pn):
        expert = (info[0] + (info[1] ^ q)).astype(F32)
        outs[q][rows : rows + TAIL, :] = jnp.zeros((TAIL, outs[q].shape[1]), BF16)
        for g in range(CHUNKS):
            tail = jnp.zeros((TAIL, rows), F32)
            for local in range(zc):
                known = outer_meta(info, meta, g * zc + local, zn)
                gate = jnp.zeros((1, tokens), F32)
                for k in range(picks):
                    gate += jnp.where(known[k : k + 1, :] == expert, known[8 + k : 9 + k, :], 0.0)
                gate = jnp.broadcast_to(gate, (TAIL, tokens)).astype(BF16)
                here = slice(local * tokens, (local + 1) * tokens)
                tail += dot_nt(gate, sels[g][q * rows : (q + 1) * rows, here])
            at = g * tail_lanes(rows)
            outs[q][rows : rows + TAIL, at : at + rows] = tail.astype(BF16)
    loads.finish()
    for q in range(pn):
        chosen = sels[0][q * rows : (q + 1) * rows, :]
        outs[q][0:rows, :] = dot_nn(chosen, whole[...]).astype(BF16)


def combine_kernel(info, *refs, zn, pn, tokens, rows):
    zr = zn // RETURNS
    chosen, backs = refs[:RETURNS], refs[RETURNS : RETURNS + pn]
    out, whole, sems = refs[RETURNS + pn :]
    loads = Loads(sems)
    for g in range(RETURNS):
        for q in range(pn):
            to = whole.at[g, pl.ds(q * rows, rows)]
            loads.add((g, q), backs[q].at[pl.ds(g * rows, rows)], to)
    for g in range(RETURNS):
        loads.need(*((g, q) for q in range(pn)))
        part = dot_nn(chosen[g][...], whole[g]).astype(BF16)
        for local in range(zr):
            place = lax.rem(info[3] - (g * zr + local) + zn, zn)
            out[place] = part[local * tokens : (local + 1) * tokens, :]


def combine_far_kernel(info, meta, sel, chosen, *refs, zn, pn, tokens, rows):
    zr, slots = zn // RETURNS, RETURNS * rows
    backs, outs, (gates, whole, tails, sems) = refs[:pn], refs[pn:-4], refs[-4:]
    loads = Loads(sems)
    for q in range(pn):
        loads.add(("t", q), backs[q].at[pl.ds(rows, TAIL)], tails.at[q])
        loads.add(q, backs[q].at[pl.ds(0, rows)], whole.at[pl.ds(q * rows, rows)])
    spreads = []
    for q in range(pn):
        loads.need(("t", q))
        spreads.append(dot_nn(tails[q, :, 0:slots], sel[q * slots : (q + 1) * slots, :])[0:8, :])
    for s in range(zn):
        ids = outer_meta(info, meta, s, zn)[0:8, :]
        total = jnp.zeros((8, tokens), F32)
        for q in range(pn):
            expert = (info[0] + (info[1] ^ q)).astype(F32)
            total += jnp.where(ids == expert, spreads[q][:, s * tokens : (s + 1) * tokens], 0.0)
        total = jnp.concatenate([total, jnp.zeros((TAIL - 8, tokens), F32)], axis=0)
        gates[:, s * tokens : (s + 1) * tokens] = total.astype(BF16)
    loads.finish()
    finish_combine(chosen, whole, gates, outs, zn - zr, tokens)


def combine_near_kernel(gates, chosen, *refs, pn, tokens, rows):
    backs, outs, (whole, sems) = refs[:pn], refs[pn:-2], refs[-2:]
    loads = Loads(sems)
    for q in range(pn):
        loads.add(q, backs[q], whole.at[pl.ds(q * rows, rows)])
    loads.finish()
    finish_combine(chosen, whole, gates, outs, 0, tokens)


def finish_combine(chosen, whole, gates, outs, first, tokens):
    part = dot_nn(chosen[...], whole[...]).astype(BF16)
    for local, out in enumerate(outs):
        at = first + local
        out[0:tokens, :] = part[local * tokens : (local + 1) * tokens, :]
        out[tokens : tokens + TAIL, :] = jnp.zeros((TAIL, part.shape[1]), BF16)
        out[tokens : tokens + TAIL, 0:tokens] = gates[:, at * tokens : (at + 1) * tokens]


def column_block(info, j, nt, cols):
    block = lax.rem(info[2] - j + nt, nt)
    return pl.ds(pl.multiple_of(block * cols, 128), cols)


def load_weight(loads, info, kind, source, target, blocks, nt, cols):
    for at, j in enumerate(blocks):
        block = source.at[:, column_block(info, j, nt, cols)]
        loads.add((kind, j), block, target.at[:, pl.ds(at * cols, cols)])


def by_core(refs, nt, pn):
    return [refs[j * pn : (j + 1) * pn] for j in range(nt)]


def load_chunk(loads, sources, target, g, pn, rows, cols):
    for j, pieces in enumerate(sources):
        for q in range(pn):
            to = target.at[pl.ds((g * pn + q) * rows, rows), pl.ds(j * cols, cols)]
            loads.add(("r", g, j, q), pieces[g * pn + q].at[pl.ds(0, rows)], to)


def halves(pn):
    units = [(g, q) for g in range(CHUNKS) for q in range(pn)]
    return units[: len(units) // 2], units[len(units) // 2 :]


def forward_kernel(info, *refs, nt, pn, rows, cols):
    n = CHUNKS * pn
    xs, refs = by_core(refs, nt, n), refs[nt * n :]
    (win, wout), outs, refs = refs[:2], by_core(refs[2:], nt, pn), refs[2 + nt * pn :]
    results, (x, tails, wg, wu, wd, kept, stage, in_sems, out_sems) = refs[:4], refs[4:]
    hs, hid, a1, a2 = (kept.at[i] for i in range(4))
    loads, stores = Loads(in_sems), Loads(out_sems)
    every = range(nt)
    load_chunk(loads, xs, x, 0, pn, rows, cols)
    load_weight(loads, info, "g", win.at[0, 0], wg, every, nt, cols)
    load_weight(loads, info, "u", win.at[0, 1], wu, every, nt, cols)
    for q in range(pn):
        loads.add(("t", q), xs[0][q].at[pl.ds(rows, TAIL)], tails.at[q])
    for g in range(1, CHUNKS):
        load_chunk(loads, xs, x, g, pn, rows, cols)
    load_weight(loads, info, "d", wout.at[0], wd, every, nt, cols)
    same = iota((rows, rows), 0) == iota((rows, rows), 1)
    tail_step = tail_lanes(rows)
    for b, units in enumerate(halves(pn)):
        here = slice(b * len(units) * rows, (b + 1) * len(units) * rows)
        loads.need(*(("r", g, j, q) for j in every for g, q in units))
        loads.need(*(("g", j) for j in every))
        gate = dot_nt(x[here, :], wg[...])
        loads.need(*(("u", j) for j in every), *(("t", q) for q in range(pn)))
        up = dot_nt(x[here, :], wu[...])
        columns = []
        for g, q in units:
            row = tails[q, :, g * tail_step : g * tail_step + rows].astype(F32)[0:1, :]
            columns.append(jnp.sum(jnp.where(same, row, 0.0), axis=1, keepdims=True))
        weight = jnp.concatenate(columns, axis=0)
        sigma = 0.5 * jnp.tanh(0.5 * gate) + 0.5
        active = gate * sigma
        hidden = active * up
        scaled = (weight * hidden).astype(BF16)
        hs[here, :] = scaled
        hid[here, :] = hidden.astype(BF16)
        a1[here, :] = (weight * (up * sigma * (1.0 + gate * (1.0 - sigma)))).astype(BF16)
        a2[here, :] = (weight * active).astype(BF16)
        span = pl.ds(b * len(units) * rows, len(units) * rows)
        for i, result in enumerate(results):
            stores.add(("kept", b, i), kept.at[i, span], result.at[span])
        loads.need(*(("d", j) for j in every))
        part = dot_nn(scaled, wd[...]).astype(BF16)
        for j in reversed(every):
            w = (nt - j) % nt
            for u, (g, q) in enumerate(units):
                block = part[u * rows : (u + 1) * rows, w * cols : (w + 1) * cols]
                stage[j, q, g * rows : (g + 1) * rows, :] = block
                if g == CHUNKS - 1:
                    stores.add((j, q), stage.at[j, q], outs[j][q])
    loads.finish()
    stores.finish()


def backward_kernel(info, *refs, nt, pn, rows, cols):
    n = CHUNKS * pn
    cs, refs = by_core(refs, nt, n), refs[nt * n :]
    n_out = RETURNS * nt * pn
    (win, wout, hid, a1, a2), outs, refs = refs[:5], refs[5 : 5 + n_out], refs[5 + n_out :]
    outs = [by_core(outs[r * nt * pn :], nt, pn) for r in range(RETURNS)]
    half = CHUNKS * rows // RETURNS
    results, (c, h, b1, b2, wg, wu, wd, kept, stage, in_sems, out_sems) = refs[:2], refs[2:]
    gg, ug = kept.at[0], kept.at[1]
    loads, stores = Loads(in_sems), Loads(out_sems)
    every = range(nt)
    load_chunk(loads, cs, c, 0, pn, rows, cols)
    load_weight(loads, info, "d", wout.at[0], wd, every, nt, cols)
    for key, source, target in (("h", hid, h), ("1", a1, b1), ("2", a2, b2)):
        loads.add(key, source, target)
    load_weight(loads, info, "g", win.at[0, 0], wg, every, nt, cols)
    load_weight(loads, info, "u", win.at[0, 1], wu, every, nt, cols)
    for g in range(1, CHUNKS):
        load_chunk(loads, cs, c, g, pn, rows, cols)
    same = iota((rows, rows), 0) == iota((rows, rows), 1)
    tail_step = tail_lanes(rows)
    bottom = slice(CHUNKS * rows, CHUNKS * rows + TAIL)
    for b, units in enumerate(halves(pn)):
        here = slice(b * len(units) * rows, (b + 1) * len(units) * rows)
        loads.need(*(("r", g, j, q) for j in every for g, q in units))
        loads.need(*(("d", j) for j in every))
        grad = dot_nt(c[here, :], wd[...])
        loads.need("h", "1", "2")
        piece = jnp.sum(grad * h[here, :].astype(F32), axis=1, keepdims=True)
        gate_grad = (grad * b1[here, :].astype(F32)).astype(BF16)
        up_grad = (grad * b2[here, :].astype(F32)).astype(BF16)
        gg[here, :] = gate_grad
        ug[here, :] = up_grad
        span = pl.ds(b * len(units) * rows, len(units) * rows)
        for i, result in enumerate(results):
            stores.add(("kept", b, i), kept.at[i, span], result.at[span])
        for u, (g, q) in enumerate(units):
            part = piece[u * rows : (u + 1) * rows, :]
            part = jnp.sum(jnp.where(same, part, 0.0), axis=0, keepdims=True)
            part = jnp.broadcast_to(part, (TAIL, rows)).astype(BF16)
            for j in every:
                if g == 0:
                    stage[j, q, bottom, :] = jnp.zeros((TAIL, cols), BF16)
                stage[j, q, bottom, g * tail_step : g * tail_step + rows] = part
        loads.need(*((k, j) for k in "gu" for j in every))
        part = (dot_nn(gate_grad, wg[...]) + dot_nn(up_grad, wu[...])).astype(BF16)
        for j in reversed(every):
            w = (nt - j) % nt
            for u, (g, q) in enumerate(units):
                block = part[u * rows : (u + 1) * rows, w * cols : (w + 1) * cols]
                stage[j, q, g * rows : (g + 1) * rows, :] = block
                for r in reversed(range(RETURNS if g == CHUNKS - 1 else 0)):
                    span = pl.ds(r * half, half + TAIL if r == RETURNS - 1 else half)
                    stores.add((j, q, r), stage.at[j, q, span], outs[r][j][q])
    loads.finish()
    stores.finish()


def weights_kernel(info, *refs, nt, pn, rows, cols):
    n = CHUNKS * pn
    xs, cs, refs = by_core(refs, nt, n), by_core(refs[nt * n :], nt, n), refs[2 * nt * n :]
    lefts, (gin, gout, left, right, stage, in_sems, out_sems) = refs[:3], refs[3:]
    loads, stores = Loads(in_sems), Loads(out_sems)
    order = ((0, 0, xs), (1, 0, xs), (2, 1, cs))
    for w, side, sources in order:
        loads.add(("l", w), lefts[w], left.at[w])
        if w == 1:
            continue
        for j in range(nt):
            for q in range(n):
                target = right.at[side, j, pl.ds(q * rows, rows)]
                loads.add((side, j, q), sources[j][q].at[pl.ds(0, rows)], target)
    for w, side, _ in order:
        loads.need(("l", w))
        for j in range(nt):
            loads.need(*((side, j, q) for q in range(n)))
            at = column_block(info, j, nt, cols)
            stage[j, w] = dot_tn(left[w], right[side, j]).astype(BF16)
            target = gout.at[0, :, at] if w == 2 else gin.at[0, w, :, at]
            stores.add((j, w), stage.at[j, w], target)
    loads.finish()
    stores.finish()


def after(value, *others):
    return lax.optimization_barrier((value, *others))[0]


def body(
    first_half,
    second_half,
    first_grad,
    second_grad,
    expert_ids,
    gate_weights,
    expert_in,
    expert_out,
):
    tokens, picks = expert_ids.shape
    groups = lax.axis_size("expert")
    nt = lax.axis_size("tensor")
    pn = PLANE
    zn = groups // pn
    cap = tokens * picks * 7 // (6 * groups)
    zc = zn // CHUNKS
    part_rows = zc * cap
    rows = CHUNKS * part_rows
    slots = pn * rows
    cols = first_half.shape[1]
    hid_n = expert_out.shape[1]
    me = lax.axis_index("expert")
    info = jnp.stack([(me // pn) * pn, me % pn, lax.axis_index("tensor"), me // pn]).astype(jnp.int32)

    def outer_send(value, s):
        if s % zn == 0:
            return value
        return lax.ppermute(
            value, "expert", [(e, ((e // pn + s) % zn) * pn + e % pn) for e in range(groups)]
        )

    def inner_send(value, q):
        if q == 0:
            return value
        return lax.ppermute(value, "expert", [(e, e ^ q) for e in range(groups)])

    def inner_exchange(pieces):
        return [inner_send(piece, q) for q, piece in enumerate(pieces)]

    def tensor_send(value, j):
        if j == 0:
            return value
        return lax.ppermute(value, "tensor", [(c, (c + j) % nt) for c in range(nt)])

    fixed = dict(zn=zn, pn=pn, tokens=tokens)

    own = jnp.concatenate(
        [
            jnp.pad(expert_ids.T.astype(F32), ((0, 8 - picks), (0, 0)), constant_values=-1.0),
            jnp.pad(gate_weights.T.astype(F32), ((0, 8 - picks), (0, 0))),
        ],
        axis=0,
    )
    columns = [[z * pn + q for z in range(zn)] for q in range(pn)]

    def outer_exchange(value):
        return lax.all_to_all(
            value,
            "expert",
            split_axis=0,
            concat_axis=0,
            axis_index_groups=columns,
            tiled=True,
        )

    def copies(value):
        return jnp.broadcast_to(value[None], (zn,) + value.shape)

    grad_copies = copies(second_grad)
    meta = outer_exchange(after(copies(own), grad_copies))
    dma = pltpu.SemaphoreType.DMA
    sizes = dict(nt=nt, pn=pn, rows=part_rows, cols=cols)

    def pack(gathered):
        return call(
            functools.partial(pack_kernel, **fixed, rows=part_rows),
            [shape(part_rows, cols)] * pn,
            [info, sels[0], gathered],
            [SMEM, VMEM, HBM],
            scratch=[pltpu.VMEM((zn * tokens, cols), BF16), dma((zn,))],
            name="pack",
        )

    def pack_gates(parts):
        return call(
            functools.partial(pack_gates_kernel, **fixed, picks=picks, rows=part_rows),
            [shape(part_rows + TAIL, cols)] * pn
            + [shape(pn * part_rows, zc * tokens)] * CHUNKS,
            [info, meta, *parts[:zc]],
            [SMEM, VMEM] + [HBM] * zc,
            scratch=[pltpu.VMEM((zc * tokens, cols), BF16), dma((zc,))],
            name="pack_gates",
        )

    zr = zn // RETURNS
    half = zr * cap

    def send_back(parts, first):
        return [outer_send(part, -(first + local)) for local, part in enumerate(parts)]

    def combine(backs):
        parts = call(
            functools.partial(combine_kernel, **fixed, rows=half),
            [shape(zn, tokens, cols)],
            [info, *chosen, *backs],
            [SMEM] + [VMEM] * RETURNS + [HBM] * pn,
            scratch=[pltpu.VMEM((RETURNS, pn * half, cols), BF16), dma((RETURNS * pn,))],
            name="combine",
        )
        return parts[0]

    def combine_far(backs):
        *parts, gates = call(
            functools.partial(combine_far_kernel, **fixed, rows=half),
            [shape(tokens + TAIL, cols)] * zr + [shape(TAIL, zn * tokens)],
            [info, meta, sels[0], chosen[RETURNS - 1], *backs],
            [SMEM] + [VMEM] * 3 + [HBM] * pn,
            scratch=[pltpu.VMEM((pn * half, cols), BF16), pltpu.VMEM((pn, TAIL, cols), BF16)]
            + [dma((2 * pn,))],
            name="combine_far",
        )
        return send_back(parts, zn - zr), gates

    def combine_near(gates, backs):
        parts = call(
            functools.partial(combine_near_kernel, pn=pn, tokens=tokens, rows=half),
            [shape(tokens + TAIL, cols)] * zr,
            [gates, chosen[0], *backs],
            [VMEM] * 2 + [HBM] * pn,
            scratch=[pltpu.VMEM((pn * half, cols), BF16), dma((pn,))],
            name="combine_near",
        )
        return send_back(parts, 0)

    def swapped(chunks):
        return [tensor_send(piece, j) for j in range(nt) for pieces in chunks for piece in pieces]

    def core_sum(arrays):
        sums = []
        for q in range(pn):
            total = sum(tensor_send(arrays[j * pn + q], j).astype(F32) for j in range(nt))
            sums.append(total.astype(BF16))
        return sums

    x_parts = [outer_send(first_half, s) for s in range(zn)]
    x_packed = pack_gates(x_parts)
    x_packed, sels = x_packed[:pn], x_packed[pn:]
    x_here = inner_exchange(x_packed)
    gathered = outer_exchange(after(grad_copies, *x_parts[1:]))
    chosen = call(
        functools.partial(route_kernel, **fixed, picks=picks, cap=cap),
        [shape(zr * tokens, pn * half)] * RETURNS,
        [info, after(meta, *x_packed)],
        [SMEM, VMEM],
        name="route",
    )
    c_packed = pack(after(gathered, *chosen))
    c_here = inner_exchange(c_packed)

    xs = swapped(([after(piece, *c_packed) for piece in x_here],))
    pieces = nt * CHUNKS * pn
    forward = call(
        functools.partial(forward_kernel, **sizes),
        [shape(rows, cols)] * (nt * pn) + [shape(slots, hid_n)] * 4,
        [after(info, *c_packed), *xs, expert_in, expert_out],
        [SMEM] + [HBM] * (pieces + 2),
        out_specs=[HBM] * (nt * pn + 4),
        scratch=[pltpu.VMEM((slots, nt * cols), BF16), pltpu.VMEM((pn, TAIL, cols), BF16)]
        + [pltpu.VMEM((hid_n, nt * cols), BF16)] * 3
        + [pltpu.VMEM((4, slots, hid_n), BF16)]
        + [pltpu.VMEM((nt, pn, rows, cols), BF16), dma((3 * nt + pieces + pn,))]
        + [dma((nt * pn + 8,))],
        name="expert_forward",
    )
    outs, (hs, hid, a1, a2) = forward[: nt * pn], forward[nt * pn :]
    cs = swapped(([after(piece, hid) for piece in c_here],))
    out_here = core_sum(outs)
    out_back = inner_exchange(out_here)

    backward = call(
        functools.partial(backward_kernel, **sizes),
        [
            shape(half + TAIL if r == RETURNS - 1 else half, cols)
            for r in range(RETURNS)
            for _ in range(nt * pn)
        ]
        + [shape(slots, hid_n)] * 2,
        [info, *cs, expert_in, expert_out, after(hid, *out_here), a1, a2],
        [SMEM] + [HBM] * (pieces + 5),
        out_specs=[HBM] * (RETURNS * nt * pn + 2),
        scratch=[pltpu.VMEM((slots, nt * cols), BF16)]
        + [pltpu.VMEM((slots, hid_n), BF16)] * 3
        + [pltpu.VMEM((hid_n, nt * cols), BF16)] * 3
        + [pltpu.VMEM((2, slots, hid_n), BF16)]
        + [pltpu.VMEM((nt, pn, rows + TAIL, cols), BF16), dma((3 * nt + pieces + 3,))]
        + [dma((RETURNS * nt * pn + 4,))],
        name="expert_backward",
    )
    grads, (gg, ug) = backward[: RETURNS * nt * pn], backward[RETURNS * nt * pn :]
    near, far = grads[: nt * pn], grads[nt * pn :]
    out_combined = combine(out_back)
    out_parts = outer_exchange(out_combined)
    far = [after(part, *out_back) for part in far]
    far_here = core_sum([after(part, out_combined) for part in far[:pn]] + far[pn:])
    far_back = inner_exchange(far_here)
    near_here = core_sum([after(part, far_back[1]) for part in near])
    near_back = inner_exchange(near_here)

    far_parts, gate_parts = combine_far([after(piece, *near_here) for piece in far_back])
    grad_parts = combine_near(gate_parts, near_back) + far_parts

    grad_in, grad_out = call(
        functools.partial(weights_kernel, **sizes),
        [shape(*expert_in.shape), shape(*expert_out.shape)],
        [after(info, grad_parts[0]), *xs, *cs, gg, ug, hs],
        [SMEM] + [HBM] * (2 * pieces + 3),
        out_specs=[HBM, HBM],
        scratch=[
            pltpu.VMEM((3, slots, hid_n), BF16),
            pltpu.VMEM((2, nt, slots, cols), BF16),
            pltpu.VMEM((nt, 3, hid_n, cols), BF16),
            dma((3 + 2 * pieces,)),
            dma((3 * nt,)),
        ],
        name="expert_weights",
    )

    branch = jnp.sum(after(out_parts, grad_in).astype(F32), axis=0)
    input_sum = sum(part[:tokens].astype(F32) for part in grad_parts)
    gate_sum = sum(part[tokens : tokens + picks, :tokens].astype(F32) for part in grad_parts)
    restored = (second_half.astype(F32) - branch).astype(BF16)
    carried_grad = (first_grad.astype(F32) + input_sum).astype(BF16)
    return (restored, carried_grad, gate_sum.T, grad_in, grad_out)


def solution(mesh):
    in_specs = (
        P("expert", "tensor"),
        P("expert", "tensor"),
        P("expert", "tensor"),
        P("expert", "tensor"),
        P("expert", None),
        P("expert", None),
        P("expert", None, "tensor", None),
        P("expert", "tensor", None),
    )
    out_specs = (
        P("expert", "tensor"),
        P("expert", "tensor"),
        P("expert", None),
        P("expert", None, "tensor", None),
        P("expert", "tensor", None),
    )
    return jax.shard_map(body, mesh=mesh, in_specs=in_specs, out_specs=out_specs, check_vma=False)
```

profile of v0, /device:TPU:0, one launch (start us, length us, event | category | flops | bytes accessed | tf_op | source)
XLA Modules:
  0.0 180.4 jit_solution(14177338615192612476)
XLA Ops:
  0.6 3.1 %collective-permute-start = (bf16[128,1024]{1,0:T(8,128)(2,1)}, bf16[128,1024]{1,0:T(8,128)(2,1)S(1)}, u32[]{:S(2)}, u32[]{:S(2)}) collective-permute-start(bf16[128,1024]{1,0:T(8,128)(2,1)} %refs_0_.1), channel_id=1, source_target_pairs={{0,8},{2,10},{4,12},{6,14},{8,16},{10,18},{12,20},{14,22},{16,24},... | collective-permute-start | bytes 786440 | tf_op jit(solution)/shard_map/ppermute | solution.py:422
  3.7 2.6 %collective-permute-start.1 = (bf16[128,1024]{1,0:T(8,128)(2,1)}, bf16[128,1024]{1,0:T(8,128)(2,1)S(1)}, u32[]{:S(2)}, u32[]{:S(2)}) collective-permute-start(bf16[128,1024]{1,0:T(8,128)(2,1)} %refs_0_.1), channel_id=1, source_target_pairs={{0,16},{2,18},{4,20},{6,22},{8,24},{10,26},{12,28},{14,30},{16,0},... | collective-permute-start | bytes 786440 | tf_op jit(solution)/shard_map/ppermute | solution.py:422
  6.3 1.3 collective-permute-start.2
  7.6 0.7 convert_bitcast_fusion
  8.3 0.7 pad_convert_fusion
  9.0 2.0 %broadcast_in_dim.5 = bf16[4,128,1024]{2,1,0:T(8,128)(2,1)} broadcast(bf16[128,1024]{1,0:T(8,128)(2,1)} %param.11), dimensions={1,2} | broadcast | bytes 1310720 | tf_op jit(solution)/shard_map/broadcast_in_dim | solution.py:461
  11.7 3.3 %all-to-all-start = ((f32[4,16,128]{2,1,0:T(8,128)}), f32[4,16,128]{2,1,0:T(8,128)S(1)}, u32[]{:S(2)}, u32[]{:S(2)}) async-start(f32[4,16,128]{2,1,0:T(8,128)} %broadcast_in_dim.4), calls=%async_computation | async-start | bytes 65536 | tf_op jit(solution)/shard_map/all_to_all | solution.py:451
  15.0 8.9 %collective-permute-done.1.refs_2_ = bf16[128,1024]{1,0:T(8,128)(2,1)S(1)} collective-permute-done((bf16[128,1024]{1,0:T(8,128)(2,1)}, bf16[128,1024]{1,0:T(8,128)(2,1)S(1)}, u32[]{:S(2)}, u32[]{:S(2)}) %collective-permute-start.1) | collective-permute-done | bytes 262176 | tf_op jit(solution)/shard_map/ppermute | solution.py:422
  23.9 6.0 %all-to-all-done.meta = f32[4,16,128]{2,1,0:T(8,128)S(1)} async-done(((f32[4,16,128]{2,1,0:T(8,128)}), f32[4,16,128]{2,1,0:T(8,128)S(1)}, u32[]{:S(2)}, u32[]{:S(2)}) %all-to-all-start) | async-done | bytes 32800 | tf_op jit(solution)/shard_map/all_to_all | solution.py:451
  29.9 3.5 %all-to-all-start.1 = ((bf16[4,128,1024]{2,1,0:T(8,128)(2,1)}), bf16[4,128,1024]{2,1,0:T(8,128)(2,1)S(1)}, u32[]{:S(2)}, u32[]{:S(2)}) async-start(bf16[4,128,1024]{2,1,0:T(8,128)(2,1)} %broadcast_in_dim.5), calls=%async_computation.1 | async-start | bytes 2097152 | tf_op jit(solution)/shard_map/all_to_all | solution.py:451
  33.4 0.6 pad_add_fusion.info
  34.1 4.6 %pack_gates.1 = (bf16[240,1024]{1,0:T(8,128)(2,1)}, bf16[240,1024]{1,0:T(8,128)(2,1)}, bf16[240,1024]{1,0:T(8,128)(2,1)}, bf16[240,1024]{1,0:T(8,128)(2,1)}, bf16[896,512]{1,0:T(8,128)(2,1)}) custom-call(s32[4]{0:T(128)} %pad_add_fusion.info, f32[4,16,128]{2,1,0:T(8,128)} %copy-done.17, bf16[128,1024]{1,0:T(8,128)(2,1)} %refs_0_.1, ...), custom_call_target="tpu_custom_call" | custom-call | flops 1024 | bytes 1024 | tf_op jit(solution)/shard_map/pack_gates/pallas_call | solution.py:41
  38.7 2.5 %collective-permute-start.5 = (bf16[240,1024]{1,0:T(8,128)(2,1)}, bf16[240,1024]{1,0:T(8,128)(2,1)S(1)}, u32[]{:S(2)}, u32[]{:S(2)}) collective-permute-start(bf16[240,1024]{1,0:T(8,128)(2,1)} %get-tuple-element.97), channel_id=1, source_target_pairs={{0,6},{2,4},{4,2},{6,0},{8,14},{10,12},{12,10},{14,8},{16,22},{18,... | collective-permute-start | bytes 1474568 | tf_op jit(solution)/shard_map/ppermute | solution.py:429
  42.3 3.1 %route.1 = (bf16[256,448]{1,0:T(8,128)(2,1)}, bf16[256,448]{1,0:T(8,128)(2,1)}) custom-call(s32[4]{0:T(128)} %pad_add_fusion.info, f32[4,16,128]{2,1,0:T(8,128)} %copy-done.17), custom_call_target="tpu_custom_call" | custom-call | flops 1024 | bytes 1024 | tf_op jit(solution)/shard_map/route/pallas_call | solution.py:41
  45.3 13.9 %all-to-all-done.1.source = bf16[4,128,1024]{2,1,0:T(8,128)(2,1)S(1)} async-done(((bf16[4,128,1024]{2,1,0:T(8,128)(2,1)}), bf16[4,128,1024]{2,1,0:T(8,128)(2,1)S(1)}, u32[]{:S(2)}, u32[]{:S(2)}) %all-to-all-start.1) | async-done | bytes 1048608 | tf_op jit(solution)/shard_map/all_to_all | solution.py:451
  59.3 1.0 copy-done
  60.2 4.3 %pack.1 = (bf16[224,1024]{1,0:T(8,128)(2,1)}, bf16[224,1024]{1,0:T(8,128)(2,1)}, bf16[224,1024]{1,0:T(8,128)(2,1)}, bf16[224,1024]{1,0:T(8,128)(2,1)}) custom-call(s32[4]{0:T(128)} %pad_add_fusion.info, bf16[896,512]{1,0:T(8,128)(2,1)} %get-tuple-element.101.sel, bf16[4,128,1024]{2,1,0:T(8,128)(2,1)} %copy-done), custom_call_target="tpu_custom_call" | custom-call | flops 1024 | bytes 1024 | tf_op jit(solution)/shard_map/pack/pallas_call | solution.py:41
  65.7 2.4 %collective-permute-start.19 = (bf16[224,1024]{1,0:T(8,128)(2,1)}, bf16[224,1024]{1,0:T(8,128)(2,1)S(1)}, u32[]{:S(2)}, u32[]{:S(2)}) collective-permute-start(bf16[224,1024]{1,0:T(8,128)(2,1)} %get-tuple-element.107), channel_id=1, source_target_pairs={{0,6},{2,4},{4,2},{6,0},{8,14},{10,12},{12,10},{14,8},{16,22},{18,... | collective-permute-start | bytes 1376264 | tf_op jit(solution)/shard_map/ppermute | solution.py:429
  68.6 0.9 collective-permute-start.17
  69.6 0.7 copy-done.7
  70.3 0.8 copy-done.8
  71.1 16.3 %expert_forward.1 = (bf16[224,1024]{1,0:T(8,128)(2,1)}, bf16[224,1024]{1,0:T(8,128)(2,1)}, bf16[224,1024]{1,0:T(8,128)(2,1)}, bf16[224,1024]{1,0:T(8,128)(2,1)},...) custom-call(s32[4]{0:T(128)} %pad_add_fusion.info, ...), custom_call_target="tpu_custom_call" | custom-call | flops 1024 | bytes 1024 | tf_op jit(solution)/shard_map/expert_forward/pallas_call | solution.py:41
  88.1 1.1 collective-permute-done.18.refs_2_.refs_10_
  89.8 1.3 add_convert_fusion
  92.1 2.4 %collective-permute-start.16 = (bf16[224,1024]{1,0:T(8,128)(2,1)S(1)}, bf16[224,1024]{1,0:T(8,128)(2,1)S(1)}, u32[]{:S(2)}, u32[]{:S(2)}) collective-permute-start(bf16[224,1024]{1,0:T(8,128)(2,1)S(1)} %add_convert_fusion), channel_id=1, source_target_pairs={{0,6},{2,4},{4,2},{6,0},{8,14},{10,12},{12,10},{14,8},{16,22},{18,... | collective-permute-start | bytes 1376264 | tf_op jit(solution)/shard_map/ppermute | solution.py:429
  95.6 1.0 add_convert_fusion.3.refs_2_
  96.6 0.7 copy-done.15
  97.6 17.9 %expert_backward.1 = (bf16[112,1024]{1,0:T(8,128)(2,1)}, bf16[112,1024]{1,0:T(8,128)(2,1)}, bf16[112,1024]{1,0:T(8,128)(2,1)}, bf16[112,1024]{1,0:T(8,128)(2,1)}...) custom-call(s32[4]{0:T(128)} %pad_add_fusion.info, ...), custom_call_target="tpu_custom_call" | custom-call | flops 1024 | bytes 1024 | tf_op jit(solution)/shard_map/expert_backward/pallas_call | solution.py:41
  116.6 4.5 %combine.1 = bf16[4,128,1024]{2,1,0:T(8,128)(2,1)} custom-call(s32[4]{0:T(128)} %pad_add_fusion.info, bf16[256,448]{1,0:T(8,128)(2,1)} %get-tuple-element.99.refs_0_.chosen, bf16[256,448]{1,0:T(8,128)(2,1)} %get-tuple-element.100.refs_1_.chosen, bf16[224,1024]{1,0:T(8,128)(2,1)} %add_convert_fusion.3.refs_2_, bf16[224,1024]{1,0:T(8,128)(2,1)} %copy-done.23, ...), custom_call_target="tpu_custom_call" | custom-call | flops 1024 | bytes 1024 | tf_op jit(solution)/shard_map/combine/pallas_call | solution.py:41
  121.2 3.7 %all-to-all-start.2 = ((bf16[4,128,1024]{2,1,0:T(8,128)(2,1)}), bf16[4,128,1024]{2,1,0:T(8,128)(2,1)S(1)}, u32[]{:S(2)}, u32[]{:S(2)}) async-start(bf16[4,128,1024]{2,1,0:T(8,128)(2,1)} %combine.1), calls=%async_computation.2 | async-start | bytes 2097152 | tf_op jit(solution)/shard_map/all_to_all | solution.py:451
  125.6 1.6 collective-permute-start.26
  127.2 1.6 collective-permute-start.34
  129.4 5.4 %collective-permute-done.26.refs_1_ = bf16[128,1024]{1,0:T(8,128)(2,1)S(1)} collective-permute-done((bf16[128,1024]{1,0:T(8,128)(2,1)S(1)}, bf16[128,1024]{1,0:T(8,128)(2,1)S(1)}, u32[]{:S(2)}, u32[]{:S(2)}) %collective-permute-start.26) | collective-permute-done | bytes 262176 | tf_op jit(solution)/shard_map/ppermute | solution.py:429
  134.9 0.8 add_convert_fusion.8.refs_0_
  137.2 2.3 %collective-permute-start.37 = (bf16[112,1024]{1,0:T(8,128)(2,1)S(1)}, bf16[112,1024]{1,0:T(8,128)(2,1)S(1)}, u32[]{:S(2)}, u32[]{:S(2)}) collective-permute-start(bf16[112,1024]{1,0:T(8,128)(2,1)S(1)} %add_convert_fusion.9), channel_id=1, source_target_pairs={{0,6},{2,4},{4,2},{6,0},{8,14},{10,12},{12,10},{14,8},{16,22},{18,... | collective-permute-start | bytes 688136 | tf_op jit(solution)/shard_map/ppermute | solution.py:429
  139.6 0.7 collective-permute-start.36
  141.0 0.8 add_convert_fusion.12.refs_0_
  141.8 6.4 %collective-permute-done.32.refs_2_ = bf16[128,1024]{1,0:T(8,128)(2,1)S(1)} collective-permute-done((bf16[128,1024]{1,0:T(8,128)(2,1)S(1)}, bf16[128,1024]{1,0:T(8,128)(2,1)S(1)}, u32[]{:S(2)}, u32[]{:S(2)}) %collective-permute-start.32) | collective-permute-done | bytes 262176 | tf_op jit(solution)/shard_map/ppermute | solution.py:429
  148.2 0.7 copy-done.27
  148.9 3.9 %combine_far.1 = (bf16[144,1024]{1,0:T(8,128)(2,1)}, bf16[144,1024]{1,0:T(8,128)(2,1)}, bf16[16,512]{1,0:T(8,128)(2,1)}) custom-call(s32[4]{0:T(128)} %pad_add_fusion.info, f32[4,16,128]{2,1,0:T(8,128)} %copy-done.17, bf16[896,512]{1,0:T(8,128)(2,1)} %get-tuple-element.101.sel, bf16[256,448]{1,0:T(8,128)(2,1)} %get-tuple-element.100.refs_1_.chosen, ...), custom_call_target="tpu_custom_call" | custom-call | flops 1024 | bytes 1024 | tf_op jit(solution)/shard_map/combine_far/pallas_call | solution.py:41
  152.9 2.9 %collective-permute-start.39 = (bf16[144,1024]{1,0:T(8,128)(2,1)}, bf16[144,1024]{1,0:T(8,128)(2,1)S(1)}, u32[]{:S(2)}, u32[]{:S(2)}) collective-permute-start(bf16[144,1024]{1,0:T(8,128)(2,1)} %get-tuple-element.178), channel_id=1, source_target_pairs={{0,16},{2,18},{4,20},{6,22},{8,24},{10,26},{12,28},{14,30},{16,0},... | collective-permute-start | bytes 884744 | tf_op jit(solution)/shard_map/ppermute | solution.py:422
  155.8 1.5 collective-permute-start.40
  157.3 0.6 copy-done.37
  158.1 3.5 %combine_near.1 = (bf16[144,1024]{1,0:T(8,128)(2,1)}, bf16[144,1024]{1,0:T(8,128)(2,1)}) custom-call(bf16[16,512]{1,0:T(8,128)(2,1)} %get-tuple-element.169.gates, bf16[256,448]{1,0:T(8,128)(2,1)} %get-tuple-element.99.refs_0_.chosen, bf16[112,1024]{1,0:T(8,128)(2,1)} %add_convert_fusion.12.refs_0_, bf16[112,1024]{1,0:T(8,128)(2,1)} %copy-done.39, ...), custom_call_target="tpu_custom_call" | custom-call | flops 1024 | bytes 1024 | tf_op jit(solution)/shard_map/combine_near/pallas_call | solution.py:41
  161.6 2.4 %collective-permute-start.38 = (bf16[144,1024]{1,0:T(8,128)(2,1)}, bf16[144,1024]{1,0:T(8,128)(2,1)S(1)}, u32[]{:S(2)}, u32[]{:S(2)}) collective-permute-start(bf16[144,1024]{1,0:T(8,128)(2,1)} %get-tuple-element.177), channel_id=1, source_target_pairs={{0,24},{2,26},{4,28},{6,30},{8,0},{10,2},{12,4},{14,6},{16,8},{18,... | collective-permute-start | bytes 884744 | tf_op jit(solution)/shard_map/ppermute | solution.py:422
  164.0 13.9 %expert_weights.1 = (bf16[1,2,704,2048]{3,2,1,0:T(8,128)(2,1)}, bf16[1,704,2048]{2,1,0:T(8,128)(2,1)}) custom-call(s32[4]{0:T(128)} %pad_add_fusion.info, bf16[240,1024]{1,0:T(8,128)(2,1)} %get-tuple-element.109.refs_0_, bf16[240,1024]{1,0:T(8,128)(2,1)} %copy-done.4, bf16[240,1024]{1,0:T(8,128)(2,1)} %copy-done.3, bf16[240,1024]{1,0:T(8,128)(2,1)} %copy-done.2, ...), custom_call_target="tpu_custom_call" | custom-call | flops 1024 | bytes 1024 | tf_op jit(solution)/shard_map/expert_weights/pallas_call | solution.py:41
  178.5 0.9 add_convert_fusion.4
  179.7 0.8 subtract_convert_fusion
  (171 shorter events, 12.7 us)
Async XLA Ops:
  0.6 14.3 %collective-permute-start = (bf16[128,1024]{1,0:T(8,128)(2,1)}, bf16[128,1024]{1,0:T(8,128)(2,1)S(1)}, u32[]{:S(2)}, u32[]{:S(2)}) collective-permute-start(bf16[128,1024]{1,0:T(8,128)(2,1)} %refs_0_.1), channel_id=1, source_target_pairs={{0,8},{2,10},{4,12},{6,14},{8,16},{10,18},{12,20},{14,22},{16,24},... | collective-permute-start | bytes 786440 | tf_op jit(solution)/shard_map/ppermute | solution.py:422
  3.7 20.1 %collective-permute-start.1 = (bf16[128,1024]{1,0:T(8,128)(2,1)}, bf16[128,1024]{1,0:T(8,128)(2,1)S(1)}, u32[]{:S(2)}, u32[]{:S(2)}) collective-permute-start(bf16[128,1024]{1,0:T(8,128)(2,1)} %refs_0_.1), channel_id=1, source_target_pairs={{0,16},{2,18},{4,20},{6,22},{8,24},{10,26},{12,28},{14,30},{16,0},... | collective-permute-start | bytes 786440 | tf_op jit(solution)/shard_map/ppermute | solution.py:422
  6.3 17.6 %collective-permute-start.2 = (bf16[128,1024]{1,0:T(8,128)(2,1)}, bf16[128,1024]{1,0:T(8,128)(2,1)S(1)}, u32[]{:S(2)}, u32[]{:S(2)}) collective-permute-start(bf16[128,1024]{1,0:T(8,128)(2,1)} %refs_0_.1), channel_id=1, source_target_pairs={{0,24},{2,26},{4,28},{6,30},{8,0},{10,2},{12,4},{14,6},{16,8},{18,... | collective-permute-start | bytes 786440 | tf_op jit(solution)/shard_map/ppermute | solution.py:422
  11.7 18.2 %all-to-all-start = ((f32[4,16,128]{2,1,0:T(8,128)}), f32[4,16,128]{2,1,0:T(8,128)S(1)}, u32[]{:S(2)}, u32[]{:S(2)}) async-start(f32[4,16,128]{2,1,0:T(8,128)} %broadcast_in_dim.4), calls=%async_computation | async-start | bytes 65536 | tf_op jit(solution)/shard_map/all_to_all | solution.py:451
  15.0 19.1 %copy-start.33 = (bf16[128,1024]{1,0:T(8,128)(2,1)}, bf16[128,1024]{1,0:T(8,128)(2,1)S(1)}, u32[]{:S(2)}) copy-start(bf16[128,1024]{1,0:T(8,128)(2,1)S(1)} %collective-permute-done.refs_1_) | copy-start | bytes 786436
  29.9 29.4 %all-to-all-start.1 = ((bf16[4,128,1024]{2,1,0:T(8,128)(2,1)}), bf16[4,128,1024]{2,1,0:T(8,128)(2,1)S(1)}, u32[]{:S(2)}, u32[]{:S(2)}) async-start(bf16[4,128,1024]{2,1,0:T(8,128)(2,1)} %broadcast_in_dim.5), calls=%async_computation.1 | async-start | bytes 2097152 | tf_op jit(solution)/shard_map/all_to_all | solution.py:451
  38.7 26.6 %copy-start.1 = (bf16[240,1024]{1,0:T(8,128)(2,1)S(1)}, bf16[240,1024]{1,0:T(8,128)(2,1)}, u32[]{:S(2)}) copy-start(bf16[240,1024]{1,0:T(8,128)(2,1)} %get-tuple-element.109.refs_0_) | copy-start | bytes 1474564
  38.7 25.9 %collective-permute-start.5 = (bf16[240,1024]{1,0:T(8,128)(2,1)}, bf16[240,1024]{1,0:T(8,128)(2,1)S(1)}, u32[]{:S(2)}, u32[]{:S(2)}) collective-permute-start(bf16[240,1024]{1,0:T(8,128)(2,1)} %get-tuple-element.97), channel_id=1, source_target_pairs={{0,6},{2,4},{4,2},{6,0},{8,14},{10,12},{12,10},{14,8},{16,22},{18,... | collective-permute-start | bytes 1474568 | tf_op jit(solution)/shard_map/ppermute | solution.py:429
  41.2 23.4 %collective-permute-start.4 = (bf16[240,1024]{1,0:T(8,128)(2,1)}, bf16[240,1024]{1,0:T(8,128)(2,1)S(1)}, u32[]{:S(2)}, u32[]{:S(2)}) collective-permute-start(bf16[240,1024]{1,0:T(8,128)(2,1)} %get-tuple-element.96), channel_id=1, source_target_pairs={{0,4},{2,6},{4,0},{6,2},{8,12},{10,14},{12,8},{14,10},{16,20},{18,... | collective-permute-start | bytes 1474568 | tf_op jit(solution)/shard_map/ppermute | solution.py:429
  41.7 23.4 %collective-permute-start.3 = (bf16[240,1024]{1,0:T(8,128)(2,1)}, bf16[240,1024]{1,0:T(8,128)(2,1)S(1)}, u32[]{:S(2)}, u32[]{:S(2)}) collective-permute-start(bf16[240,1024]{1,0:T(8,128)(2,1)} %get-tuple-element.95), channel_id=1, source_target_pairs={{0,2},{2,0},{4,6},{6,4},{8,10},{10,8},{12,14},{14,12},{16,18},{18,... | collective-permute-start | bytes 1474568 | tf_op jit(solution)/shard_map/ppermute | solution.py:429
  64.6 3.6 %collective-permute-start.9 = (bf16[240,1024]{1,0:T(8,128)(2,1)S(1)}, bf16[240,1024]{1,0:T(8,128)(2,1)S(1)}, u32[]{:S(2)}, u32[]{:S(2)}) collective-permute-start(bf16[240,1024]{1,0:T(8,128)(2,1)S(1)} %collective-permute-done.5.refs_3_), channel_id=1, source_target_pairs={{0,1},{1,0},{2,3},{3,2},{4,5},{5,4},{6,7},{7,6},{8,9},{9,8},{10,11... | collective-permute-start | bytes 1474568 | tf_op jit(solution)/shard_map/ppermute | solution.py:437
  64.7 4.0 %collective-permute-start.8 = (bf16[240,1024]{1,0:T(8,128)(2,1)S(1)}, bf16[240,1024]{1,0:T(8,128)(2,1)S(1)}, u32[]{:S(2)}, u32[]{:S(2)}) collective-permute-start(bf16[240,1024]{1,0:T(8,128)(2,1)S(1)} %collective-permute-done.4.refs_2_), channel_id=1, source_target_pairs={{0,1},{1,0},{2,3},{3,2},{4,5},{5,4},{6,7},{7,6},{8,9},{9,8},{10,11... | collective-permute-start | bytes 1474568 | tf_op jit(solution)/shard_map/ppermute | solution.py:437
  65.2 4.4 %collective-permute-start.7 = (bf16[240,1024]{1,0:T(8,128)(2,1)S(1)}, bf16[240,1024]{1,0:T(8,128)(2,1)S(1)}, u32[]{:S(2)}, u32[]{:S(2)}) collective-permute-start(bf16[240,1024]{1,0:T(8,128)(2,1)S(1)} %collective-permute-done.3.refs_1_), channel_id=1, source_target_pairs={{0,1},{1,0},{2,3},{3,2},{4,5},{5,4},{6,7},{7,6},{8,9},{9,8},{10,11... | collective-permute-start | bytes 1474568 | tf_op jit(solution)/shard_map/ppermute | solution.py:437
  65.3 4.3 %collective-permute-start.6 = (bf16[240,1024]{1,0:T(8,128)(2,1)S(1)}, bf16[240,1024]{1,0:T(8,128)(2,1)S(1)}, u32[]{:S(2)}, u32[]{:S(2)}) collective-permute-start(bf16[240,1024]{1,0:T(8,128)(2,1)S(1)} %copy-done.1), channel_id=1, source_target_pairs={{0,1},{1,0},{2,3},{3,2},{4,5},{5,4},{6,7},{7,6},{8,9},{9,8},{10,11... | collective-permute-start | bytes 1474568 | tf_op jit(solution)/shard_map/ppermute | solution.py:437
  65.7 22.3 %collective-permute-start.19 = (bf16[224,1024]{1,0:T(8,128)(2,1)}, bf16[224,1024]{1,0:T(8,128)(2,1)S(1)}, u32[]{:S(2)}, u32[]{:S(2)}) collective-permute-start(bf16[224,1024]{1,0:T(8,128)(2,1)} %get-tuple-element.107), channel_id=1, source_target_pairs={{0,6},{2,4},{4,2},{6,0},{8,14},{10,12},{12,10},{14,8},{16,22},{18,... | collective-permute-start | bytes 1376264 | tf_op jit(solution)/shard_map/ppermute | solution.py:429
  68.1 21.0 %collective-permute-start.18 = (bf16[224,1024]{1,0:T(8,128)(2,1)}, bf16[224,1024]{1,0:T(8,128)(2,1)S(1)}, u32[]{:S(2)}, u32[]{:S(2)}) collective-permute-start(bf16[224,1024]{1,0:T(8,128)(2,1)} %get-tuple-element.106), channel_id=1, source_target_pairs={{0,4},{2,6},{4,0},{6,2},{8,12},{10,14},{12,8},{14,10},{16,20},{18,... | collective-permute-start | bytes 1376264 | tf_op jit(solution)/shard_map/ppermute | solution.py:429
  68.6 20.6 %collective-permute-start.17 = (bf16[224,1024]{1,0:T(8,128)(2,1)}, bf16[224,1024]{1,0:T(8,128)(2,1)S(1)}, u32[]{:S(2)}, u32[]{:S(2)}) collective-permute-start(bf16[224,1024]{1,0:T(8,128)(2,1)} %get-tuple-element.105), channel_id=1, source_target_pairs={{0,2},{2,0},{4,6},{6,4},{8,10},{10,8},{12,14},{14,12},{16,18},{18,... | collective-permute-start | bytes 1376264 | tf_op jit(solution)/shard_map/ppermute | solution.py:429
  87.4 2.3 %collective-permute-start.15 = (bf16[224,1024]{1,0:T(8,128)(2,1)}, bf16[224,1024]{1,0:T(8,128)(2,1)S(1)}, u32[]{:S(2)}, u32[]{:S(2)}) collective-permute-start(bf16[224,1024]{1,0:T(8,128)(2,1)} %get-tuple-element.120), channel_id=1, source_target_pairs={{0,1},{1,0},{2,3},{3,2},{4,5},{5,4},{6,7},{7,6},{8,9},{9,8},{10,11... | collective-permute-start | bytes 1376264 | tf_op jit(solution)/shard_map/ppermute | solution.py:437
  87.5 3.6 %collective-permute-start.13 = (bf16[224,1024]{1,0:T(8,128)(2,1)}, bf16[224,1024]{1,0:T(8,128)(2,1)S(1)}, u32[]{:S(2)}, u32[]{:S(2)}) collective-permute-start(bf16[224,1024]{1,0:T(8,128)(2,1)} %get-tuple-element.118), channel_id=1, source_target_pairs={{0,1},{1,0},{2,3},{3,2},{4,5},{5,4},{6,7},{7,6},{8,9},{9,8},{10,11... | collective-permute-start | bytes 1376264 | tf_op jit(solution)/shard_map/ppermute | solution.py:437
  88.0 3.7 %collective-permute-start.11 = (bf16[224,1024]{1,0:T(8,128)(2,1)}, bf16[224,1024]{1,0:T(8,128)(2,1)S(1)}, u32[]{:S(2)}, u32[]{:S(2)}) collective-permute-start(bf16[224,1024]{1,0:T(8,128)(2,1)} %get-tuple-element.116), channel_id=1, source_target_pairs={{0,1},{1,0},{2,3},{3,2},{4,5},{5,4},{6,7},{7,6},{8,9},{9,8},{10,11... | collective-permute-start | bytes 1376264 | tf_op jit(solution)/shard_map/ppermute | solution.py:437
  89.1 3.0 %collective-permute-start.10 = (bf16[224,1024]{1,0:T(8,128)(2,1)}, bf16[224,1024]{1,0:T(8,128)(2,1)S(1)}, u32[]{:S(2)}, u32[]{:S(2)}) collective-permute-start(bf16[224,1024]{1,0:T(8,128)(2,1)} %get-tuple-element.114), channel_id=1, source_target_pairs={{0,1},{1,0},{2,3},{3,2},{4,5},{5,4},{6,7},{7,6},{8,9},{9,8},{10,11... | collective-permute-start | bytes 1376264 | tf_op jit(solution)/shard_map/ppermute | solution.py:437
  89.2 5.3 %collective-permute-start.23 = (bf16[224,1024]{1,0:T(8,128)(2,1)S(1)}, bf16[224,1024]{1,0:T(8,128)(2,1)S(1)}, u32[]{:S(2)}, u32[]{:S(2)}) collective-permute-start(bf16[224,1024]{1,0:T(8,128)(2,1)S(1)} %collective-permute-done.19.refs_3_.refs_11_), channel_id=1, source_target_pairs={{0,1},{1,0},{2,3},{3,2},{4,5},{5,4},{6,7},{7,6},{8,9},{9,8},{10,11... | collective-permute-start | bytes 1376264 | tf_op jit(solution)/shard_map/ppermute | solution.py:437
  89.7 5.4 %collective-permute-start.22 = (bf16[224,1024]{1,0:T(8,128)(2,1)S(1)}, bf16[224,1024]{1,0:T(8,128)(2,1)S(1)}, u32[]{:S(2)}, u32[]{:S(2)}) collective-permute-start(bf16[224,1024]{1,0:T(8,128)(2,1)S(1)} %collective-permute-done.18.refs_2_.refs_10_), channel_id=1, source_target_pairs={{0,1},{1,0},{2,3},{3,2},{4,5},{5,4},{6,7},{7,6},{8,9},{9,8},{10,11... | collective-permute-start | bytes 1376264 | tf_op jit(solution)/shard_map/ppermute | solution.py:437
  91.0 5.6 %collective-permute-start.21 = (bf16[224,1024]{1,0:T(8,128)(2,1)S(1)}, bf16[224,1024]{1,0:T(8,128)(2,1)S(1)}, u32[]{:S(2)}, u32[]{:S(2)}) collective-permute-start(bf16[224,1024]{1,0:T(8,128)(2,1)S(1)} %collective-permute-done.17.refs_1_.refs_9_), channel_id=1, source_target_pairs={{0,1},{1,0},{2,3},{3,2},{4,5},{5,4},{6,7},{7,6},{8,9},{9,8},{10,11... | collective-permute-start | bytes 1376264 | tf_op jit(solution)/shard_map/ppermute | solution.py:437
  91.7 4.9 %collective-permute-start.20 = (bf16[224,1024]{1,0:T(8,128)(2,1)S(1)}, bf16[224,1024]{1,0:T(8,128)(2,1)S(1)}, u32[]{:S(2)}, u32[]{:S(2)}) collective-permute-start(bf16[224,1024]{1,0:T(8,128)(2,1)S(1)} %copy-done.9), channel_id=1, source_target_pairs={{0,1},{1,0},{2,3},{3,2},{4,5},{5,4},{6,7},{7,6},{8,9},{9,8},{10,11... | collective-permute-start | bytes 1376264 | tf_op jit(solution)/shard_map/ppermute | solution.py:437
  92.1 23.4 %collective-permute-start.16 = (bf16[224,1024]{1,0:T(8,128)(2,1)S(1)}, bf16[224,1024]{1,0:T(8,128)(2,1)S(1)}, u32[]{:S(2)}, u32[]{:S(2)}) collective-permute-start(bf16[224,1024]{1,0:T(8,128)(2,1)S(1)} %add_convert_fusion), channel_id=1, source_target_pairs={{0,6},{2,4},{4,2},{6,0},{8,14},{10,12},{12,10},{14,8},{16,22},{18,... | collective-permute-start | bytes 1376264 | tf_op jit(solution)/shard_map/ppermute | solution.py:429
  94.6 21.2 %collective-permute-start.14 = (bf16[224,1024]{1,0:T(8,128)(2,1)S(1)}, bf16[224,1024]{1,0:T(8,128)(2,1)S(1)}, u32[]{:S(2)}, u32[]{:S(2)}) collective-permute-start(bf16[224,1024]{1,0:T(8,128)(2,1)S(1)} %add_convert_fusion.1), channel_id=1, source_target_pairs={{0,4},{2,6},{4,0},{6,2},{8,12},{10,14},{12,8},{14,10},{16,20},{18,... | collective-permute-start | bytes 1376264 | tf_op jit(solution)/shard_map/ppermute | solution.py:429
  95.1 20.7 %collective-permute-start.12 = (bf16[224,1024]{1,0:T(8,128)(2,1)S(1)}, bf16[224,1024]{1,0:T(8,128)(2,1)S(1)}, u32[]{:S(2)}, u32[]{:S(2)}) collective-permute-start(bf16[224,1024]{1,0:T(8,128)(2,1)S(1)} %add_convert_fusion.2), channel_id=1, source_target_pairs={{0,2},{2,0},{4,6},{6,4},{8,10},{10,8},{12,14},{14,12},{16,18},{18,... | collective-permute-start | bytes 1376264 | tf_op jit(solution)/shard_map/ppermute | solution.py:429
  115.8 9.6 %collective-permute-start.25 = (bf16[128,1024]{1,0:T(8,128)(2,1)}, bf16[128,1024]{1,0:T(8,128)(2,1)S(1)}, u32[]{:S(2)}, u32[]{:S(2)}) collective-permute-start(bf16[128,1024]{1,0:T(8,128)(2,1)} %get-tuple-element.139), channel_id=1, source_target_pairs={{0,1},{1,0},{2,3},{3,2},{4,5},{5,4},{6,7},{7,6},{8,9},{9,8},{10,11... | collective-permute-start | bytes 786440 | tf_op jit(solution)/shard_map/ppermute | solution.py:437
  115.8 11.3 %collective-permute-start.33 = (bf16[128,1024]{1,0:T(8,128)(2,1)}, bf16[128,1024]{1,0:T(8,128)(2,1)S(1)}, u32[]{:S(2)}, u32[]{:S(2)}) collective-permute-start(bf16[128,1024]{1,0:T(8,128)(2,1)} %get-tuple-element.167), channel_id=1, source_target_pairs={{0,1},{1,0},{2,3},{3,2},{4,5},{5,4},{6,7},{7,6},{8,9},{9,8},{10,11... | collective-permute-start | bytes 786440 | tf_op jit(solution)/shard_map/ppermute | solution.py:437
  121.2 58.3 %all-to-all-start.2 = ((bf16[4,128,1024]{2,1,0:T(8,128)(2,1)}), bf16[4,128,1024]{2,1,0:T(8,128)(2,1)S(1)}, u32[]{:S(2)}, u32[]{:S(2)}) async-start(bf16[4,128,1024]{2,1,0:T(8,128)(2,1)} %combine.1), calls=%async_computation.2 | async-start | bytes 2097152 | tf_op jit(solution)/shard_map/all_to_all | solution.py:451
  124.9 3.9 %collective-permute-start.31 = (bf16[128,1024]{1,0:T(8,128)(2,1)S(1)}, bf16[128,1024]{1,0:T(8,128)(2,1)S(1)}, u32[]{:S(2)}, u32[]{:S(2)}) collective-permute-start(bf16[128,1024]{1,0:T(8,128)(2,1)S(1)} %copy-done.45), channel_id=1, source_target_pairs={{0,1},{1,0},{2,3},{3,2},{4,5},{5,4},{6,7},{7,6},{8,9},{9,8},{10,11... | collective-permute-start | bytes 786440 | tf_op jit(solution)/shard_map/ppermute | solution.py:437
  125.0 9.8 %collective-permute-start.24 = (bf16[128,1024]{1,0:T(8,128)(2,1)S(1)}, bf16[128,1024]{1,0:T(8,128)(2,1)S(1)}, u32[]{:S(2)}, u32[]{:S(2)}) collective-permute-start(bf16[128,1024]{1,0:T(8,128)(2,1)S(1)} %copy-done.44), channel_id=1, source_target_pairs={{0,1},{1,0},{2,3},{3,2},{4,5},{5,4},{6,7},{7,6},{8,9},{9,8},{10,11... | collective-permute-start | bytes 786440 | tf_op jit(solution)/shard_map/ppermute | solution.py:437
  125.6 14.0 %copy-start.42 = (bf16[112,1024]{1,0:T(8,128)(2,1)S(1)}, bf16[112,1024]{1,0:T(8,128)(2,1)}, u32[]{:S(2)}) copy-start(bf16[112,1024]{1,0:T(8,128)(2,1)} %get-tuple-element.148) | copy-start | bytes 688132
  125.6 9.2 %collective-permute-start.26 = (bf16[128,1024]{1,0:T(8,128)(2,1)S(1)}, bf16[128,1024]{1,0:T(8,128)(2,1)S(1)}, u32[]{:S(2)}, u32[]{:S(2)}) collective-permute-start(bf16[128,1024]{1,0:T(8,128)(2,1)S(1)} %add_convert_fusion.7), channel_id=1, source_target_pairs={{0,2},{2,0},{4,6},{6,4},{8,10},{10,8},{12,14},{14,12},{16,18},{18,... | collective-permute-start | bytes 786440 | tf_op jit(solution)/shard_map/ppermute | solution.py:429
  127.2 14.6 %collective-permute-start.34 = (bf16[128,1024]{1,0:T(8,128)(2,1)S(1)}, bf16[128,1024]{1,0:T(8,128)(2,1)S(1)}, u32[]{:S(2)}, u32[]{:S(2)}) collective-permute-start(bf16[128,1024]{1,0:T(8,128)(2,1)S(1)} %add_convert_fusion.5), channel_id=1, source_target_pairs={{0,6},{2,4},{4,2},{6,0},{8,14},{10,12},{12,10},{14,8},{16,22},{18,... | collective-permute-start | bytes 786440 | tf_op jit(solution)/shard_map/ppermute | solution.py:429
  128.9 19.4 %collective-permute-start.32 = (bf16[128,1024]{1,0:T(8,128)(2,1)S(1)}, bf16[128,1024]{1,0:T(8,128)(2,1)S(1)}, u32[]{:S(2)}, u32[]{:S(2)}) collective-permute-start(bf16[128,1024]{1,0:T(8,128)(2,1)S(1)} %add_convert_fusion.6), channel_id=1, source_target_pairs={{0,4},{2,6},{4,0},{6,2},{8,12},{10,14},{12,8},{14,10},{16,20},{18,... | collective-permute-start | bytes 786440 | tf_op jit(solution)/shard_map/ppermute | solution.py:429
  134.8 1.5 collective-permute-start.30
  135.6 1.6 collective-permute-start.29
  136.1 3.5 %collective-permute-start.28 = (bf16[112,1024]{1,0:T(8,128)(2,1)S(1)}, bf16[112,1024]{1,0:T(8,128)(2,1)S(1)}, u32[]{:S(2)}, u32[]{:S(2)}) collective-permute-start(bf16[112,1024]{1,0:T(8,128)(2,1)S(1)} %copy-done.47), channel_id=1, source_target_pairs={{0,1},{1,0},{2,3},{3,2},{4,5},{5,4},{6,7},{7,6},{8,9},{9,8},{10,11... | collective-permute-start | bytes 688136 | tf_op jit(solution)/shard_map/ppermute | solution.py:437
  136.3 4.1 %collective-permute-start.27 = (bf16[112,1024]{1,0:T(8,128)(2,1)S(1)}, bf16[112,1024]{1,0:T(8,128)(2,1)S(1)}, u32[]{:S(2)}, u32[]{:S(2)}) collective-permute-start(bf16[112,1024]{1,0:T(8,128)(2,1)S(1)} %copy-done.46), channel_id=1, source_target_pairs={{0,1},{1,0},{2,3},{3,2},{4,5},{5,4},{6,7},{7,6},{8,9},{9,8},{10,11... | collective-permute-start | bytes 688136 | tf_op jit(solution)/shard_map/ppermute | solution.py:437
  137.2 20.0 %collective-permute-start.37 = (bf16[112,1024]{1,0:T(8,128)(2,1)S(1)}, bf16[112,1024]{1,0:T(8,128)(2,1)S(1)}, u32[]{:S(2)}, u32[]{:S(2)}) collective-permute-start(bf16[112,1024]{1,0:T(8,128)(2,1)S(1)} %add_convert_fusion.9), channel_id=1, source_target_pairs={{0,6},{2,4},{4,2},{6,0},{8,14},{10,12},{12,10},{14,8},{16,22},{18,... | collective-permute-start | bytes 688136 | tf_op jit(solution)/shard_map/ppermute | solution.py:429
  139.6 17.6 %collective-permute-start.36 = (bf16[112,1024]{1,0:T(8,128)(2,1)S(1)}, bf16[112,1024]{1,0:T(8,128)(2,1)S(1)}, u32[]{:S(2)}, u32[]{:S(2)}) collective-permute-start(bf16[112,1024]{1,0:T(8,128)(2,1)S(1)} %add_convert_fusion.10), channel_id=1, source_target_pairs={{0,4},{2,6},{4,0},{6,2},{8,12},{10,14},{12,8},{14,10},{16,20},{18,... | collective-permute-start | bytes 688136 | tf_op jit(solution)/shard_map/ppermute | solution.py:429
  140.4 16.9 %collective-permute-start.35 = (bf16[112,1024]{1,0:T(8,128)(2,1)S(1)}, bf16[112,1024]{1,0:T(8,128)(2,1)S(1)}, u32[]{:S(2)}, u32[]{:S(2)}) collective-permute-start(bf16[112,1024]{1,0:T(8,128)(2,1)S(1)} %add_convert_fusion.11), channel_id=1, source_target_pairs={{0,2},{2,0},{4,6},{6,4},{8,10},{10,8},{12,14},{14,12},{16,18},{18,... | collective-permute-start | bytes 688136 | tf_op jit(solution)/shard_map/ppermute | solution.py:429
  152.9 25.0 %collective-permute-start.39 = (bf16[144,1024]{1,0:T(8,128)(2,1)}, bf16[144,1024]{1,0:T(8,128)(2,1)S(1)}, u32[]{:S(2)}, u32[]{:S(2)}) collective-permute-start(bf16[144,1024]{1,0:T(8,128)(2,1)} %get-tuple-element.178), channel_id=1, source_target_pairs={{0,16},{2,18},{4,20},{6,22},{8,24},{10,26},{12,28},{14,30},{16,0},... | collective-permute-start | bytes 884744 | tf_op jit(solution)/shard_map/ppermute | solution.py:422
  155.8 22.1 %collective-permute-start.40 = (bf16[144,1024]{1,0:T(8,128)(2,1)}, bf16[144,1024]{1,0:T(8,128)(2,1)S(1)}, u32[]{:S(2)}, u32[]{:S(2)}) collective-permute-start(bf16[144,1024]{1,0:T(8,128)(2,1)} %get-tuple-element.179), channel_id=1, source_target_pairs={{0,8},{2,10},{4,12},{6,14},{8,16},{10,18},{12,20},{14,22},{16,24},... | collective-permute-start | bytes 884744 | tf_op jit(solution)/shard_map/ppermute | solution.py:422
  161.6 16.3 %collective-permute-start.38 = (bf16[144,1024]{1,0:T(8,128)(2,1)}, bf16[144,1024]{1,0:T(8,128)(2,1)S(1)}, u32[]{:S(2)}, u32[]{:S(2)}) collective-permute-start(bf16[144,1024]{1,0:T(8,128)(2,1)} %get-tuple-element.177), channel_id=1, source_target_pairs={{0,24},{2,26},{4,28},{6,30},{8,0},{10,2},{12,4},{14,6},{16,8},{18,... | collective-permute-start | bytes 884744 | tf_op jit(solution)/shard_map/ppermute | solution.py:422
  164.0 14.5 %copy-start.31 = (bf16[128,1024]{1,0:T(8,128)(2,1)S(1)}, bf16[128,1024]{1,0:T(8,128)(2,1)}, u32[]{:S(2)}) copy-start(bf16[128,1024]{1,0:T(8,128)(2,1)} %param.10) | copy-start | bytes 786436
  (46 other events, 210.1 us)
where the time goes:
time: 181 us; the launch traced here: 180 us
  Pallas kernels  71.9 us (40%)
  starting transfers between devices  47.3 us (26%)
  waiting for transfers between devices  42.9 us (24%)
  other arithmetic  8.92 us (5%)
  local copies, waits for them, and re-layouts  8.06 us (4%)
    pallas_call x9, Pallas kernels, call(): pl.pallas_call(kernel, out_shape=outs, in_specs=specs, out_specs=out_spec...  71.9 us
    all_to_all x3, waiting for transfers between devices, outer_exchange(): lax.all_to_all(value, 'expert', split_axis=0, concat_axis=0, axis_index_g...  20 us
    ppermute x15, starting transfers between devices, inner_send(): return lax.ppermute(value, 'expert', [(e, e ^ q) for e in range(groups)])  18.2 us
    ppermute x6, starting transfers between devices, outer_send(): lax.ppermute(value, 'expert', [(e, (e // pn + s) % zn * pn + e % pn) for...  13.8 us
    ppermute x15, waiting for transfers between devices, inner_send(): return lax.ppermute(value, 'expert', [(e, e ^ q) for e in range(groups)])  13.3 us
    all_to_all x3, starting transfers between devices, outer_exchange(): lax.all_to_all(value, 'expert', split_axis=0, concat_axis=0, axis_index_g...  10.4 us
    ppermute x6, waiting for transfers between devices, outer_send(): lax.ppermute(value, 'expert', [(e, (e // pn + s) % zn * pn + e % pn) for...  8.88 us
    unnamed x100, local copies, waits for them, and re-layouts  5.39 us
  transfers between devices with their start and end apart: 44, of which 11 were waited for; matrix products, arithmetic and copies ran while one was open for 6% of the time, Pallas kernels for 40%

commit v1 on v0

--- a/solution.py
+++ b/solution.py
@@ -12,6 +12,7 @@
 RETURNS = 2
 TAIL = 16
 VMEM_LIMIT = 56 * 1024 * 1024
+SMALL_LIMIT = 16 * 1024 * 1024
 F32 = jnp.float32
 BF16 = jnp.bfloat16
 
@@ -37,14 +38,14 @@
 HBM = pl.BlockSpec(memory_space=pl.ANY)
 
 
-def call(kernel, outs, args, specs, out_specs=None, scratch=(), name=None):
+def call(kernel, outs, args, specs, out_specs=None, scratch=(), name=None, limit=SMALL_LIMIT):
     return pl.pallas_call(
         kernel,
         out_shape=outs,
         in_specs=specs,
         out_specs=out_specs if out_specs is not None else [VMEM] * len(outs),
         scratch_shapes=list(scratch),
-        compiler_params=pltpu.CompilerParams(vmem_limit_bytes=VMEM_LIMIT),
+        compiler_params=pltpu.CompilerParams(vmem_limit_bytes=limit),
         cost_estimate=pl.CostEstimate(flops=1024, bytes_accessed=1024, transcendentals=0),
         name=name,
     )(*args)
@@ -361,27 +362,25 @@
     stores.finish()
 
 
-def weights_kernel(info, *refs, nt, pn, rows, cols):
+def weights_kernel(info, *refs, nt, pn, rows, cols, kinds):
     n = CHUNKS * pn
-    xs, cs, refs = by_core(refs, nt, n), by_core(refs[nt * n :], nt, n), refs[2 * nt * n :]
-    lefts, (gin, gout, left, right, stage, in_sems, out_sems) = refs[:3], refs[3:]
+    sources, refs = by_core(refs, nt, n), refs[nt * n :]
+    lefts, out, (left, right, stage, in_sems, out_sems) = refs[:kinds], refs[kinds], refs[kinds + 1 :]
     loads, stores = Loads(in_sems), Loads(out_sems)
-    order = ((0, 0, xs), (1, 0, xs), (2, 1, cs))
-    for w, side, sources in order:
+    loads.add(("l", 0), lefts[0], left.at[0])
+    for j in range(nt):
+        for q in range(n):
+            target = right.at[j, pl.ds(q * rows, rows)]
+            loads.add((j, q), sources[j][q].at[pl.ds(0, rows)], target)
+    for w in range(1, kinds):
         loads.add(("l", w), lefts[w], left.at[w])
-        if w == 1:
-            continue
-        for j in range(nt):
-            for q in range(n):
-                target = right.at[side, j, pl.ds(q * rows, rows)]
-                loads.add((side, j, q), sources[j][q].at[pl.ds(0, rows)], target)
-    for w, side, _ in order:
+    for w in range(kinds):
         loads.need(("l", w))
         for j in range(nt):
-            loads.need(*((side, j, q) for q in range(n)))
+            loads.need(*((j, q) for q in range(n)))
             at = column_block(info, j, nt, cols)
-            stage[j, w] = dot_tn(left[w], right[side, j]).astype(BF16)
-            target = gout.at[0, :, at] if w == 2 else gin.at[0, w, :, at]
+            stage[j, w] = dot_tn(left[w], right[j]).astype(BF16)
+            target = out.at[0, w, :, at] if kinds > 1 else out.at[0, :, at]
             stores.add((j, w), stage.at[j, w], target)
     loads.finish()
     stores.finish()
@@ -461,7 +460,7 @@
         return jnp.broadcast_to(value[None], (zn,) + value.shape)
 
     grad_copies = copies(second_grad)
-    meta = outer_exchange(after(copies(own), grad_copies))
+    meta = outer_exchange(after(copies(own), grad_copies, info))
     dma = pltpu.SemaphoreType.DMA
     sizes = dict(nt=nt, pn=pn, rows=part_rows, cols=cols)
 
@@ -551,8 +550,27 @@
     c_packed = pack(after(gathered, *chosen))
     c_here = inner_exchange(c_packed)
 
+    def weight_grad(like, info, sources, lefts):
+        kinds = len(lefts)
+        return call(
+            functools.partial(weights_kernel, **sizes, kinds=kinds),
+            [shape(*like.shape)],
+            [info, *sources, *lefts],
+            [SMEM] + [HBM] * (pieces + kinds),
+            out_specs=[HBM],
+            scratch=[
+                pltpu.VMEM((kinds, slots, hid_n), BF16),
+                pltpu.VMEM((nt, slots, cols), BF16),
+                pltpu.VMEM((nt, kinds, hid_n, cols), BF16),
+                dma((kinds + pieces,)),
+                dma((kinds * nt,)),
+            ],
+            name="expert_weights",
+            limit=VMEM_LIMIT,
+        )[0]
+
+    pieces = nt * CHUNKS * pn
     xs = swapped(([after(piece, *c_packed) for piece in x_here],))
-    pieces = nt * CHUNKS * pn
     forward = call(
         functools.partial(forward_kernel, **sizes),
         [shape(rows, cols)] * (nt * pn) + [shape(slots, hid_n)] * 4,
@@ -565,6 +583,7 @@
         + [pltpu.VMEM((nt, pn, rows, cols), BF16), dma((3 * nt + pieces + pn,))]
         + [dma((nt * pn + 8,))],
         name="expert_forward",
+        limit=VMEM_LIMIT,
     )
     outs, (hs, hid, a1, a2) = forward[: nt * pn], forward[nt * pn :]
     cs = swapped(([after(piece, hid) for piece in c_here],))
@@ -589,6 +608,7 @@
         + [pltpu.VMEM((nt, pn, rows + TAIL, cols), BF16), dma((3 * nt + pieces + 3,))]
         + [dma((RETURNS * nt * pn + 4,))],
         name="expert_backward",
+        limit=VMEM_LIMIT,
     )
     grads, (gg, ug) = backward[: RETURNS * nt * pn], backward[RETURNS * nt * pn :]
     near, far = grads[: nt * pn], grads[nt * pn :]
@@ -599,25 +619,12 @@
     far_back = inner_exchange(far_here)
     near_here = core_sum([after(part, far_back[1]) for part in near])
     near_back = inner_exchange(near_here)
-
-    far_parts, gate_parts = combine_far([after(piece, *near_here) for piece in far_back])
+    grad_out = weight_grad(expert_out, after(info, *near_here), cs, (hs,))
+
+    far_parts, gate_parts = combine_far([after(piece, *near_here, grad_out) for piece in far_back])
     grad_parts = combine_near(gate_parts, near_back) + far_parts
 
-    grad_in, grad_out = call(
-        functools.partial(weights_kernel, **sizes),
-        [shape(*expert_in.shape), shape(*expert_out.shape)],
-        [after(info, grad_parts[0]), *xs, *cs, gg, ug, hs],
-        [SMEM] + [HBM] * (2 * pieces + 3),
-        out_specs=[HBM, HBM],
-        scratch=[
-            pltpu.VMEM((3, slots, hid_n), BF16),
-            pltpu.VMEM((2, nt, slots, cols), BF16),
-            pltpu.VMEM((nt, 3, hid_n, cols), BF16),
-            dma((3 + 2 * pieces,)),
-            dma((3 * nt,)),
-        ],
-        name="expert_weights",
-    )
+    grad_in = weight_grad(expert_in, after(info, grad_parts[0]), xs, (gg, ug))
 
     branch = jnp.sum(after(out_parts, grad_in).astype(F32), axis=0)
     input_sum = sum(part[:tokens].astype(F32) for part in grad_parts)

time: 181 us -> 182 us (level)
  the two profiles are of different devices: /device:TPU:0 before, /device:TPU:9 now
where the time goes in v1:
time: 182 us; the launch traced here: 181 us
  Pallas kernels  68.9 us (38%)
  waiting for transfers between devices  49.3 us (27%)
  starting transfers between devices  44.8 us (25%)
  other arithmetic  9.6 us (5%)
  local copies, waits for them, and re-layouts  6.95 us (4%)
    pallas_call x10, Pallas kernels, call(): pl.pallas_call(kernel, out_shape=outs, in_specs=specs, out_specs=out_spec...  68.9 us
    ppermute x6, waiting for transfers between devices, outer_send(): lax.ppermute(value, 'expert', [(e, (e // pn + s) % zn * pn + e % pn) for...  26.4 us
    ppermute x15, starting transfers between devices, inner_send(): return lax.ppermute(value, 'expert', [(e, e ^ q) for e in range(groups)])  13.7 us
    all_to_all x3, starting transfers between devices, outer_exchange(): lax.all_to_all(value, 'expert', split_axis=0, concat_axis=0, axis_index_g...  13 us
    all_to_all x3, waiting for transfers between devices, outer_exchange(): lax.all_to_all(value, 'expert', split_axis=0, concat_axis=0, axis_index_g...  12.8 us
    ppermute x20, starting transfers between devices, tensor_send(): return lax.ppermute(value, 'tensor', [(c, (c + j) % nt) for c in range(nt)])  10.7 us
    ppermute x15, waiting for transfers between devices, inner_send(): return lax.ppermute(value, 'expert', [(e, e ^ q) for e in range(groups)])  9.52 us
    ppermute x6, starting transfers between devices, outer_send(): lax.ppermute(value, 'expert', [(e, (e // pn + s) % zn * pn + e % pn) for...  7.48 us
  transfers between devices with their start and end apart: 44, of which 11 were waited for; matrix products, arithmetic and copies ran while one was open for 6% of the time, Pallas kernels for 38%

profile of v1, /device:TPU:9, one launch (start us, length us, event | category | flops | bytes accessed | tf_op | source)
XLA Modules:
  0.0 180.7 jit_solution(3006720632035917577)
XLA Ops:
  0.6 1.3 collective-permute-start
  2.0 1.1 collective-permute-start.1
  3.1 1.4 collective-permute-start.2
  5.9 2.0 %broadcast_in_dim.5 = bf16[4,128,1024]{2,1,0:T(8,128)(2,1)} broadcast(bf16[128,1024]{1,0:T(8,128)(2,1)} %param.11), dimensions={1,2} | broadcast | bytes 1310720 | tf_op jit(solution)/shard_map/broadcast_in_dim | solution.py:460
  8.6 4.3 %all-to-all-start = ((f32[4,16,128]{2,1,0:T(8,128)}), f32[4,16,128]{2,1,0:T(8,128)S(1)}, u32[]{:S(2)}, u32[]{:S(2)}) async-start(f32[4,16,128]{2,1,0:T(8,128)} %broadcast_in_dim.4), calls=%async_computation | async-start | bytes 65536 | tf_op jit(solution)/shard_map/all_to_all | solution.py:450
  12.9 11.6 %collective-permute-done.1.refs_2_ = bf16[128,1024]{1,0:T(8,128)(2,1)S(1)} collective-permute-done((bf16[128,1024]{1,0:T(8,128)(2,1)}, bf16[128,1024]{1,0:T(8,128)(2,1)S(1)}, u32[]{:S(2)}, u32[]{:S(2)}) %collective-permute-start.1) | collective-permute-done | bytes 262176 | tf_op jit(solution)/shard_map/ppermute | solution.py:421
  24.5 2.8 %collective-permute-done.2.refs_3_ = bf16[128,1024]{1,0:T(8,128)(2,1)S(1)} collective-permute-done((bf16[128,1024]{1,0:T(8,128)(2,1)}, bf16[128,1024]{1,0:T(8,128)(2,1)S(1)}, u32[]{:S(2)}, u32[]{:S(2)}) %collective-permute-start.2) | collective-permute-done | bytes 262176 | tf_op jit(solution)/shard_map/ppermute | solution.py:421
  28.0 4.0 %all-to-all-start.1 = ((bf16[4,128,1024]{2,1,0:T(8,128)(2,1)}), bf16[4,128,1024]{2,1,0:T(8,128)(2,1)S(1)}, u32[]{:S(2)}, u32[]{:S(2)}) async-start(bf16[4,128,1024]{2,1,0:T(8,128)(2,1)} %broadcast_in_dim.5), calls=%async_computation.1 | async-start | bytes 2097152 | tf_op jit(solution)/shard_map/all_to_all | solution.py:450
  32.0 0.9 copy-done.4
  32.9 3.3 %pack_gates.1 = (bf16[240,1024]{1,0:T(8,128)(2,1)S(1)}, bf16[240,1024]{1,0:T(8,128)(2,1)}, bf16[240,1024]{1,0:T(8,128)(2,1)}, bf16[240,1024]{1,0:T(8,128)(2,1)}, bf16[896,512]{1,0:T(8,128)(2,1)S(1)}) custom-call(s32[4]{0:T(128)S(1)} %pad_add_fusion.info, f32[4,16,128]{2,1,0:T(8,128)S(1)} %all-to-all-done.meta, bf16[128,1024]{1,0:T(8,128)(2,1)S(1)} %copy-done.2, ...), custom_call_target="tpu_custom_call" | custom-call | flops 1024 | bytes 1024 | tf_op jit(solution)/shard_map/pack_gates/pallas_call | solution.py:42
  36.3 2.2 %collective-permute-start.5 = (bf16[240,1024]{1,0:T(8,128)(2,1)}, bf16[240,1024]{1,0:T(8,128)(2,1)}, u32[]{:S(2)}, u32[]{:S(2)}) collective-permute-start(bf16[240,1024]{1,0:T(8,128)(2,1)} %get-tuple-element.96), channel_id=1, source_target_pairs={{0,6},{2,4},{4,2},{6,0},{8,14},{10,12},{12,10},{14,8},{16,22},{18,... | collective-permute-start | bytes 1474568 | tf_op jit(solution)/shard_map/ppermute | solution.py:428
  39.0 2.2 %route.1 = (bf16[256,448]{1,0:T(8,128)(2,1)S(1)}, bf16[256,448]{1,0:T(8,128)(2,1)S(1)}) custom-call(s32[4]{0:T(128)S(1)} %pad_add_fusion.info, f32[4,16,128]{2,1,0:T(8,128)S(1)} %all-to-all-done.meta), custom_call_target="tpu_custom_call" | custom-call | flops 1024 | bytes 1024 | tf_op jit(solution)/shard_map/route/pallas_call | solution.py:42
  41.2 12.8 %all-to-all-done.1.source = bf16[4,128,1024]{2,1,0:T(8,128)(2,1)S(1)} async-done(((bf16[4,128,1024]{2,1,0:T(8,128)(2,1)}), bf16[4,128,1024]{2,1,0:T(8,128)(2,1)S(1)}, u32[]{:S(2)}, u32[]{:S(2)}) %all-to-all-start.1) | async-done | bytes 1048608 | tf_op jit(solution)/shard_map/all_to_all | solution.py:450
  54.0 2.0 %pack.1 = (bf16[224,1024]{1,0:T(8,128)(2,1)S(1)}, bf16[224,1024]{1,0:T(8,128)(2,1)S(1)}, bf16[224,1024]{1,0:T(8,128)(2,1)S(1)}, bf16[224,1024]{1,0:T(8,128)(2,1)S(1)}) custom-call(s32[4]{0:T(128)S(1)} %pad_add_fusion.info, bf16[896,512]{1,0:T(8,128)(2,1)S(1)} %get-tuple-element.100.sel, bf16[4,128,1024]{2,1,0:T(8,128)(2,1)S(1)} %all-to-all-done.1.source), custom_call_target="tpu_custom_call" | custom-call | flops 1024 | bytes 1024 | tf_op jit(solution)/shard_map/pack/pallas_call | solution.py:42
  56.0 1.7 collective-permute-start.9
  57.8 3.5 %collective-permute-done.4.refs_2_ = bf16[240,1024]{1,0:T(8,128)(2,1)} collective-permute-done((bf16[240,1024]{1,0:T(8,128)(2,1)}, bf16[240,1024]{1,0:T(8,128)(2,1)}, u32[]{:S(2)}, u32[]{:S(2)}) %collective-permute-start.4) | collective-permute-done | bytes 491552 | tf_op jit(solution)/shard_map/ppermute | solution.py:428
  62.3 1.5 collective-permute-start.19
  63.7 0.9 collective-permute-start.18
  66.6 16.0 %expert_forward.1 = (bf16[224,1024]{1,0:T(8,128)(2,1)}, bf16[224,1024]{1,0:T(8,128)(2,1)}, bf16[224,1024]{1,0:T(8,128)(2,1)}, bf16[224,1024]{1,0:T(8,128)(2,1)},...) custom-call(s32[4]{0:T(128)} %copy-done.5, ...), custom_call_target="tpu_custom_call" | custom-call | flops 1024 | bytes 1024 | tf_op jit(solution)/shard_map/expert_forward/pallas_call | solution.py:42
  82.6 1.0 collective-permute-start.15
  84.1 1.3 collective-permute-done.18.refs_2_
  86.5 1.2 add_convert_fusion
  87.9 1.0 add_convert_fusion.1
  89.3 0.9 add_convert_fusion.2
  90.3 1.5 collective-permute-start.16
  91.8 0.9 collective-permute-start.14
  94.1 18.3 %expert_backward.1 = (bf16[112,1024]{1,0:T(8,128)(2,1)}, bf16[112,1024]{1,0:T(8,128)(2,1)}, bf16[112,1024]{1,0:T(8,128)(2,1)}, bf16[112,1024]{1,0:T(8,128)(2,1)}...) custom-call(s32[4]{0:T(128)} %copy-done.5, ...), custom_call_target="tpu_custom_call" | custom-call | flops 1024 | bytes 1024 | tf_op jit(solution)/shard_map/expert_backward/pallas_call | solution.py:42
  112.3 1.1 collective-permute-done.14.refs_4_
  114.1 4.8 %combine.1 = bf16[4,128,1024]{2,1,0:T(8,128)(2,1)} custom-call(s32[4]{0:T(128)S(1)} %copy-done.6, bf16[256,448]{1,0:T(8,128)(2,1)S(1)} %get-tuple-element.98.refs_0_.chosen, bf16[256,448]{1,0:T(8,128)(2,1)S(1)} %get-tuple-element.99.refs_1_.chosen, bf16[224,1024]{1,0:T(8,128)(2,1)S(1)} %add_convert_fusion.3.refs_2_, ...), custom_call_target="tpu_custom_call" | custom-call | flops 1024 | bytes 1024 | tf_op jit(solution)/shard_map/combine/pallas_call | solution.py:42
  118.9 4.7 %all-to-all-start.2 = ((bf16[4,128,1024]{2,1,0:T(8,128)(2,1)}), bf16[4,128,1024]{2,1,0:T(8,128)(2,1)S(1)}, u32[]{:S(2)}, u32[]{:S(2)}) async-start(bf16[4,128,1024]{2,1,0:T(8,128)(2,1)} %combine.1), calls=%async_computation.2 | async-start | bytes 2097152 | tf_op jit(solution)/shard_map/all_to_all | solution.py:450
  123.6 1.1 collective-permute-start.31
  124.8 1.0 add_convert_fusion.7
  125.8 1.2 collective-permute-start.26
  127.0 1.0 add_convert_fusion.5
  128.1 1.3 collective-permute-start.34
  129.8 3.5 %collective-permute-done.26.refs_1_ = bf16[128,1024]{1,0:T(8,128)(2,1)S(1)} collective-permute-done((bf16[128,1024]{1,0:T(8,128)(2,1)S(1)}, bf16[128,1024]{1,0:T(8,128)(2,1)S(1)}, u32[]{:S(2)}, u32[]{:S(2)}) %collective-permute-start.26) | collective-permute-done | bytes 262176 | tf_op jit(solution)/shard_map/ppermute | solution.py:428
  133.3 2.2 %collective-permute-start.30 = (bf16[112,1024]{1,0:T(8,128)(2,1)S(1)}, bf16[112,1024]{1,0:T(8,128)(2,1)S(1)}, u32[]{:S(2)}, u32[]{:S(2)}) collective-permute-start(bf16[112,1024]{1,0:T(8,128)(2,1)S(1)} %copy-done.35), channel_id=1, source_target_pairs={{0,1},{1,0},{2,3},{3,2},{4,5},{5,4},{6,7},{7,6},{8,9},{9,8},{10,11... | collective-permute-start | bytes 688136 | tf_op jit(solution)/shard_map/ppermute | solution.py:436
  137.1 1.4 collective-permute-start.37
  138.6 1.0 collective-permute-start.36
  140.1 7.2 %expert_weights.2 = bf16[1,704,2048]{2,1,0:T(8,128)(2,1)} custom-call(s32[4]{0:T(128)} %copy-done.5, bf16[224,1024]{1,0:T(8,128)(2,1)} %copy-done.1, bf16[224,1024]{1,0:T(8,128)(2,1)} %copy-done.14, bf16[224,1024]{1,0:T(8,128)(2,1)} %copy-done.13, bf16[224,1024]{1,0:T(8,128)(2,1)} %copy-done.12, bf16[224,1024]{1,0:T(8,128)(2,1)} %copy-done.18, ...), custom_call_target="tpu_custom_call" | custom-call | flops 1024 | bytes 1024 | tf_op jit(solution)/shard_map/expert_weights/pallas_call | solution.py:42
  147.4 3.0 %combine_far.1 = (bf16[144,1024]{1,0:T(8,128)(2,1)S(1)}, bf16[144,1024]{1,0:T(8,128)(2,1)S(1)}, bf16[16,512]{1,0:T(8,128)(2,1)S(1)}) custom-call(s32[4]{0:T(128)S(1)} %copy-done.7, f32[4,16,128]{2,1,0:T(8,128)S(1)} %all-to-all-done.meta, bf16[896,512]{1,0:T(8,128)(2,1)S(1)} %get-tuple-element.100.sel, bf16[256,448]{1,0:T(8,128)(2,1)S(1)} %get-tuple-element.99.refs_1_.chosen, ...), custom_call_target="tpu_custom_call" | custom-call | flops 1024 | bytes 1024 | tf_op jit(solution)/shard_map/combine_far/pallas_call | solution.py:42
  150.4 2.1 %collective-permute-start.39 = (bf16[144,1024]{1,0:T(8,128)(2,1)S(1)}, bf16[144,1024]{1,0:T(8,128)(2,1)S(1)}, u32[]{:S(2)}, u32[]{:S(2)}) collective-permute-start(bf16[144,1024]{1,0:T(8,128)(2,1)S(1)} %get-tuple-element.177), channel_id=1, source_target_pairs={{0,16},{2,18},{4,20},{6,22},{8,24},{10,26},{12,28},{14,30},{16,0},... | collective-permute-start | bytes 884744 | tf_op jit(solution)/shard_map/ppermute | solution.py:421
  152.6 1.7 combine_near.1
  154.2 1.5 collective-permute-start.38
  155.7 10.4 %expert_weights.3 = bf16[1,2,704,2048]{3,2,1,0:T(8,128)(2,1)} custom-call(s32[4]{0:T(128)} %copy-done.5, bf16[240,1024]{1,0:T(8,128)(2,1)} %copy-done, bf16[240,1024]{1,0:T(8,128)(2,1)} %collective-permute-done.3.refs_1_, bf16[240,1024]{1,0:T(8,128)(2,1)} %collective-permute-done.4.refs_2_, bf16[240,1024]{1,0:T(8,128)(2,1)} %collective-permute-done.5.refs_3_, ...), custom_call_target="tpu_custom_call" | custom-call | flops 1024 | bytes 1024 | tf_op jit(solution)/shard_map/expert_weights/pallas_call | solution.py:42
  166.1 2.0 %collective-permute-done.39 = bf16[144,1024]{1,0:T(8,128)(2,1)S(1)} collective-permute-done((bf16[144,1024]{1,0:T(8,128)(2,1)S(1)}, bf16[144,1024]{1,0:T(8,128)(2,1)S(1)}, u32[]{:S(2)}, u32[]{:S(2)}) %collective-permute-start.39) | collective-permute-done | bytes 294944 | tf_op jit(solution)/shard_map/ppermute | solution.py:421
  168.2 10.0 %collective-permute-done.40 = bf16[144,1024]{1,0:T(8,128)(2,1)S(1)} collective-permute-done((bf16[144,1024]{1,0:T(8,128)(2,1)S(1)}, bf16[144,1024]{1,0:T(8,128)(2,1)S(1)}, u32[]{:S(2)}, u32[]{:S(2)}) %collective-permute-start.40) | collective-permute-done | bytes 294944 | tf_op jit(solution)/shard_map/ppermute | solution.py:421
  178.8 0.9 add_convert_fusion.4
  (144 shorter events, 14.6 us)
Async XLA Ops:
  0.6 12.3 %collective-permute-start = (bf16[128,1024]{1,0:T(8,128)(2,1)}, bf16[128,1024]{1,0:T(8,128)(2,1)S(1)}, u32[]{:S(2)}, u32[]{:S(2)}) collective-permute-start(bf16[128,1024]{1,0:T(8,128)(2,1)} %refs_0_.1), channel_id=1, source_target_pairs={{0,8},{2,10},{4,12},{6,14},{8,16},{10,18},{12,20},{14,22},{16,24},... | collective-permute-start | bytes 786440 | tf_op jit(solution)/shard_map/ppermute | solution.py:421
  2.0 22.5 %collective-permute-start.1 = (bf16[128,1024]{1,0:T(8,128)(2,1)}, bf16[128,1024]{1,0:T(8,128)(2,1)S(1)}, u32[]{:S(2)}, u32[]{:S(2)}) collective-permute-start(bf16[128,1024]{1,0:T(8,128)(2,1)} %refs_0_.1), channel_id=1, source_target_pairs={{0,16},{2,18},{4,20},{6,22},{8,24},{10,26},{12,28},{14,30},{16,0},... | collective-permute-start | bytes 786440 | tf_op jit(solution)/shard_map/ppermute | solution.py:421
  3.1 24.2 %collective-permute-start.2 = (bf16[128,1024]{1,0:T(8,128)(2,1)}, bf16[128,1024]{1,0:T(8,128)(2,1)S(1)}, u32[]{:S(2)}, u32[]{:S(2)}) collective-permute-start(bf16[128,1024]{1,0:T(8,128)(2,1)} %refs_0_.1), channel_id=1, source_target_pairs={{0,24},{2,26},{4,28},{6,30},{8,0},{10,2},{12,4},{14,6},{16,8},{18,... | collective-permute-start | bytes 786440 | tf_op jit(solution)/shard_map/ppermute | solution.py:421
  5.9 48.1 %copy-start.5 = (s32[4]{0:T(128)}, s32[4]{0:T(128)S(1)}, u32[]{:S(2)}) copy-start(s32[4]{0:T(128)S(1)} %pad_add_fusion.info) | copy-start | bytes 52
  8.0 24.0 %copy-start.2 = (bf16[128,1024]{1,0:T(8,128)(2,1)S(1)}, bf16[128,1024]{1,0:T(8,128)(2,1)}, u32[]{:S(2)}) copy-start(bf16[128,1024]{1,0:T(8,128)(2,1)} %refs_0_.1) | copy-start | bytes 786436
  8.6 19.4 %all-to-all-start = ((f32[4,16,128]{2,1,0:T(8,128)}), f32[4,16,128]{2,1,0:T(8,128)S(1)}, u32[]{:S(2)}, u32[]{:S(2)}) async-start(f32[4,16,128]{2,1,0:T(8,128)} %broadcast_in_dim.4), calls=%async_computation | async-start | bytes 65536 | tf_op jit(solution)/shard_map/all_to_all | solution.py:450
  28.0 26.0 %all-to-all-start.1 = ((bf16[4,128,1024]{2,1,0:T(8,128)(2,1)}), bf16[4,128,1024]{2,1,0:T(8,128)(2,1)S(1)}, u32[]{:S(2)}, u32[]{:S(2)}) async-start(bf16[4,128,1024]{2,1,0:T(8,128)(2,1)} %broadcast_in_dim.5), calls=%async_computation.1 | async-start | bytes 2097152 | tf_op jit(solution)/shard_map/all_to_all | solution.py:450
  36.3 28.7 %copy-start = (bf16[240,1024]{1,0:T(8,128)(2,1)}, bf16[240,1024]{1,0:T(8,128)(2,1)S(1)}, u32[]{:S(2)}) copy-start(bf16[240,1024]{1,0:T(8,128)(2,1)S(1)} %get-tuple-element.108.refs_0_) | copy-start | bytes 1474564
  36.3 19.7 %collective-permute-start.5 = (bf16[240,1024]{1,0:T(8,128)(2,1)}, bf16[240,1024]{1,0:T(8,128)(2,1)}, u32[]{:S(2)}, u32[]{:S(2)}) collective-permute-start(bf16[240,1024]{1,0:T(8,128)(2,1)} %get-tuple-element.96), channel_id=1, source_target_pairs={{0,6},{2,4},{4,2},{6,0},{8,14},{10,12},{12,10},{14,8},{16,22},{18,... | collective-permute-start | bytes 1474568 | tf_op jit(solution)/shard_map/ppermute | solution.py:428
  38.5 22.7 %collective-permute-start.4 = (bf16[240,1024]{1,0:T(8,128)(2,1)}, bf16[240,1024]{1,0:T(8,128)(2,1)}, u32[]{:S(2)}, u32[]{:S(2)}) collective-permute-start(bf16[240,1024]{1,0:T(8,128)(2,1)} %get-tuple-element.95), channel_id=1, source_target_pairs={{0,4},{2,6},{4,0},{6,2},{8,12},{10,14},{12,8},{14,10},{16,20},{18,... | collective-permute-start | bytes 1474568 | tf_op jit(solution)/shard_map/ppermute | solution.py:428
  38.8 23.0 %collective-permute-start.3 = (bf16[240,1024]{1,0:T(8,128)(2,1)}, bf16[240,1024]{1,0:T(8,128)(2,1)}, u32[]{:S(2)}, u32[]{:S(2)}) collective-permute-start(bf16[240,1024]{1,0:T(8,128)(2,1)} %get-tuple-element.94), channel_id=1, source_target_pairs={{0,2},{2,0},{4,6},{6,4},{8,10},{10,8},{12,14},{14,12},{16,18},{18,... | collective-permute-start | bytes 1474568 | tf_op jit(solution)/shard_map/ppermute | solution.py:428
  56.0 32.8 %copy-start.1 = (bf16[224,1024]{1,0:T(8,128)(2,1)}, bf16[224,1024]{1,0:T(8,128)(2,1)S(1)}, u32[]{:S(2)}) copy-start(bf16[224,1024]{1,0:T(8,128)(2,1)S(1)} %get-tuple-element.121.refs_0_) | copy-start | bytes 1376260
  56.0 7.7 %collective-permute-start.9 = (bf16[240,1024]{1,0:T(8,128)(2,1)}, bf16[240,1024]{1,0:T(8,128)(2,1)S(1)}, u32[]{:S(2)}, u32[]{:S(2)}) collective-permute-start(bf16[240,1024]{1,0:T(8,128)(2,1)} %collective-permute-done.5.refs_3_), channel_id=1, source_target_pairs={{0,1},{1,0},{2,3},{3,2},{4,5},{5,4},{6,7},{7,6},{8,9},{9,8},{10,11... | collective-permute-start | bytes 1474568 | tf_op jit(solution)/shard_map/ppermute | solution.py:436
  61.3 3.4 %collective-permute-start.8 = (bf16[240,1024]{1,0:T(8,128)(2,1)}, bf16[240,1024]{1,0:T(8,128)(2,1)S(1)}, u32[]{:S(2)}, u32[]{:S(2)}) collective-permute-start(bf16[240,1024]{1,0:T(8,128)(2,1)} %collective-permute-done.4.refs_2_), channel_id=1, source_target_pairs={{0,1},{1,0},{2,3},{3,2},{4,5},{5,4},{6,7},{7,6},{8,9},{9,8},{10,11... | collective-permute-start | bytes 1474568 | tf_op jit(solution)/shard_map/ppermute | solution.py:436
  61.7 3.2 %collective-permute-start.7 = (bf16[240,1024]{1,0:T(8,128)(2,1)}, bf16[240,1024]{1,0:T(8,128)(2,1)S(1)}, u32[]{:S(2)}, u32[]{:S(2)}) collective-permute-start(bf16[240,1024]{1,0:T(8,128)(2,1)} %collective-permute-done.3.refs_1_), channel_id=1, source_target_pairs={{0,1},{1,0},{2,3},{3,2},{4,5},{5,4},{6,7},{7,6},{8,9},{9,8},{10,11... | collective-permute-start | bytes 1474568 | tf_op jit(solution)/shard_map/ppermute | solution.py:436
  61.8 3.1 %collective-permute-start.6 = (bf16[240,1024]{1,0:T(8,128)(2,1)S(1)}, bf16[240,1024]{1,0:T(8,128)(2,1)S(1)}, u32[]{:S(2)}, u32[]{:S(2)}) collective-permute-start(bf16[240,1024]{1,0:T(8,128)(2,1)S(1)} %get-tuple-element.108.refs_0_), channel_id=1, source_target_pairs={{0,1},{1,0},{2,3},{3,2},{4,5},{5,4},{6,7},{7,6},{8,9},{9,8},{10,11... | collective-permute-start | bytes 1474568 | tf_op jit(solution)/shard_map/ppermute | solution.py:436
  62.3 21.4 %collective-permute-start.19 = (bf16[224,1024]{1,0:T(8,128)(2,1)S(1)}, bf16[224,1024]{1,0:T(8,128)(2,1)S(1)}, u32[]{:S(2)}, u32[]{:S(2)}) collective-permute-start(bf16[224,1024]{1,0:T(8,128)(2,1)S(1)} %get-tuple-element.106), channel_id=1, source_target_pairs={{0,6},{2,4},{4,2},{6,0},{8,14},{10,12},{12,10},{14,8},{16,22},{18,... | collective-permute-start | bytes 1376264 | tf_op jit(solution)/shard_map/ppermute | solution.py:428
  63.7 21.7 %collective-permute-start.18 = (bf16[224,1024]{1,0:T(8,128)(2,1)S(1)}, bf16[224,1024]{1,0:T(8,128)(2,1)S(1)}, u32[]{:S(2)}, u32[]{:S(2)}) collective-permute-start(bf16[224,1024]{1,0:T(8,128)(2,1)S(1)} %get-tuple-element.105), channel_id=1, source_target_pairs={{0,4},{2,6},{4,0},{6,2},{8,12},{10,14},{12,8},{14,10},{16,20},{18,... | collective-permute-start | bytes 1376264 | tf_op jit(solution)/shard_map/ppermute | solution.py:428
  64.7 21.3 %collective-permute-start.17 = (bf16[224,1024]{1,0:T(8,128)(2,1)S(1)}, bf16[224,1024]{1,0:T(8,128)(2,1)S(1)}, u32[]{:S(2)}, u32[]{:S(2)}) collective-permute-start(bf16[224,1024]{1,0:T(8,128)(2,1)S(1)} %get-tuple-element.104), channel_id=1, source_target_pairs={{0,2},{2,0},{4,6},{6,4},{8,10},{10,8},{12,14},{14,12},{16,18},{18,... | collective-permute-start | bytes 1376264 | tf_op jit(solution)/shard_map/ppermute | solution.py:428
  82.6 3.4 %collective-permute-start.15 = (bf16[224,1024]{1,0:T(8,128)(2,1)}, bf16[224,1024]{1,0:T(8,128)(2,1)S(1)}, u32[]{:S(2)}, u32[]{:S(2)}) collective-permute-start(bf16[224,1024]{1,0:T(8,128)(2,1)} %get-tuple-element.119), channel_id=1, source_target_pairs={{0,1},{1,0},{2,3},{3,2},{4,5},{5,4},{6,7},{7,6},{8,9},{9,8},{10,11... | collective-permute-start | bytes 1376264 | tf_op jit(solution)/shard_map/ppermute | solution.py:436
  83.6 4.1 %collective-permute-start.13 = (bf16[224,1024]{1,0:T(8,128)(2,1)}, bf16[224,1024]{1,0:T(8,128)(2,1)S(1)}, u32[]{:S(2)}, u32[]{:S(2)}) collective-permute-start(bf16[224,1024]{1,0:T(8,128)(2,1)} %get-tuple-element.117), channel_id=1, source_target_pairs={{0,1},{1,0},{2,3},{3,2},{4,5},{5,4},{6,7},{7,6},{8,9},{9,8},{10,11... | collective-permute-start | bytes 1376264 | tf_op jit(solution)/shard_map/ppermute | solution.py:436
  83.7 5.1 %collective-permute-start.11 = (bf16[224,1024]{1,0:T(8,128)(2,1)}, bf16[224,1024]{1,0:T(8,128)(2,1)S(1)}, u32[]{:S(2)}, u32[]{:S(2)}) collective-permute-start(bf16[224,1024]{1,0:T(8,128)(2,1)} %get-tuple-element.115), channel_id=1, source_target_pairs={{0,1},{1,0},{2,3},{3,2},{4,5},{5,4},{6,7},{7,6},{8,9},{9,8},{10,11... | collective-permute-start | bytes 1376264 | tf_op jit(solution)/shard_map/ppermute | solution.py:436
  85.5 4.8 %collective-permute-start.10 = (bf16[224,1024]{1,0:T(8,128)(2,1)}, bf16[224,1024]{1,0:T(8,128)(2,1)S(1)}, u32[]{:S(2)}, u32[]{:S(2)}) collective-permute-start(bf16[224,1024]{1,0:T(8,128)(2,1)} %get-tuple-element.113), channel_id=1, source_target_pairs={{0,1},{1,0},{2,3},{3,2},{4,5},{5,4},{6,7},{7,6},{8,9},{9,8},{10,11... | collective-permute-start | bytes 1376264 | tf_op jit(solution)/shard_map/ppermute | solution.py:436
  85.9 5.8 %collective-permute-start.23 = (bf16[224,1024]{1,0:T(8,128)(2,1)S(1)}, bf16[224,1024]{1,0:T(8,128)(2,1)S(1)}, u32[]{:S(2)}, u32[]{:S(2)}) collective-permute-start(bf16[224,1024]{1,0:T(8,128)(2,1)S(1)} %collective-permute-done.19.refs_3_), channel_id=1, source_target_pairs={{0,1},{1,0},{2,3},{3,2},{4,5},{5,4},{6,7},{7,6},{8,9},{9,8},{10,11... | collective-permute-start | bytes 1376264 | tf_op jit(solution)/shard_map/ppermute | solution.py:436
  86.0 6.7 %collective-permute-start.22 = (bf16[224,1024]{1,0:T(8,128)(2,1)S(1)}, bf16[224,1024]{1,0:T(8,128)(2,1)S(1)}, u32[]{:S(2)}, u32[]{:S(2)}) collective-permute-start(bf16[224,1024]{1,0:T(8,128)(2,1)S(1)} %collective-permute-done.18.refs_2_), channel_id=1, source_target_pairs={{0,1},{1,0},{2,3},{3,2},{4,5},{5,4},{6,7},{7,6},{8,9},{9,8},{10,11... | collective-permute-start | bytes 1376264 | tf_op jit(solution)/shard_map/ppermute | solution.py:436
  87.7 5.4 %collective-permute-start.21 = (bf16[224,1024]{1,0:T(8,128)(2,1)S(1)}, bf16[224,1024]{1,0:T(8,128)(2,1)S(1)}, u32[]{:S(2)}, u32[]{:S(2)}) collective-permute-start(bf16[224,1024]{1,0:T(8,128)(2,1)S(1)} %collective-permute-done.17.refs_1_), channel_id=1, source_target_pairs={{0,1},{1,0},{2,3},{3,2},{4,5},{5,4},{6,7},{7,6},{8,9},{9,8},{10,11... | collective-permute-start | bytes 1376264 | tf_op jit(solution)/shard_map/ppermute | solution.py:436
  88.8 4.3 %collective-permute-start.20 = (bf16[224,1024]{1,0:T(8,128)(2,1)S(1)}, bf16[224,1024]{1,0:T(8,128)(2,1)S(1)}, u32[]{:S(2)}, u32[]{:S(2)}) collective-permute-start(bf16[224,1024]{1,0:T(8,128)(2,1)S(1)} %get-tuple-element.121.refs_0_), channel_id=1, source_target_pairs={{0,1},{1,0},{2,3},{3,2},{4,5},{5,4},{6,7},{7,6},{8,9},{9,8},{10,11... | collective-permute-start | bytes 1376264 | tf_op jit(solution)/shard_map/ppermute | solution.py:436
  90.3 22.1 %collective-permute-start.16 = (bf16[224,1024]{1,0:T(8,128)(2,1)S(1)}, bf16[224,1024]{1,0:T(8,128)(2,1)S(1)}, u32[]{:S(2)}, u32[]{:S(2)}) collective-permute-start(bf16[224,1024]{1,0:T(8,128)(2,1)S(1)} %add_convert_fusion), channel_id=1, source_target_pairs={{0,6},{2,4},{4,2},{6,0},{8,14},{10,12},{12,10},{14,8},{16,22},{18,... | collective-permute-start | bytes 1376264 | tf_op jit(solution)/shard_map/ppermute | solution.py:428
  91.8 21.7 %collective-permute-start.14 = (bf16[224,1024]{1,0:T(8,128)(2,1)}, bf16[224,1024]{1,0:T(8,128)(2,1)S(1)}, u32[]{:S(2)}, u32[]{:S(2)}) collective-permute-start(bf16[224,1024]{1,0:T(8,128)(2,1)} %add_convert_fusion.1), channel_id=1, source_target_pairs={{0,4},{2,6},{4,0},{6,2},{8,12},{10,14},{12,8},{14,10},{16,20},{18,... | collective-permute-start | bytes 1376264 | tf_op jit(solution)/shard_map/ppermute | solution.py:428
  92.7 20.8 %collective-permute-start.12 = (bf16[224,1024]{1,0:T(8,128)(2,1)}, bf16[224,1024]{1,0:T(8,128)(2,1)S(1)}, u32[]{:S(2)}, u32[]{:S(2)}) collective-permute-start(bf16[224,1024]{1,0:T(8,128)(2,1)} %add_convert_fusion.2), channel_id=1, source_target_pairs={{0,2},{2,0},{4,6},{6,4},{8,10},{10,8},{12,14},{14,12},{16,18},{18,... | collective-permute-start | bytes 1376264 | tf_op jit(solution)/shard_map/ppermute | solution.py:428
  113.5 11.3 %collective-permute-start.25 = (bf16[128,1024]{1,0:T(8,128)(2,1)}, bf16[128,1024]{1,0:T(8,128)(2,1)}, u32[]{:S(2)}, u32[]{:S(2)}) collective-permute-start(bf16[128,1024]{1,0:T(8,128)(2,1)} %get-tuple-element.138), channel_id=1, source_target_pairs={{0,1},{1,0},{2,3},{3,2},{4,5},{5,4},{6,7},{7,6},{8,9},{9,8},{10,11... | collective-permute-start | bytes 786440 | tf_op jit(solution)/shard_map/ppermute | solution.py:436
  114.0 13.0 %collective-permute-start.33 = (bf16[128,1024]{1,0:T(8,128)(2,1)}, bf16[128,1024]{1,0:T(8,128)(2,1)}, u32[]{:S(2)}, u32[]{:S(2)}) collective-permute-start(bf16[128,1024]{1,0:T(8,128)(2,1)} %get-tuple-element.168), channel_id=1, source_target_pairs={{0,1},{1,0},{2,3},{3,2},{4,5},{5,4},{6,7},{7,6},{8,9},{9,8},{10,11... | collective-permute-start | bytes 786440 | tf_op jit(solution)/shard_map/ppermute | solution.py:436
  118.9 60.8 %all-to-all-start.2 = ((bf16[4,128,1024]{2,1,0:T(8,128)(2,1)}), bf16[4,128,1024]{2,1,0:T(8,128)(2,1)S(1)}, u32[]{:S(2)}, u32[]{:S(2)}) async-start(bf16[4,128,1024]{2,1,0:T(8,128)(2,1)} %combine.1), calls=%async_computation.2 | async-start | bytes 2097152 | tf_op jit(solution)/shard_map/all_to_all | solution.py:450
  123.6 5.7 %collective-permute-start.31 = (bf16[128,1024]{1,0:T(8,128)(2,1)}, bf16[128,1024]{1,0:T(8,128)(2,1)S(1)}, u32[]{:S(2)}, u32[]{:S(2)}) collective-permute-start(bf16[128,1024]{1,0:T(8,128)(2,1)} %get-tuple-element.162), channel_id=1, source_target_pairs={{0,1},{1,0},{2,3},{3,2},{4,5},{5,4},{6,7},{7,6},{8,9},{9,8},{10,11... | collective-permute-start | bytes 786440 | tf_op jit(solution)/shard_map/ppermute | solution.py:436
  124.7 10.8 %collective-permute-start.24 = (bf16[128,1024]{1,0:T(8,128)(2,1)}, bf16[128,1024]{1,0:T(8,128)(2,1)S(1)}, u32[]{:S(2)}, u32[]{:S(2)}) collective-permute-start(bf16[128,1024]{1,0:T(8,128)(2,1)} %get-tuple-element.132), channel_id=1, source_target_pairs={{0,1},{1,0},{2,3},{3,2},{4,5},{5,4},{6,7},{7,6},{8,9},{9,8},{10,11... | collective-permute-start | bytes 786440 | tf_op jit(solution)/shard_map/ppermute | solution.py:436
  125.8 7.5 %collective-permute-start.26 = (bf16[128,1024]{1,0:T(8,128)(2,1)S(1)}, bf16[128,1024]{1,0:T(8,128)(2,1)S(1)}, u32[]{:S(2)}, u32[]{:S(2)}) collective-permute-start(bf16[128,1024]{1,0:T(8,128)(2,1)S(1)} %add_convert_fusion.7), channel_id=1, source_target_pairs={{0,2},{2,0},{4,6},{6,4},{8,10},{10,8},{12,14},{14,12},{16,18},{18,... | collective-permute-start | bytes 786440 | tf_op jit(solution)/shard_map/ppermute | solution.py:428
  128.1 19.3 %collective-permute-start.34 = (bf16[128,1024]{1,0:T(8,128)(2,1)S(1)}, bf16[128,1024]{1,0:T(8,128)(2,1)S(1)}, u32[]{:S(2)}, u32[]{:S(2)}) collective-permute-start(bf16[128,1024]{1,0:T(8,128)(2,1)S(1)} %add_convert_fusion.5), channel_id=1, source_target_pairs={{0,6},{2,4},{4,2},{6,0},{8,14},{10,12},{12,10},{14,8},{16,22},{18,... | collective-permute-start | bytes 786440 | tf_op jit(solution)/shard_map/ppermute | solution.py:428
  129.4 18.0 %collective-permute-start.32 = (bf16[128,1024]{1,0:T(8,128)(2,1)S(1)}, bf16[128,1024]{1,0:T(8,128)(2,1)S(1)}, u32[]{:S(2)}, u32[]{:S(2)}) collective-permute-start(bf16[128,1024]{1,0:T(8,128)(2,1)S(1)} %add_convert_fusion.6), channel_id=1, source_target_pairs={{0,4},{2,6},{4,0},{6,2},{8,12},{10,14},{12,8},{14,10},{16,20},{18,... | collective-permute-start | bytes 786440 | tf_op jit(solution)/shard_map/ppermute | solution.py:428
  133.3 3.3 %collective-permute-start.30 = (bf16[112,1024]{1,0:T(8,128)(2,1)S(1)}, bf16[112,1024]{1,0:T(8,128)(2,1)S(1)}, u32[]{:S(2)}, u32[]{:S(2)}) collective-permute-start(bf16[112,1024]{1,0:T(8,128)(2,1)S(1)} %copy-done.35), channel_id=1, source_target_pairs={{0,1},{1,0},{2,3},{3,2},{4,5},{5,4},{6,7},{7,6},{8,9},{9,8},{10,11... | collective-permute-start | bytes 688136 | tf_op jit(solution)/shard_map/ppermute | solution.py:436
  135.6 1.6 collective-permute-start.29
  135.7 2.9 %collective-permute-start.28 = (bf16[112,1024]{1,0:T(8,128)(2,1)S(1)}, bf16[112,1024]{1,0:T(8,128)(2,1)S(1)}, u32[]{:S(2)}, u32[]{:S(2)}) collective-permute-start(bf16[112,1024]{1,0:T(8,128)(2,1)S(1)} %copy-done.33), channel_id=1, source_target_pairs={{0,1},{1,0},{2,3},{3,2},{4,5},{5,4},{6,7},{7,6},{8,9},{9,8},{10,11... | collective-permute-start | bytes 688136 | tf_op jit(solution)/shard_map/ppermute | solution.py:436
  136.6 3.0 %collective-permute-start.27 = (bf16[112,1024]{1,0:T(8,128)(2,1)S(1)}, bf16[112,1024]{1,0:T(8,128)(2,1)S(1)}, u32[]{:S(2)}, u32[]{:S(2)}) collective-permute-start(bf16[112,1024]{1,0:T(8,128)(2,1)S(1)} %copy-done.32), channel_id=1, source_target_pairs={{0,1},{1,0},{2,3},{3,2},{4,5},{5,4},{6,7},{7,6},{8,9},{9,8},{10,11... | collective-permute-start | bytes 688136 | tf_op jit(solution)/shard_map/ppermute | solution.py:436
  137.1 15.4 %collective-permute-start.37 = (bf16[112,1024]{1,0:T(8,128)(2,1)S(1)}, bf16[112,1024]{1,0:T(8,128)(2,1)S(1)}, u32[]{:S(2)}, u32[]{:S(2)}) collective-permute-start(bf16[112,1024]{1,0:T(8,128)(2,1)S(1)} %add_convert_fusion.9), channel_id=1, source_target_pairs={{0,6},{2,4},{4,2},{6,0},{8,14},{10,12},{12,10},{14,8},{16,22},{18,... | collective-permute-start | bytes 688136 | tf_op jit(solution)/shard_map/ppermute | solution.py:428
  138.6 14.0 %collective-permute-start.36 = (bf16[112,1024]{1,0:T(8,128)(2,1)S(1)}, bf16[112,1024]{1,0:T(8,128)(2,1)S(1)}, u32[]{:S(2)}, u32[]{:S(2)}) collective-permute-start(bf16[112,1024]{1,0:T(8,128)(2,1)S(1)} %add_convert_fusion.10), channel_id=1, source_target_pairs={{0,4},{2,6},{4,0},{6,2},{8,12},{10,14},{12,8},{14,10},{16,20},{18,... | collective-permute-start | bytes 688136 | tf_op jit(solution)/shard_map/ppermute | solution.py:428
  139.7 12.9 %collective-permute-start.35 = (bf16[112,1024]{1,0:T(8,128)(2,1)S(1)}, bf16[112,1024]{1,0:T(8,128)(2,1)S(1)}, u32[]{:S(2)}, u32[]{:S(2)}) collective-permute-start(bf16[112,1024]{1,0:T(8,128)(2,1)S(1)} %add_convert_fusion.11), channel_id=1, source_target_pairs={{0,2},{2,0},{4,6},{6,4},{8,10},{10,8},{12,14},{14,12},{16,18},{18,... | collective-permute-start | bytes 688136 | tf_op jit(solution)/shard_map/ppermute | solution.py:428
  150.4 17.8 %collective-permute-start.39 = (bf16[144,1024]{1,0:T(8,128)(2,1)S(1)}, bf16[144,1024]{1,0:T(8,128)(2,1)S(1)}, u32[]{:S(2)}, u32[]{:S(2)}) collective-permute-start(bf16[144,1024]{1,0:T(8,128)(2,1)S(1)} %get-tuple-element.177), channel_id=1, source_target_pairs={{0,16},{2,18},{4,20},{6,22},{8,24},{10,26},{12,28},{14,30},{16,0},... | collective-permute-start | bytes 884744 | tf_op jit(solution)/shard_map/ppermute | solution.py:421
  152.5 25.6 %collective-permute-start.40 = (bf16[144,1024]{1,0:T(8,128)(2,1)S(1)}, bf16[144,1024]{1,0:T(8,128)(2,1)S(1)}, u32[]{:S(2)}, u32[]{:S(2)}) collective-permute-start(bf16[144,1024]{1,0:T(8,128)(2,1)S(1)} %get-tuple-element.178), channel_id=1, source_target_pairs={{0,8},{2,10},{4,12},{6,14},{8,16},{10,18},{12,20},{14,22},{16,24},... | collective-permute-start | bytes 884744 | tf_op jit(solution)/shard_map/ppermute | solution.py:421
  154.2 24.0 %collective-permute-start.38 = (bf16[144,1024]{1,0:T(8,128)(2,1)S(1)}, bf16[144,1024]{1,0:T(8,128)(2,1)S(1)}, u32[]{:S(2)}, u32[]{:S(2)}) collective-permute-start(bf16[144,1024]{1,0:T(8,128)(2,1)S(1)} %get-tuple-element.176), channel_id=1, source_target_pairs={{0,24},{2,26},{4,28},{6,30},{8,0},{10,2},{12,4},{14,6},{16,8},{18,... | collective-permute-start | bytes 884744 | tf_op jit(solution)/shard_map/ppermute | solution.py:421
  (32 other events, 203.8 us)

commit v2 on v0

--- a/solution.py
+++ b/solution.py
@@ -10,8 +10,10 @@
 PLANE = 4
 CHUNKS = 1
 RETURNS = 2
+BLOCKS = 1
 TAIL = 16
 VMEM_LIMIT = 56 * 1024 * 1024
+SMALL_LIMIT = 16 * 1024 * 1024
 F32 = jnp.float32
 BF16 = jnp.bfloat16
 
@@ -37,14 +39,14 @@
 HBM = pl.BlockSpec(memory_space=pl.ANY)
 
 
-def call(kernel, outs, args, specs, out_specs=None, scratch=(), name=None):
+def call(kernel, outs, args, specs, out_specs=None, scratch=(), name=None, limit=SMALL_LIMIT):
     return pl.pallas_call(
         kernel,
         out_shape=outs,
         in_specs=specs,
         out_specs=out_specs if out_specs is not None else [VMEM] * len(outs),
         scratch_shapes=list(scratch),
-        compiler_params=pltpu.CompilerParams(vmem_limit_bytes=VMEM_LIMIT),
+        compiler_params=pltpu.CompilerParams(vmem_limit_bytes=limit),
         cost_estimate=pl.CostEstimate(flops=1024, bytes_accessed=1024, transcendentals=0),
         name=name,
     )(*args)
@@ -244,9 +246,10 @@
             loads.add(("r", g, j, q), pieces[g * pn + q].at[pl.ds(0, rows)], to)
 
 
-def halves(pn):
+def blocks(pn):
     units = [(g, q) for g in range(CHUNKS) for q in range(pn)]
-    return units[: len(units) // 2], units[len(units) // 2 :]
+    size = len(units) // BLOCKS
+    return [units[b * size : (b + 1) * size] for b in range(BLOCKS)]
 
 
 def forward_kernel(info, *refs, nt, pn, rows, cols):
@@ -267,7 +270,7 @@
     load_weight(loads, info, "d", wout.at[0], wd, every, nt, cols)
     same = iota((rows, rows), 0) == iota((rows, rows), 1)
     tail_step = tail_lanes(rows)
-    for b, units in enumerate(halves(pn)):
+    for b, units in enumerate(blocks(pn)):
         here = slice(b * len(units) * rows, (b + 1) * len(units) * rows)
         loads.need(*(("r", g, j, q) for j in every for g, q in units))
         loads.need(*(("g", j) for j in every))
@@ -325,7 +328,7 @@
     same = iota((rows, rows), 0) == iota((rows, rows), 1)
     tail_step = tail_lanes(rows)
     bottom = slice(CHUNKS * rows, CHUNKS * rows + TAIL)
-    for b, units in enumerate(halves(pn)):
+    for b, units in enumerate(blocks(pn)):
         here = slice(b * len(units) * rows, (b + 1) * len(units) * rows)
         loads.need(*(("r", g, j, q) for j in every for g, q in units))
         loads.need(*(("d", j) for j in every))
@@ -461,7 +464,7 @@
         return jnp.broadcast_to(value[None], (zn,) + value.shape)
 
     grad_copies = copies(second_grad)
-    meta = outer_exchange(after(copies(own), grad_copies))
+    meta = outer_exchange(after(copies(own), grad_copies, info))
     dma = pltpu.SemaphoreType.DMA
     sizes = dict(nt=nt, pn=pn, rows=part_rows, cols=cols)
 
@@ -551,8 +554,8 @@
     c_packed = pack(after(gathered, *chosen))
     c_here = inner_exchange(c_packed)
 
+    pieces = nt * CHUNKS * pn
     xs = swapped(([after(piece, *c_packed) for piece in x_here],))
-    pieces = nt * CHUNKS * pn
     forward = call(
         functools.partial(forward_kernel, **sizes),
         [shape(rows, cols)] * (nt * pn) + [shape(slots, hid_n)] * 4,
@@ -563,8 +566,9 @@
         + [pltpu.VMEM((hid_n, nt * cols), BF16)] * 3
         + [pltpu.VMEM((4, slots, hid_n), BF16)]
         + [pltpu.VMEM((nt, pn, rows, cols), BF16), dma((3 * nt + pieces + pn,))]
-        + [dma((nt * pn + 8,))],
+        + [dma((nt * pn + 4 * BLOCKS,))],
         name="expert_forward",
+        limit=VMEM_LIMIT,
     )
     outs, (hs, hid, a1, a2) = forward[: nt * pn], forward[nt * pn :]
     cs = swapped(([after(piece, hid) for piece in c_here],))
@@ -587,8 +591,9 @@
         + [pltpu.VMEM((hid_n, nt * cols), BF16)] * 3
         + [pltpu.VMEM((2, slots, hid_n), BF16)]
         + [pltpu.VMEM((nt, pn, rows + TAIL, cols), BF16), dma((3 * nt + pieces + 3,))]
-        + [dma((RETURNS * nt * pn + 4,))],
+        + [dma((RETURNS * nt * pn + 2 * BLOCKS,))],
         name="expert_backward",
+        limit=VMEM_LIMIT,
     )
     grads, (gg, ug) = backward[: RETURNS * nt * pn], backward[RETURNS * nt * pn :]
     near, far = grads[: nt * pn], grads[nt * pn :]
@@ -597,7 +602,7 @@
     far = [after(part, *out_back) for part in far]
     far_here = core_sum([after(part, out_combined) for part in far[:pn]] + far[pn:])
     far_back = inner_exchange(far_here)
-    near_here = core_sum([after(part, far_back[1]) for part in near])
+    near_here = core_sum([after(part, far_back[pn - 1]) for part in near])
     near_back = inner_exchange(near_here)
 
     far_parts, gate_parts = combine_far([after(piece, *near_here) for piece in far_back])
@@ -617,6 +622,7 @@
             dma((3 * nt,)),
         ],
         name="expert_weights",
+        limit=VMEM_LIMIT,
     )
 
     branch = jnp.sum(after(out_parts, grad_in).astype(F32), axis=0)

time: 181 us -> 180 us (level)
  the two profiles are of different devices: /device:TPU:0 before, /device:TPU:9 now
where the time goes in v2:
time: 180 us; the launch traced here: 176 us
  Pallas kernels  67.4 us (37%)
  waiting for transfers between devices  47.5 us (26%)
  starting transfers between devices  43.8 us (24%)
  other arithmetic  9.6 us (5%)
  local copies, waits for them, and re-layouts  6.94 us (4%)
    pallas_call x9, Pallas kernels, call(): pl.pallas_call(kernel, out_shape=outs, in_specs=specs, out_specs=out_spec...  67.4 us
    ppermute x6, waiting for transfers between devices, outer_send(): lax.ppermute(value, 'expert', [(e, (e // pn + s) % zn * pn + e % pn) for...  20.4 us
    ppermute x15, starting transfers between devices, inner_send(): return lax.ppermute(value, 'expert', [(e, e ^ q) for e in range(groups)])  13.7 us
    ppermute x15, waiting for transfers between devices, inner_send(): return lax.ppermute(value, 'expert', [(e, e ^ q) for e in range(groups)])  13.5 us
    all_to_all x3, starting transfers between devices, outer_exchange(): lax.all_to_all(value, 'expert', split_axis=0, concat_axis=0, axis_index_g...  13 us
    all_to_all x3, waiting for transfers between devices, outer_exchange(): lax.all_to_all(value, 'expert', split_axis=0, concat_axis=0, axis_index_g...  12.8 us
    ppermute x20, starting transfers between devices, tensor_send(): return lax.ppermute(value, 'tensor', [(c, (c + j) % nt) for c in range(nt)])  11.1 us
    ppermute x6, starting transfers between devices, outer_send(): lax.ppermute(value, 'expert', [(e, (e // pn + s) % zn * pn + e % pn) for...  6.04 us
  transfers between devices with their start and end apart: 44, of which 12 were waited for; matrix products, arithmetic and copies ran while one was open for 6% of the time, Pallas kernels for 38%

profile of v2, /device:TPU:9, one launch (start us, length us, event | category | flops | bytes accessed | tf_op | source)
XLA Modules:
  0.0 176.4 jit_solution(18424603833908172472)
XLA Ops:
  0.6 1.3 collective-permute-start
  2.0 1.1 collective-permute-start.1
  3.1 1.4 collective-permute-start.2
  5.9 2.0 %broadcast_in_dim.5 = bf16[4,128,1024]{2,1,0:T(8,128)(2,1)} broadcast(bf16[128,1024]{1,0:T(8,128)(2,1)} %param.11), dimensions={1,2} | broadcast | bytes 1310720 | tf_op jit(solution)/shard_map/broadcast_in_dim | solution.py:464
  8.6 4.3 %all-to-all-start = ((f32[4,16,128]{2,1,0:T(8,128)}), f32[4,16,128]{2,1,0:T(8,128)S(1)}, u32[]{:S(2)}, u32[]{:S(2)}) async-start(f32[4,16,128]{2,1,0:T(8,128)} %broadcast_in_dim.4), calls=%async_computation | async-start | bytes 65536 | tf_op jit(solution)/shard_map/all_to_all | solution.py:454
  12.9 11.6 %collective-permute-done.1.refs_2_ = bf16[128,1024]{1,0:T(8,128)(2,1)S(1)} collective-permute-done((bf16[128,1024]{1,0:T(8,128)(2,1)}, bf16[128,1024]{1,0:T(8,128)(2,1)S(1)}, u32[]{:S(2)}, u32[]{:S(2)}) %collective-permute-start.1) | collective-permute-done | bytes 262176 | tf_op jit(solution)/shard_map/ppermute | solution.py:425
  24.5 2.8 %collective-permute-done.2.refs_3_ = bf16[128,1024]{1,0:T(8,128)(2,1)S(1)} collective-permute-done((bf16[128,1024]{1,0:T(8,128)(2,1)}, bf16[128,1024]{1,0:T(8,128)(2,1)S(1)}, u32[]{:S(2)}, u32[]{:S(2)}) %collective-permute-start.2) | collective-permute-done | bytes 262176 | tf_op jit(solution)/shard_map/ppermute | solution.py:425
  28.0 4.0 %all-to-all-start.1 = ((bf16[4,128,1024]{2,1,0:T(8,128)(2,1)}), bf16[4,128,1024]{2,1,0:T(8,128)(2,1)S(1)}, u32[]{:S(2)}, u32[]{:S(2)}) async-start(bf16[4,128,1024]{2,1,0:T(8,128)(2,1)} %broadcast_in_dim.5), calls=%async_computation.1 | async-start | bytes 2097152 | tf_op jit(solution)/shard_map/all_to_all | solution.py:454
  32.0 0.9 copy-done.4
  32.9 3.3 %pack_gates.1 = (bf16[240,1024]{1,0:T(8,128)(2,1)S(1)}, bf16[240,1024]{1,0:T(8,128)(2,1)}, bf16[240,1024]{1,0:T(8,128)(2,1)}, bf16[240,1024]{1,0:T(8,128)(2,1)}, bf16[896,512]{1,0:T(8,128)(2,1)S(1)}) custom-call(s32[4]{0:T(128)S(1)} %pad_add_fusion.info, f32[4,16,128]{2,1,0:T(8,128)S(1)} %all-to-all-done.meta, bf16[128,1024]{1,0:T(8,128)(2,1)S(1)} %copy-done.2, ...), custom_call_target="tpu_custom_call" | custom-call | flops 1024 | bytes 1024 | tf_op jit(solution)/shard_map/pack_gates/pallas_call | solution.py:43
  36.3 2.2 %collective-permute-start.5 = (bf16[240,1024]{1,0:T(8,128)(2,1)}, bf16[240,1024]{1,0:T(8,128)(2,1)}, u32[]{:S(2)}, u32[]{:S(2)}) collective-permute-start(bf16[240,1024]{1,0:T(8,128)(2,1)} %get-tuple-element.97), channel_id=1, source_target_pairs={{0,6},{2,4},{4,2},{6,0},{8,14},{10,12},{12,10},{14,8},{16,22},{18,... | collective-permute-start | bytes 1474568 | tf_op jit(solution)/shard_map/ppermute | solution.py:432
  39.0 2.2 %route.1 = (bf16[256,448]{1,0:T(8,128)(2,1)S(1)}, bf16[256,448]{1,0:T(8,128)(2,1)S(1)}) custom-call(s32[4]{0:T(128)S(1)} %pad_add_fusion.info, f32[4,16,128]{2,1,0:T(8,128)S(1)} %all-to-all-done.meta), custom_call_target="tpu_custom_call" | custom-call | flops 1024 | bytes 1024 | tf_op jit(solution)/shard_map/route/pallas_call | solution.py:43
  41.2 12.8 %all-to-all-done.1.source = bf16[4,128,1024]{2,1,0:T(8,128)(2,1)S(1)} async-done(((bf16[4,128,1024]{2,1,0:T(8,128)(2,1)}), bf16[4,128,1024]{2,1,0:T(8,128)(2,1)S(1)}, u32[]{:S(2)}, u32[]{:S(2)}) %all-to-all-start.1) | async-done | bytes 1048608 | tf_op jit(solution)/shard_map/all_to_all | solution.py:454
  54.0 2.0 %pack.1 = (bf16[224,1024]{1,0:T(8,128)(2,1)S(1)}, bf16[224,1024]{1,0:T(8,128)(2,1)S(1)}, bf16[224,1024]{1,0:T(8,128)(2,1)S(1)}, bf16[224,1024]{1,0:T(8,128)(2,1)S(1)}) custom-call(s32[4]{0:T(128)S(1)} %pad_add_fusion.info, bf16[896,512]{1,0:T(8,128)(2,1)S(1)} %get-tuple-element.101.sel, bf16[4,128,1024]{2,1,0:T(8,128)(2,1)S(1)} %all-to-all-done.1.source), custom_call_target="tpu_custom_call" | custom-call | flops 1024 | bytes 1024 | tf_op jit(solution)/shard_map/pack/pallas_call | solution.py:43
  56.0 1.7 collective-permute-start.9
  57.8 3.5 %collective-permute-done.4.refs_2_ = bf16[240,1024]{1,0:T(8,128)(2,1)} collective-permute-done((bf16[240,1024]{1,0:T(8,128)(2,1)}, bf16[240,1024]{1,0:T(8,128)(2,1)}, u32[]{:S(2)}, u32[]{:S(2)}) %collective-permute-start.4) | collective-permute-done | bytes 491552 | tf_op jit(solution)/shard_map/ppermute | solution.py:432
  62.3 1.5 collective-permute-start.19
  63.7 0.9 collective-permute-start.18
  65.7 0.8 copy-done.10
  66.6 17.1 %expert_forward.1 = (bf16[224,1024]{1,0:T(8,128)(2,1)}, bf16[224,1024]{1,0:T(8,128)(2,1)}, bf16[224,1024]{1,0:T(8,128)(2,1)}, bf16[224,1024]{1,0:T(8,128)(2,1)},...) custom-call(s32[4]{0:T(128)} %copy-done.5, ...), custom_call_target="tpu_custom_call" | custom-call | flops 1024 | bytes 1024 | tf_op jit(solution)/shard_map/expert_forward/pallas_call | solution.py:43
  83.7 1.0 collective-permute-start.15
  86.7 1.2 add_convert_fusion
  88.1 1.0 add_convert_fusion.1
  89.6 0.9 add_convert_fusion.2
  90.5 1.4 collective-permute-start.16
  91.9 1.0 collective-permute-start.14
  94.3 19.4 %expert_backward.1 = (bf16[112,1024]{1,0:T(8,128)(2,1)}, bf16[112,1024]{1,0:T(8,128)(2,1)}, bf16[112,1024]{1,0:T(8,128)(2,1)}, bf16[112,1024]{1,0:T(8,128)(2,1)}...) custom-call(s32[4]{0:T(128)} %copy-done.5, ...), custom_call_target="tpu_custom_call" | custom-call | flops 1024 | bytes 1024 | tf_op jit(solution)/shard_map/expert_backward/pallas_call | solution.py:43
  113.7 1.1 collective-permute-start.25
  114.9 4.9 %combine.1 = bf16[4,128,1024]{2,1,0:T(8,128)(2,1)} custom-call(s32[4]{0:T(128)S(1)} %copy-done.6, bf16[256,448]{1,0:T(8,128)(2,1)S(1)} %get-tuple-element.99.refs_0_.chosen, bf16[256,448]{1,0:T(8,128)(2,1)S(1)} %get-tuple-element.100.refs_1_.chosen, bf16[224,1024]{1,0:T(8,128)(2,1)S(1)} %add_convert_fusion.3.refs_2_, ...), custom_call_target="tpu_custom_call" | custom-call | flops 1024 | bytes 1024 | tf_op jit(solution)/shard_map/combine/pallas_call | solution.py:43
  119.8 4.7 %all-to-all-start.2 = ((bf16[4,128,1024]{2,1,0:T(8,128)(2,1)}), bf16[4,128,1024]{2,1,0:T(8,128)(2,1)S(1)}, u32[]{:S(2)}, u32[]{:S(2)}) async-start(bf16[4,128,1024]{2,1,0:T(8,128)(2,1)} %combine.1), calls=%async_computation.2 | async-start | bytes 2097152 | tf_op jit(solution)/shard_map/all_to_all | solution.py:454
  124.5 1.0 collective-permute-start.31
  125.5 1.0 add_convert_fusion.7
  126.6 1.4 collective-permute-start.26
  128.0 1.0 add_convert_fusion.5
  129.1 1.1 collective-permute-start.34
  130.6 4.5 %collective-permute-done.26.refs_3_ = bf16[128,1024]{1,0:T(8,128)(2,1)S(1)} collective-permute-done((bf16[128,1024]{1,0:T(8,128)(2,1)S(1)}, bf16[128,1024]{1,0:T(8,128)(2,1)S(1)}, u32[]{:S(2)}, u32[]{:S(2)}) %collective-permute-start.26) | collective-permute-done | bytes 262176 | tf_op jit(solution)/shard_map/ppermute | solution.py:432
  135.1 2.2 %collective-permute-start.30 = (bf16[112,1024]{1,0:T(8,128)(2,1)S(1)}, bf16[112,1024]{1,0:T(8,128)(2,1)S(1)}, u32[]{:S(2)}, u32[]{:S(2)}) collective-permute-start(bf16[112,1024]{1,0:T(8,128)(2,1)S(1)} %copy-done.34), channel_id=1, source_target_pairs={{0,1},{1,0},{2,3},{3,2},{4,5},{5,4},{6,7},{7,6},{8,9},{9,8},{10,11... | collective-permute-start | bytes 688136 | tf_op jit(solution)/shard_map/ppermute | solution.py:440
  138.9 1.4 collective-permute-start.37
  140.3 1.1 collective-permute-start.36
  141.9 3.0 %combine_far.1 = (bf16[144,1024]{1,0:T(8,128)(2,1)S(1)}, bf16[144,1024]{1,0:T(8,128)(2,1)S(1)}, bf16[16,512]{1,0:T(8,128)(2,1)S(1)}) custom-call(s32[4]{0:T(128)S(1)} %copy-done.6, f32[4,16,128]{2,1,0:T(8,128)S(1)} %all-to-all-done.meta, bf16[896,512]{1,0:T(8,128)(2,1)S(1)} %get-tuple-element.101.sel, ...), custom_call_target="tpu_custom_call" | custom-call | flops 1024 | bytes 1024 | tf_op jit(solution)/shard_map/combine_far/pallas_call | solution.py:43
  144.9 2.2 %collective-permute-start.39 = (bf16[144,1024]{1,0:T(8,128)(2,1)S(1)}, bf16[144,1024]{1,0:T(8,128)(2,1)S(1)}, u32[]{:S(2)}, u32[]{:S(2)}) collective-permute-start(bf16[144,1024]{1,0:T(8,128)(2,1)S(1)} %get-tuple-element.178), channel_id=1, source_target_pairs={{0,16},{2,18},{4,20},{6,22},{8,24},{10,26},{12,28},{14,30},{16,0},... | collective-permute-start | bytes 884744 | tf_op jit(solution)/shard_map/ppermute | solution.py:425
  147.0 5.2 %collective-permute-done.36.refs_2_ = bf16[112,1024]{1,0:T(8,128)(2,1)S(1)} collective-permute-done((bf16[112,1024]{1,0:T(8,128)(2,1)S(1)}, bf16[112,1024]{1,0:T(8,128)(2,1)S(1)}, u32[]{:S(2)}, u32[]{:S(2)}) %collective-permute-start.36) | collective-permute-done | bytes 229408 | tf_op jit(solution)/shard_map/ppermute | solution.py:432
  152.2 1.6 combine_near.1
  153.9 13.9 %expert_weights.1 = (bf16[1,2,704,2048]{3,2,1,0:T(8,128)(2,1)}, bf16[1,704,2048]{2,1,0:T(8,128)(2,1)}) custom-call(s32[4]{0:T(128)} %copy-done.5, bf16[240,1024]{1,0:T(8,128)(2,1)} %copy-done, bf16[240,1024]{1,0:T(8,128)(2,1)} %collective-permute-done.3.refs_1_, bf16[240,1024]{1,0:T(8,128)(2,1)} %collective-permute-done.4.refs_2_, ...), custom_call_target="tpu_custom_call" | custom-call | flops 1024 | bytes 1024 | tf_op jit(solution)/shard_map/expert_weights/pallas_call | solution.py:43
  167.8 5.0 %collective-permute-done.40 = bf16[144,1024]{1,0:T(8,128)(2,1)S(1)} collective-permute-done((bf16[144,1024]{1,0:T(8,128)(2,1)S(1)}, bf16[144,1024]{1,0:T(8,128)(2,1)S(1)}, u32[]{:S(2)}, u32[]{:S(2)}) %collective-permute-start.40) | collective-permute-done | bytes 294944 | tf_op jit(solution)/shard_map/ppermute | solution.py:425
  172.9 1.0 collective-permute-done.38
  174.5 0.9 add_convert_fusion.4
  175.6 0.8 subtract_convert_fusion
  (141 shorter events, 13.0 us)
Async XLA Ops:
  0.6 12.3 %collective-permute-start = (bf16[128,1024]{1,0:T(8,128)(2,1)}, bf16[128,1024]{1,0:T(8,128)(2,1)S(1)}, u32[]{:S(2)}, u32[]{:S(2)}) collective-permute-start(bf16[128,1024]{1,0:T(8,128)(2,1)} %refs_0_.1), channel_id=1, source_target_pairs={{0,8},{2,10},{4,12},{6,14},{8,16},{10,18},{12,20},{14,22},{16,24},... | collective-permute-start | bytes 786440 | tf_op jit(solution)/shard_map/ppermute | solution.py:425
  2.0 22.5 %collective-permute-start.1 = (bf16[128,1024]{1,0:T(8,128)(2,1)}, bf16[128,1024]{1,0:T(8,128)(2,1)S(1)}, u32[]{:S(2)}, u32[]{:S(2)}) collective-permute-start(bf16[128,1024]{1,0:T(8,128)(2,1)} %refs_0_.1), channel_id=1, source_target_pairs={{0,16},{2,18},{4,20},{6,22},{8,24},{10,26},{12,28},{14,30},{16,0},... | collective-permute-start | bytes 786440 | tf_op jit(solution)/shard_map/ppermute | solution.py:425
  3.1 24.2 %collective-permute-start.2 = (bf16[128,1024]{1,0:T(8,128)(2,1)}, bf16[128,1024]{1,0:T(8,128)(2,1)S(1)}, u32[]{:S(2)}, u32[]{:S(2)}) collective-permute-start(bf16[128,1024]{1,0:T(8,128)(2,1)} %refs_0_.1), channel_id=1, source_target_pairs={{0,24},{2,26},{4,28},{6,30},{8,0},{10,2},{12,4},{14,6},{16,8},{18,... | collective-permute-start | bytes 786440 | tf_op jit(solution)/shard_map/ppermute | solution.py:425
  5.9 48.1 %copy-start.5 = (s32[4]{0:T(128)}, s32[4]{0:T(128)S(1)}, u32[]{:S(2)}) copy-start(s32[4]{0:T(128)S(1)} %pad_add_fusion.info) | copy-start | bytes 52
  8.0 24.0 %copy-start.2 = (bf16[128,1024]{1,0:T(8,128)(2,1)S(1)}, bf16[128,1024]{1,0:T(8,128)(2,1)}, u32[]{:S(2)}) copy-start(bf16[128,1024]{1,0:T(8,128)(2,1)} %refs_0_.1) | copy-start | bytes 786436
  8.6 19.4 %all-to-all-start = ((f32[4,16,128]{2,1,0:T(8,128)}), f32[4,16,128]{2,1,0:T(8,128)S(1)}, u32[]{:S(2)}, u32[]{:S(2)}) async-start(f32[4,16,128]{2,1,0:T(8,128)} %broadcast_in_dim.4), calls=%async_computation | async-start | bytes 65536 | tf_op jit(solution)/shard_map/all_to_all | solution.py:454
  28.0 26.0 %all-to-all-start.1 = ((bf16[4,128,1024]{2,1,0:T(8,128)(2,1)}), bf16[4,128,1024]{2,1,0:T(8,128)(2,1)S(1)}, u32[]{:S(2)}, u32[]{:S(2)}) async-start(bf16[4,128,1024]{2,1,0:T(8,128)(2,1)} %broadcast_in_dim.5), calls=%async_computation.1 | async-start | bytes 2097152 | tf_op jit(solution)/shard_map/all_to_all | solution.py:454
  36.3 28.7 %copy-start = (bf16[240,1024]{1,0:T(8,128)(2,1)}, bf16[240,1024]{1,0:T(8,128)(2,1)S(1)}, u32[]{:S(2)}) copy-start(bf16[240,1024]{1,0:T(8,128)(2,1)S(1)} %get-tuple-element.109.refs_0_) | copy-start | bytes 1474564
  36.3 19.7 %collective-permute-start.5 = (bf16[240,1024]{1,0:T(8,128)(2,1)}, bf16[240,1024]{1,0:T(8,128)(2,1)}, u32[]{:S(2)}, u32[]{:S(2)}) collective-permute-start(bf16[240,1024]{1,0:T(8,128)(2,1)} %get-tuple-element.97), channel_id=1, source_target_pairs={{0,6},{2,4},{4,2},{6,0},{8,14},{10,12},{12,10},{14,8},{16,22},{18,... | collective-permute-start | bytes 1474568 | tf_op jit(solution)/shard_map/ppermute | solution.py:432
  38.5 22.7 %collective-permute-start.4 = (bf16[240,1024]{1,0:T(8,128)(2,1)}, bf16[240,1024]{1,0:T(8,128)(2,1)}, u32[]{:S(2)}, u32[]{:S(2)}) collective-permute-start(bf16[240,1024]{1,0:T(8,128)(2,1)} %get-tuple-element.96), channel_id=1, source_target_pairs={{0,4},{2,6},{4,0},{6,2},{8,12},{10,14},{12,8},{14,10},{16,20},{18,... | collective-permute-start | bytes 1474568 | tf_op jit(solution)/shard_map/ppermute | solution.py:432
  38.8 23.0 %collective-permute-start.3 = (bf16[240,1024]{1,0:T(8,128)(2,1)}, bf16[240,1024]{1,0:T(8,128)(2,1)}, u32[]{:S(2)}, u32[]{:S(2)}) collective-permute-start(bf16[240,1024]{1,0:T(8,128)(2,1)} %get-tuple-element.95), channel_id=1, source_target_pairs={{0,2},{2,0},{4,6},{6,4},{8,10},{10,8},{12,14},{14,12},{16,18},{18,... | collective-permute-start | bytes 1474568 | tf_op jit(solution)/shard_map/ppermute | solution.py:432
  56.0 33.1 %copy-start.1 = (bf16[224,1024]{1,0:T(8,128)(2,1)}, bf16[224,1024]{1,0:T(8,128)(2,1)S(1)}, u32[]{:S(2)}) copy-start(bf16[224,1024]{1,0:T(8,128)(2,1)S(1)} %get-tuple-element.122.refs_0_.refs_8_) | copy-start | bytes 1376260
  56.0 7.7 %collective-permute-start.9 = (bf16[240,1024]{1,0:T(8,128)(2,1)}, bf16[240,1024]{1,0:T(8,128)(2,1)S(1)}, u32[]{:S(2)}, u32[]{:S(2)}) collective-permute-start(bf16[240,1024]{1,0:T(8,128)(2,1)} %collective-permute-done.5.refs_3_), channel_id=1, source_target_pairs={{0,1},{1,0},{2,3},{3,2},{4,5},{5,4},{6,7},{7,6},{8,9},{9,8},{10,11... | collective-permute-start | bytes 1474568 | tf_op jit(solution)/shard_map/ppermute | solution.py:440
  61.3 3.4 %collective-permute-start.8 = (bf16[240,1024]{1,0:T(8,128)(2,1)}, bf16[240,1024]{1,0:T(8,128)(2,1)S(1)}, u32[]{:S(2)}, u32[]{:S(2)}) collective-permute-start(bf16[240,1024]{1,0:T(8,128)(2,1)} %collective-permute-done.4.refs_2_), channel_id=1, source_target_pairs={{0,1},{1,0},{2,3},{3,2},{4,5},{5,4},{6,7},{7,6},{8,9},{9,8},{10,11... | collective-permute-start | bytes 1474568 | tf_op jit(solution)/shard_map/ppermute | solution.py:440
  61.7 3.2 %collective-permute-start.7 = (bf16[240,1024]{1,0:T(8,128)(2,1)}, bf16[240,1024]{1,0:T(8,128)(2,1)S(1)}, u32[]{:S(2)}, u32[]{:S(2)}) collective-permute-start(bf16[240,1024]{1,0:T(8,128)(2,1)} %collective-permute-done.3.refs_1_), channel_id=1, source_target_pairs={{0,1},{1,0},{2,3},{3,2},{4,5},{5,4},{6,7},{7,6},{8,9},{9,8},{10,11... | collective-permute-start | bytes 1474568 | tf_op jit(solution)/shard_map/ppermute | solution.py:440
  61.8 3.1 %collective-permute-start.6 = (bf16[240,1024]{1,0:T(8,128)(2,1)S(1)}, bf16[240,1024]{1,0:T(8,128)(2,1)S(1)}, u32[]{:S(2)}, u32[]{:S(2)}) collective-permute-start(bf16[240,1024]{1,0:T(8,128)(2,1)S(1)} %get-tuple-element.109.refs_0_), channel_id=1, source_target_pairs={{0,1},{1,0},{2,3},{3,2},{4,5},{5,4},{6,7},{7,6},{8,9},{9,8},{10,11... | collective-permute-start | bytes 1474568 | tf_op jit(solution)/shard_map/ppermute | solution.py:440
  62.3 22.5 %collective-permute-start.19 = (bf16[224,1024]{1,0:T(8,128)(2,1)S(1)}, bf16[224,1024]{1,0:T(8,128)(2,1)S(1)}, u32[]{:S(2)}, u32[]{:S(2)}) collective-permute-start(bf16[224,1024]{1,0:T(8,128)(2,1)S(1)} %get-tuple-element.107), channel_id=1, source_target_pairs={{0,6},{2,4},{4,2},{6,0},{8,14},{10,12},{12,10},{14,8},{16,22},{18,... | collective-permute-start | bytes 1376264 | tf_op jit(solution)/shard_map/ppermute | solution.py:432
  63.7 21.7 %collective-permute-start.18 = (bf16[224,1024]{1,0:T(8,128)(2,1)S(1)}, bf16[224,1024]{1,0:T(8,128)(2,1)S(1)}, u32[]{:S(2)}, u32[]{:S(2)}) collective-permute-start(bf16[224,1024]{1,0:T(8,128)(2,1)S(1)} %get-tuple-element.106), channel_id=1, source_target_pairs={{0,4},{2,6},{4,0},{6,2},{8,12},{10,14},{12,8},{14,10},{16,20},{18,... | collective-permute-start | bytes 1376264 | tf_op jit(solution)/shard_map/ppermute | solution.py:432
  64.7 21.3 %collective-permute-start.17 = (bf16[224,1024]{1,0:T(8,128)(2,1)S(1)}, bf16[224,1024]{1,0:T(8,128)(2,1)S(1)}, u32[]{:S(2)}, u32[]{:S(2)}) collective-permute-start(bf16[224,1024]{1,0:T(8,128)(2,1)S(1)} %get-tuple-element.105), channel_id=1, source_target_pairs={{0,2},{2,0},{4,6},{6,4},{8,10},{10,8},{12,14},{14,12},{16,18},{18,... | collective-permute-start | bytes 1376264 | tf_op jit(solution)/shard_map/ppermute | solution.py:432
  83.7 2.6 %collective-permute-start.15 = (bf16[224,1024]{1,0:T(8,128)(2,1)}, bf16[224,1024]{1,0:T(8,128)(2,1)S(1)}, u32[]{:S(2)}, u32[]{:S(2)}) collective-permute-start(bf16[224,1024]{1,0:T(8,128)(2,1)} %get-tuple-element.120), channel_id=1, source_target_pairs={{0,1},{1,0},{2,3},{3,2},{4,5},{5,4},{6,7},{7,6},{8,9},{9,8},{10,11... | collective-permute-start | bytes 1376264 | tf_op jit(solution)/shard_map/ppermute | solution.py:440
  84.7 3.3 %collective-permute-start.13 = (bf16[224,1024]{1,0:T(8,128)(2,1)}, bf16[224,1024]{1,0:T(8,128)(2,1)S(1)}, u32[]{:S(2)}, u32[]{:S(2)}) collective-permute-start(bf16[224,1024]{1,0:T(8,128)(2,1)} %get-tuple-element.118), channel_id=1, source_target_pairs={{0,1},{1,0},{2,3},{3,2},{4,5},{5,4},{6,7},{7,6},{8,9},{9,8},{10,11... | collective-permute-start | bytes 1376264 | tf_op jit(solution)/shard_map/ppermute | solution.py:440
  84.7 4.4 %collective-permute-start.11 = (bf16[224,1024]{1,0:T(8,128)(2,1)}, bf16[224,1024]{1,0:T(8,128)(2,1)S(1)}, u32[]{:S(2)}, u32[]{:S(2)}) collective-permute-start(bf16[224,1024]{1,0:T(8,128)(2,1)} %get-tuple-element.116), channel_id=1, source_target_pairs={{0,1},{1,0},{2,3},{3,2},{4,5},{5,4},{6,7},{7,6},{8,9},{9,8},{10,11... | collective-permute-start | bytes 1376264 | tf_op jit(solution)/shard_map/ppermute | solution.py:440
  85.5 5.0 %collective-permute-start.10 = (bf16[224,1024]{1,0:T(8,128)(2,1)}, bf16[224,1024]{1,0:T(8,128)(2,1)S(1)}, u32[]{:S(2)}, u32[]{:S(2)}) collective-permute-start(bf16[224,1024]{1,0:T(8,128)(2,1)} %get-tuple-element.114), channel_id=1, source_target_pairs={{0,1},{1,0},{2,3},{3,2},{4,5},{5,4},{6,7},{7,6},{8,9},{9,8},{10,11... | collective-permute-start | bytes 1376264 | tf_op jit(solution)/shard_map/ppermute | solution.py:440
  85.9 6.0 %collective-permute-start.23 = (bf16[224,1024]{1,0:T(8,128)(2,1)S(1)}, bf16[224,1024]{1,0:T(8,128)(2,1)S(1)}, u32[]{:S(2)}, u32[]{:S(2)}) collective-permute-start(bf16[224,1024]{1,0:T(8,128)(2,1)S(1)} %collective-permute-done.19.refs_3_.refs_11_), channel_id=1, source_target_pairs={{0,1},{1,0},{2,3},{3,2},{4,5},{5,4},{6,7},{7,6},{8,9},{9,8},{10,11... | collective-permute-start | bytes 1376264 | tf_op jit(solution)/shard_map/ppermute | solution.py:440
  86.3 6.6 %collective-permute-start.22 = (bf16[224,1024]{1,0:T(8,128)(2,1)S(1)}, bf16[224,1024]{1,0:T(8,128)(2,1)S(1)}, u32[]{:S(2)}, u32[]{:S(2)}) collective-permute-start(bf16[224,1024]{1,0:T(8,128)(2,1)S(1)} %collective-permute-done.18.refs_2_.refs_10_), channel_id=1, source_target_pairs={{0,1},{1,0},{2,3},{3,2},{4,5},{5,4},{6,7},{7,6},{8,9},{9,8},{10,11... | collective-permute-start | bytes 1376264 | tf_op jit(solution)/shard_map/ppermute | solution.py:440
  87.9 5.4 %collective-permute-start.21 = (bf16[224,1024]{1,0:T(8,128)(2,1)S(1)}, bf16[224,1024]{1,0:T(8,128)(2,1)S(1)}, u32[]{:S(2)}, u32[]{:S(2)}) collective-permute-start(bf16[224,1024]{1,0:T(8,128)(2,1)S(1)} %collective-permute-done.17.refs_1_.refs_9_), channel_id=1, source_target_pairs={{0,1},{1,0},{2,3},{3,2},{4,5},{5,4},{6,7},{7,6},{8,9},{9,8},{10,11... | collective-permute-start | bytes 1376264 | tf_op jit(solution)/shard_map/ppermute | solution.py:440
  89.1 4.2 %collective-permute-start.20 = (bf16[224,1024]{1,0:T(8,128)(2,1)S(1)}, bf16[224,1024]{1,0:T(8,128)(2,1)S(1)}, u32[]{:S(2)}, u32[]{:S(2)}) collective-permute-start(bf16[224,1024]{1,0:T(8,128)(2,1)S(1)} %get-tuple-element.122.refs_0_.refs_8_), channel_id=1, source_target_pairs={{0,1},{1,0},{2,3},{3,2},{4,5},{5,4},{6,7},{7,6},{8,9},{9,8},{10,11... | collective-permute-start | bytes 1376264 | tf_op jit(solution)/shard_map/ppermute | solution.py:440
  90.5 23.2 %collective-permute-start.16 = (bf16[224,1024]{1,0:T(8,128)(2,1)S(1)}, bf16[224,1024]{1,0:T(8,128)(2,1)S(1)}, u32[]{:S(2)}, u32[]{:S(2)}) collective-permute-start(bf16[224,1024]{1,0:T(8,128)(2,1)S(1)} %add_convert_fusion), channel_id=1, source_target_pairs={{0,6},{2,4},{4,2},{6,0},{8,14},{10,12},{12,10},{14,8},{16,22},{18,... | collective-permute-start | bytes 1376264 | tf_op jit(solution)/shard_map/ppermute | solution.py:432
  91.9 21.8 %collective-permute-start.14 = (bf16[224,1024]{1,0:T(8,128)(2,1)}, bf16[224,1024]{1,0:T(8,128)(2,1)S(1)}, u32[]{:S(2)}, u32[]{:S(2)}) collective-permute-start(bf16[224,1024]{1,0:T(8,128)(2,1)} %add_convert_fusion.1), channel_id=1, source_target_pairs={{0,4},{2,6},{4,0},{6,2},{8,12},{10,14},{12,8},{14,10},{16,20},{18,... | collective-permute-start | bytes 1376264 | tf_op jit(solution)/shard_map/ppermute | solution.py:432
  92.9 20.8 %collective-permute-start.12 = (bf16[224,1024]{1,0:T(8,128)(2,1)}, bf16[224,1024]{1,0:T(8,128)(2,1)S(1)}, u32[]{:S(2)}, u32[]{:S(2)}) collective-permute-start(bf16[224,1024]{1,0:T(8,128)(2,1)} %add_convert_fusion.2), channel_id=1, source_target_pairs={{0,2},{2,0},{4,6},{6,4},{8,10},{10,8},{12,14},{14,12},{16,18},{18,... | collective-permute-start | bytes 1376264 | tf_op jit(solution)/shard_map/ppermute | solution.py:432
  113.7 11.8 %collective-permute-start.25 = (bf16[128,1024]{1,0:T(8,128)(2,1)}, bf16[128,1024]{1,0:T(8,128)(2,1)}, u32[]{:S(2)}, u32[]{:S(2)}) collective-permute-start(bf16[128,1024]{1,0:T(8,128)(2,1)} %get-tuple-element.139), channel_id=1, source_target_pairs={{0,1},{1,0},{2,3},{3,2},{4,5},{5,4},{6,7},{7,6},{8,9},{9,8},{10,11... | collective-permute-start | bytes 786440 | tf_op jit(solution)/shard_map/ppermute | solution.py:440
  114.8 13.3 %collective-permute-start.33 = (bf16[128,1024]{1,0:T(8,128)(2,1)}, bf16[128,1024]{1,0:T(8,128)(2,1)}, u32[]{:S(2)}, u32[]{:S(2)}) collective-permute-start(bf16[128,1024]{1,0:T(8,128)(2,1)} %get-tuple-element.166), channel_id=1, source_target_pairs={{0,1},{1,0},{2,3},{3,2},{4,5},{5,4},{6,7},{7,6},{8,9},{9,8},{10,11... | collective-permute-start | bytes 786440 | tf_op jit(solution)/shard_map/ppermute | solution.py:440
  119.8 55.6 %all-to-all-start.2 = ((bf16[4,128,1024]{2,1,0:T(8,128)(2,1)}), bf16[4,128,1024]{2,1,0:T(8,128)(2,1)S(1)}, u32[]{:S(2)}, u32[]{:S(2)}) async-start(bf16[4,128,1024]{2,1,0:T(8,128)(2,1)} %combine.1), calls=%async_computation.2 | async-start | bytes 2097152 | tf_op jit(solution)/shard_map/all_to_all | solution.py:454
  124.5 5.7 %collective-permute-start.31 = (bf16[128,1024]{1,0:T(8,128)(2,1)}, bf16[128,1024]{1,0:T(8,128)(2,1)S(1)}, u32[]{:S(2)}, u32[]{:S(2)}) collective-permute-start(bf16[128,1024]{1,0:T(8,128)(2,1)} %get-tuple-element.160), channel_id=1, source_target_pairs={{0,1},{1,0},{2,3},{3,2},{4,5},{5,4},{6,7},{7,6},{8,9},{9,8},{10,11... | collective-permute-start | bytes 786440 | tf_op jit(solution)/shard_map/ppermute | solution.py:440
  125.5 11.8 %collective-permute-start.24 = (bf16[128,1024]{1,0:T(8,128)(2,1)}, bf16[128,1024]{1,0:T(8,128)(2,1)S(1)}, u32[]{:S(2)}, u32[]{:S(2)}) collective-permute-start(bf16[128,1024]{1,0:T(8,128)(2,1)} %get-tuple-element.133), channel_id=1, source_target_pairs={{0,1},{1,0},{2,3},{3,2},{4,5},{5,4},{6,7},{7,6},{8,9},{9,8},{10,11... | collective-permute-start | bytes 786440 | tf_op jit(solution)/shard_map/ppermute | solution.py:440
  126.6 8.5 %collective-permute-start.26 = (bf16[128,1024]{1,0:T(8,128)(2,1)S(1)}, bf16[128,1024]{1,0:T(8,128)(2,1)S(1)}, u32[]{:S(2)}, u32[]{:S(2)}) collective-permute-start(bf16[128,1024]{1,0:T(8,128)(2,1)S(1)} %add_convert_fusion.7), channel_id=1, source_target_pairs={{0,6},{2,4},{4,2},{6,0},{8,14},{10,12},{12,10},{14,8},{16,22},{18,... | collective-permute-start | bytes 786440 | tf_op jit(solution)/shard_map/ppermute | solution.py:432
  129.1 12.8 %collective-permute-start.34 = (bf16[128,1024]{1,0:T(8,128)(2,1)S(1)}, bf16[128,1024]{1,0:T(8,128)(2,1)S(1)}, u32[]{:S(2)}, u32[]{:S(2)}) collective-permute-start(bf16[128,1024]{1,0:T(8,128)(2,1)S(1)} %add_convert_fusion.5), channel_id=1, source_target_pairs={{0,4},{2,6},{4,0},{6,2},{8,12},{10,14},{12,8},{14,10},{16,20},{18,... | collective-permute-start | bytes 786440 | tf_op jit(solution)/shard_map/ppermute | solution.py:432
  130.2 11.6 %collective-permute-start.32 = (bf16[128,1024]{1,0:T(8,128)(2,1)S(1)}, bf16[128,1024]{1,0:T(8,128)(2,1)S(1)}, u32[]{:S(2)}, u32[]{:S(2)}) collective-permute-start(bf16[128,1024]{1,0:T(8,128)(2,1)S(1)} %add_convert_fusion.6), channel_id=1, source_target_pairs={{0,2},{2,0},{4,6},{6,4},{8,10},{10,8},{12,14},{14,12},{16,18},{18,... | collective-permute-start | bytes 786440 | tf_op jit(solution)/shard_map/ppermute | solution.py:432
  135.1 3.3 %collective-permute-start.30 = (bf16[112,1024]{1,0:T(8,128)(2,1)S(1)}, bf16[112,1024]{1,0:T(8,128)(2,1)S(1)}, u32[]{:S(2)}, u32[]{:S(2)}) collective-permute-start(bf16[112,1024]{1,0:T(8,128)(2,1)S(1)} %copy-done.34), channel_id=1, source_target_pairs={{0,1},{1,0},{2,3},{3,2},{4,5},{5,4},{6,7},{7,6},{8,9},{9,8},{10,11... | collective-permute-start | bytes 688136 | tf_op jit(solution)/shard_map/ppermute | solution.py:440
  137.3 1.6 collective-permute-start.29
  137.4 2.9 %collective-permute-start.28 = (bf16[112,1024]{1,0:T(8,128)(2,1)S(1)}, bf16[112,1024]{1,0:T(8,128)(2,1)S(1)}, u32[]{:S(2)}, u32[]{:S(2)}) collective-permute-start(bf16[112,1024]{1,0:T(8,128)(2,1)S(1)} %copy-done.32), channel_id=1, source_target_pairs={{0,1},{1,0},{2,3},{3,2},{4,5},{5,4},{6,7},{7,6},{8,9},{9,8},{10,11... | collective-permute-start | bytes 688136 | tf_op jit(solution)/shard_map/ppermute | solution.py:440
  138.3 3.1 %collective-permute-start.27 = (bf16[112,1024]{1,0:T(8,128)(2,1)S(1)}, bf16[112,1024]{1,0:T(8,128)(2,1)S(1)}, u32[]{:S(2)}, u32[]{:S(2)}) collective-permute-start(bf16[112,1024]{1,0:T(8,128)(2,1)S(1)} %copy-done.31), channel_id=1, source_target_pairs={{0,1},{1,0},{2,3},{3,2},{4,5},{5,4},{6,7},{7,6},{8,9},{9,8},{10,11... | collective-permute-start | bytes 688136 | tf_op jit(solution)/shard_map/ppermute | solution.py:440
  138.9 8.2 %collective-permute-start.37 = (bf16[112,1024]{1,0:T(8,128)(2,1)S(1)}, bf16[112,1024]{1,0:T(8,128)(2,1)S(1)}, u32[]{:S(2)}, u32[]{:S(2)}) collective-permute-start(bf16[112,1024]{1,0:T(8,128)(2,1)S(1)} %add_convert_fusion.9), channel_id=1, source_target_pairs={{0,6},{2,4},{4,2},{6,0},{8,14},{10,12},{12,10},{14,8},{16,22},{18,... | collective-permute-start | bytes 688136 | tf_op jit(solution)/shard_map/ppermute | solution.py:432
  140.3 11.9 %collective-permute-start.36 = (bf16[112,1024]{1,0:T(8,128)(2,1)S(1)}, bf16[112,1024]{1,0:T(8,128)(2,1)S(1)}, u32[]{:S(2)}, u32[]{:S(2)}) collective-permute-start(bf16[112,1024]{1,0:T(8,128)(2,1)S(1)} %add_convert_fusion.10), channel_id=1, source_target_pairs={{0,4},{2,6},{4,0},{6,2},{8,12},{10,14},{12,8},{14,10},{16,20},{18,... | collective-permute-start | bytes 688136 | tf_op jit(solution)/shard_map/ppermute | solution.py:432
  141.5 10.8 %collective-permute-start.35 = (bf16[112,1024]{1,0:T(8,128)(2,1)S(1)}, bf16[112,1024]{1,0:T(8,128)(2,1)S(1)}, u32[]{:S(2)}, u32[]{:S(2)}) collective-permute-start(bf16[112,1024]{1,0:T(8,128)(2,1)S(1)} %add_convert_fusion.11), channel_id=1, source_target_pairs={{0,2},{2,0},{4,6},{6,4},{8,10},{10,8},{12,14},{14,12},{16,18},{18,... | collective-permute-start | bytes 688136 | tf_op jit(solution)/shard_map/ppermute | solution.py:432
  144.9 22.9 %collective-permute-start.39 = (bf16[144,1024]{1,0:T(8,128)(2,1)S(1)}, bf16[144,1024]{1,0:T(8,128)(2,1)S(1)}, u32[]{:S(2)}, u32[]{:S(2)}) collective-permute-start(bf16[144,1024]{1,0:T(8,128)(2,1)S(1)} %get-tuple-element.178), channel_id=1, source_target_pairs={{0,16},{2,18},{4,20},{6,22},{8,24},{10,26},{12,28},{14,30},{16,0},... | collective-permute-start | bytes 884744 | tf_op jit(solution)/shard_map/ppermute | solution.py:425
  147.0 25.8 %collective-permute-start.40 = (bf16[144,1024]{1,0:T(8,128)(2,1)S(1)}, bf16[144,1024]{1,0:T(8,128)(2,1)S(1)}, u32[]{:S(2)}, u32[]{:S(2)}) collective-permute-start(bf16[144,1024]{1,0:T(8,128)(2,1)S(1)} %get-tuple-element.179), channel_id=1, source_target_pairs={{0,8},{2,10},{4,12},{6,14},{8,16},{10,18},{12,20},{14,22},{16,24},... | collective-permute-start | bytes 884744 | tf_op jit(solution)/shard_map/ppermute | solution.py:425
  153.9 20.0 %collective-permute-start.38 = (bf16[144,1024]{1,0:T(8,128)(2,1)S(1)}, bf16[144,1024]{1,0:T(8,128)(2,1)S(1)}, u32[]{:S(2)}, u32[]{:S(2)}) collective-permute-start(bf16[144,1024]{1,0:T(8,128)(2,1)S(1)} %get-tuple-element.177), channel_id=1, source_target_pairs={{0,24},{2,26},{4,28},{6,30},{8,0},{10,2},{12,4},{14,6},{16,8},{18,... | collective-permute-start | bytes 884744 | tf_op jit(solution)/shard_map/ppermute | solution.py:425
  (31 other events, 201.1 us)

commit v3 on v2

--- a/solution.py
+++ b/solution.py
@@ -10,9 +10,9 @@
 PLANE = 4
 CHUNKS = 1
 RETURNS = 2
-BLOCKS = 1
+BLOCKS = 2
 TAIL = 16
-VMEM_LIMIT = 56 * 1024 * 1024
+VMEM_LIMIT = 62 * 1024 * 1024
 SMALL_LIMIT = 16 * 1024 * 1024
 F32 = jnp.float32
 BF16 = jnp.bfloat16
@@ -137,13 +137,15 @@
         outs[q][...] = dot_nn(sel[q * rows : (q + 1) * rows, :], whole[...]).astype(BF16)
 
 
-def pack_gates_kernel(info, meta, *refs, zn, pn, tokens, picks, rows):
+def pack_gates_kernel(info, meta_hbm, *refs, zn, pn, tokens, picks, rows):
     zc = zn // CHUNKS
     sources, outs, refs = refs[:zc], refs[zc : zc + pn], refs[zc + pn :]
-    sels, (whole, sems) = refs[:CHUNKS], refs[CHUNKS:]
+    sels, (meta, whole, sems) = refs[:CHUNKS], refs[CHUNKS:]
     loads = Loads(sems)
+    loads.add("meta", meta_hbm, meta)
     for s in range(zc):
         loads.add(s, sources[s], whole.at[pl.ds(s * tokens, tokens)])
+    loads.need("meta")
     select(info, meta, sels, zn, pn, tokens, picks, rows)
     for q in range(pn):
         expert = (info[0] + (info[1] ^ q)).astype(F32)
@@ -484,8 +486,9 @@
             [shape(part_rows + TAIL, cols)] * pn
             + [shape(pn * part_rows, zc * tokens)] * CHUNKS,
             [info, meta, *parts[:zc]],
-            [SMEM, VMEM] + [HBM] * zc,
-            scratch=[pltpu.VMEM((zc * tokens, cols), BF16), dma((zc,))],
+            [SMEM, HBM] + [HBM] * zc,
+            scratch=[pltpu.VMEM(meta.shape, F32), pltpu.VMEM((zc * tokens, cols), BF16)]
+            + [dma((zc + 1,))],
             name="pack_gates",
         )
 

time: 180 us -> 183 us (1.017)
  other arithmetic: 9.6 us -> 12.3 us
    ppermute x15, waiting for transfers between devices: 13.5 us -> 18.3 us  [inner_send(): return lax.ppermute(value, 'expert', [(e, e ^ q) for e in range(groups)])]
    all_to_all x3, waiting for transfers between devices: 12.8 us -> 10.5 us  [outer_exchange(): lax.all_to_all(value, 'expert', split_axis=0, concat_axis=0, axis_index_g...]
    unnamed x70 -> x72, local copies, waits for them, and re-layouts: 4.28 us -> 5.01 us
  transfers between devices with their start and end apart: 44 -> 44, of which waited for: 12 -> 11; matrix products, arithmetic and copies ran while one was open for 6% -> 7% of each run, Pallas kernels for 38% -> 37%
where the time goes in v3:
time: 183 us; the launch traced here: 180 us
  Pallas kernels  65.8 us (36%)
  waiting for transfers between devices  49.1 us (27%)
  starting transfers between devices  43.9 us (24%)
  other arithmetic  12.3 us (7%)
  local copies, waits for them, and re-layouts  7.67 us (4%)
    pallas_call x9, Pallas kernels, call(): pl.pallas_call(kernel, out_shape=outs, in_specs=specs, out_specs=out_spec...  65.8 us
    ppermute x6, waiting for transfers between devices, outer_send(): lax.ppermute(value, 'expert', [(e, (e // pn + s) % zn * pn + e % pn) for...  19.7 us
    ppermute x15, waiting for transfers between devices, inner_send(): return lax.ppermute(value, 'expert', [(e, e ^ q) for e in range(groups)])  18.3 us
    ppermute x15, starting transfers between devices, inner_send(): return lax.ppermute(value, 'expert', [(e, e ^ q) for e in range(groups)])  13.7 us
    all_to_all x3, starting transfers between devices, outer_exchange(): lax.all_to_all(value, 'expert', split_axis=0, concat_axis=0, axis_index_g...  13 us
    ppermute x20, starting transfers between devices, tensor_send(): return lax.ppermute(value, 'tensor', [(c, (c + j) % nt) for c in range(nt)])  11.2 us
    all_to_all x3, waiting for transfers between devices, outer_exchange(): lax.all_to_all(value, 'expert', split_axis=0, concat_axis=0, axis_index_g...  10.5 us
    ppermute x6, starting transfers between devices, outer_send(): lax.ppermute(value, 'expert', [(e, (e // pn + s) % zn * pn + e % pn) for...  6.04 us
  transfers between devices with their start and end apart: 44, of which 11 were waited for; matrix products, arithmetic and copies ran while one was open for 7% of the time, Pallas kernels for 37%

profile of v3, /device:TPU:9, one launch (start us, length us, event | category | flops | bytes accessed | tf_op | source)
XLA Modules:
  0.0 179.8 jit_solution(3883607137553161119)
XLA Ops:
  0.6 1.3 collective-permute-start
  2.0 1.1 collective-permute-start.1
  3.1 1.4 collective-permute-start.2
  5.9 2.0 %broadcast_in_dim.5 = bf16[4,128,1024]{2,1,0:T(8,128)(2,1)} broadcast(bf16[128,1024]{1,0:T(8,128)(2,1)} %param.11), dimensions={1,2} | broadcast | bytes 1310720 | tf_op jit(solution)/shard_map/broadcast_in_dim | solution.py:466
  8.6 4.3 %all-to-all-start = ((f32[4,16,128]{2,1,0:T(8,128)}), f32[4,16,128]{2,1,0:T(8,128)S(1)}, u32[]{:S(2)}, u32[]{:S(2)}) async-start(f32[4,16,128]{2,1,0:T(8,128)} %broadcast_in_dim.4), calls=%async_computation | async-start | bytes 65536 | tf_op jit(solution)/shard_map/all_to_all | solution.py:456
  12.9 11.6 %collective-permute-done.1.refs_2_ = bf16[128,1024]{1,0:T(8,128)(2,1)S(1)} collective-permute-done((bf16[128,1024]{1,0:T(8,128)(2,1)}, bf16[128,1024]{1,0:T(8,128)(2,1)S(1)}, u32[]{:S(2)}, u32[]{:S(2)}) %collective-permute-start.1) | collective-permute-done | bytes 262176 | tf_op jit(solution)/shard_map/ppermute | solution.py:427
  25.2 2.1 %collective-permute-done.2.refs_3_ = bf16[128,1024]{1,0:T(8,128)(2,1)S(1)} collective-permute-done((bf16[128,1024]{1,0:T(8,128)(2,1)}, bf16[128,1024]{1,0:T(8,128)(2,1)S(1)}, u32[]{:S(2)}, u32[]{:S(2)}) %collective-permute-start.2) | collective-permute-done | bytes 262176 | tf_op jit(solution)/shard_map/ppermute | solution.py:427
  28.0 4.0 %all-to-all-start.1 = ((bf16[4,128,1024]{2,1,0:T(8,128)(2,1)}), bf16[4,128,1024]{2,1,0:T(8,128)(2,1)S(1)}, u32[]{:S(2)}, u32[]{:S(2)}) async-start(bf16[4,128,1024]{2,1,0:T(8,128)(2,1)} %broadcast_in_dim.5), calls=%async_computation.1 | async-start | bytes 2097152 | tf_op jit(solution)/shard_map/all_to_all | solution.py:456
  32.0 0.9 copy-done.8
  32.9 0.9 copy-done.10
  33.9 3.4 %pack_gates.1 = (bf16[240,1024]{1,0:T(8,128)(2,1)S(1)}, bf16[240,1024]{1,0:T(8,128)(2,1)}, bf16[240,1024]{1,0:T(8,128)(2,1)}, bf16[240,1024]{1,0:T(8,128)(2,1)}, bf16[896,512]{1,0:T(8,128)(2,1)S(1)}) custom-call(s32[4]{0:T(128)S(1)} %pad_add_fusion.info, f32[4,16,128]{2,1,0:T(8,128)S(1)} %all-to-all-done.meta_hbm.meta, bf16[128,1024]{1,0:T(8,128)(2,1)S(1)} %copy-done.6, ...), custom_call_target="tpu_custom_call" | custom-call | flops 1024 | bytes 1024 | tf_op jit(solution)/shard_map/pack_gates/pallas_call | solution.py:43
  37.3 2.2 %collective-permute-start.5 = (bf16[240,1024]{1,0:T(8,128)(2,1)}, bf16[240,1024]{1,0:T(8,128)(2,1)}, u32[]{:S(2)}, u32[]{:S(2)}) collective-permute-start(bf16[240,1024]{1,0:T(8,128)(2,1)} %get-tuple-element.97), channel_id=1, source_target_pairs={{0,6},{2,4},{4,2},{6,0},{8,14},{10,12},{12,10},{14,8},{16,22},{18,... | collective-permute-start | bytes 1474568 | tf_op jit(solution)/shard_map/ppermute | solution.py:434
  40.0 2.2 %route.1 = (bf16[256,448]{1,0:T(8,128)(2,1)S(1)}, bf16[256,448]{1,0:T(8,128)(2,1)S(1)}) custom-call(s32[4]{0:T(128)S(1)} %pad_add_fusion.info, f32[4,16,128]{2,1,0:T(8,128)S(1)} %all-to-all-done.meta_hbm.meta), custom_call_target="tpu_custom_call" | custom-call | flops 1024 | bytes 1024 | tf_op jit(solution)/shard_map/route/pallas_call | solution.py:43
  42.9 10.5 %all-to-all-done.1.source = bf16[4,128,1024]{2,1,0:T(8,128)(2,1)S(1)} async-done(((bf16[4,128,1024]{2,1,0:T(8,128)(2,1)}), bf16[4,128,1024]{2,1,0:T(8,128)(2,1)S(1)}, u32[]{:S(2)}, u32[]{:S(2)}) %all-to-all-start.1) | async-done | bytes 1048608 | tf_op jit(solution)/shard_map/all_to_all | solution.py:456
  53.4 2.8 %pack.1 = (bf16[224,1024]{1,0:T(8,128)(2,1)S(1)}, bf16[224,1024]{1,0:T(8,128)(2,1)}, bf16[224,1024]{1,0:T(8,128)(2,1)}, bf16[224,1024]{1,0:T(8,128)(2,1)}) custom-call(s32[4]{0:T(128)S(1)} %pad_add_fusion.info, bf16[896,512]{1,0:T(8,128)(2,1)S(1)} %get-tuple-element.101.sel, bf16[4,128,1024]{2,1,0:T(8,128)(2,1)S(1)} %all-to-all-done.1.source), custom_call_target="tpu_custom_call" | custom-call | flops 1024 | bytes 1024 | tf_op jit(solution)/shard_map/pack/pallas_call | solution.py:43
  56.2 2.4 %collective-permute-start.9 = (bf16[240,1024]{1,0:T(8,128)(2,1)}, bf16[240,1024]{1,0:T(8,128)(2,1)}, u32[]{:S(2)}, u32[]{:S(2)}) collective-permute-start(bf16[240,1024]{1,0:T(8,128)(2,1)} %collective-permute-done.5.refs_3_), channel_id=1, source_target_pairs={{0,1},{1,0},{2,3},{3,2},{4,5},{5,4},{6,7},{7,6},{8,9},{9,8},{10,11... | collective-permute-start | bytes 1474568 | tf_op jit(solution)/shard_map/ppermute | solution.py:442
  58.5 3.7 %collective-permute-done.4.refs_2_ = bf16[240,1024]{1,0:T(8,128)(2,1)} collective-permute-done((bf16[240,1024]{1,0:T(8,128)(2,1)}, bf16[240,1024]{1,0:T(8,128)(2,1)}, u32[]{:S(2)}, u32[]{:S(2)}) %collective-permute-start.4) | collective-permute-done | bytes 491552 | tf_op jit(solution)/shard_map/ppermute | solution.py:434
  63.2 1.5 collective-permute-start.19
  64.7 0.9 collective-permute-start.18
  66.0 16.0 %expert_forward.1 = (bf16[224,1024]{1,0:T(8,128)(2,1)}, bf16[224,1024]{1,0:T(8,128)(2,1)}, bf16[224,1024]{1,0:T(8,128)(2,1)}, bf16[224,1024]{1,0:T(8,128)(2,1)},...) custom-call(s32[4]{0:T(128)} %copy-done.11, ...), custom_call_target="tpu_custom_call" | custom-call | flops 1024 | bytes 1024 | tf_op jit(solution)/shard_map/expert_forward/pallas_call | solution.py:43
  82.0 1.0 collective-permute-start.15
  83.5 3.3 %collective-permute-done.18.refs_2_.refs_10_ = bf16[224,1024]{1,0:T(8,128)(2,1)} collective-permute-done((bf16[224,1024]{1,0:T(8,128)(2,1)}, bf16[224,1024]{1,0:T(8,128)(2,1)}, u32[]{:S(2)}, u32[]{:S(2)}) %collective-permute-start.18) | collective-permute-done | bytes 458784 | tf_op jit(solution)/shard_map/ppermute | solution.py:434
  87.8 2.0 %add_convert_fusion = bf16[224,1024]{1,0:T(8,128)(2,1)} fusion(bf16[224,1024]{1,0:T(8,128)(2,1)S(1)} %collective-permute-done.15, bf16[224,1024]{1,0:T(8,128)(2,1)} %get-tuple-element.119), kind=kLoop, calls=%fused_computation.1 | loop fusion | flops 917504 | bytes 1376256 | tf_op jit(solution)/shard_map/convert_element_type | solution.py:542
  89.9 1.0 add_convert_fusion.1
  91.3 0.9 add_convert_fusion.2
  92.2 1.4 collective-permute-start.16
  93.7 0.9 collective-permute-start.14
  96.0 18.2 %expert_backward.1 = (bf16[112,1024]{1,0:T(8,128)(2,1)}, bf16[112,1024]{1,0:T(8,128)(2,1)}, bf16[112,1024]{1,0:T(8,128)(2,1)}, bf16[112,1024]{1,0:T(8,128)(2,1)}...) custom-call(s32[4]{0:T(128)} %copy-done.11, ...), custom_call_target="tpu_custom_call" | custom-call | flops 1024 | bytes 1024 | tf_op jit(solution)/shard_map/expert_backward/pallas_call | solution.py:43
  114.3 1.5 collective-permute-done.14.refs_4_
  116.3 3.9 %combine.1 = bf16[4,128,1024]{2,1,0:T(8,128)(2,1)} custom-call(s32[4]{0:T(128)S(1)} %copy-done.12, bf16[256,448]{1,0:T(8,128)(2,1)S(1)} %copy-done.5, bf16[256,448]{1,0:T(8,128)(2,1)S(1)} %copy-done.3, bf16[224,1024]{1,0:T(8,128)(2,1)S(1)} %add_convert_fusion.3.refs_2_, bf16[224,1024]{1,0:T(8,128)(2,1)} %collective-permute-done.12.refs_3_, ...), custom_call_target="tpu_custom_call" | custom-call | flops 1024 | bytes 1024 | tf_op jit(solution)/shard_map/combine/pallas_call | solution.py:43
  120.3 4.7 %all-to-all-start.2 = ((bf16[4,128,1024]{2,1,0:T(8,128)(2,1)}), bf16[4,128,1024]{2,1,0:T(8,128)(2,1)}, u32[]{:S(2)}, u32[]{:S(2)}) async-start(bf16[4,128,1024]{2,1,0:T(8,128)(2,1)} %combine.1), calls=%async_computation.2 | async-start | bytes 2097152 | tf_op jit(solution)/shard_map/all_to_all | solution.py:456
  125.0 1.1 collective-permute-start.31
  126.2 1.0 add_convert_fusion.7
  127.2 1.4 collective-permute-start.26
  128.8 1.0 collective-permute-start.34
  130.3 5.4 %collective-permute-done.26.refs_3_ = bf16[128,1024]{1,0:T(8,128)(2,1)S(1)} collective-permute-done((bf16[128,1024]{1,0:T(8,128)(2,1)S(1)}, bf16[128,1024]{1,0:T(8,128)(2,1)S(1)}, u32[]{:S(2)}, u32[]{:S(2)}) %collective-permute-start.26) | collective-permute-done | bytes 262176 | tf_op jit(solution)/shard_map/ppermute | solution.py:434
  135.7 2.1 %collective-permute-start.30 = (bf16[112,1024]{1,0:T(8,128)(2,1)S(1)}, bf16[112,1024]{1,0:T(8,128)(2,1)S(1)}, u32[]{:S(2)}, u32[]{:S(2)}) collective-permute-start(bf16[112,1024]{1,0:T(8,128)(2,1)S(1)} %copy-done.35), channel_id=1, source_target_pairs={{0,1},{1,0},{2,3},{3,2},{4,5},{5,4},{6,7},{7,6},{8,9},{9,8},{10,11... | collective-permute-start | bytes 688136 | tf_op jit(solution)/shard_map/ppermute | solution.py:442
  139.5 1.4 collective-permute-start.37
  141.0 1.0 collective-permute-start.36
  142.5 3.8 %combine_far.1 = (bf16[144,1024]{1,0:T(8,128)(2,1)}, bf16[144,1024]{1,0:T(8,128)(2,1)}, bf16[16,512]{1,0:T(8,128)(2,1)S(1)}) custom-call(s32[4]{0:T(128)S(1)} %copy-done.12, f32[4,16,128]{2,1,0:T(8,128)S(1)} %all-to-all-done.meta_hbm.meta, bf16[896,512]{1,0:T(8,128)(2,1)S(1)} %get-tuple-element.101.sel, bf16[256,448]{1,0:T(8,128)(2,1)S(1)} %copy-done.3, ...), custom_call_target="tpu_custom_call" | custom-call | flops 1024 | bytes 1024 | tf_op jit(solution)/shard_map/combine_far/pallas_call | solution.py:43
  146.3 2.1 %collective-permute-start.39 = (bf16[144,1024]{1,0:T(8,128)(2,1)}, bf16[144,1024]{1,0:T(8,128)(2,1)S(1)}, u32[]{:S(2)}, u32[]{:S(2)}) collective-permute-start(bf16[144,1024]{1,0:T(8,128)(2,1)} %get-tuple-element.178), channel_id=1, source_target_pairs={{0,16},{2,18},{4,20},{6,22},{8,24},{10,26},{12,28},{14,30},{16,0},... | collective-permute-start | bytes 884744 | tf_op jit(solution)/shard_map/ppermute | solution.py:427
  148.5 4.4 %collective-permute-done.36.refs_2_ = bf16[112,1024]{1,0:T(8,128)(2,1)S(1)} collective-permute-done((bf16[112,1024]{1,0:T(8,128)(2,1)S(1)}, bf16[112,1024]{1,0:T(8,128)(2,1)S(1)}, u32[]{:S(2)}, u32[]{:S(2)}) %collective-permute-start.36) | collective-permute-done | bytes 229408 | tf_op jit(solution)/shard_map/ppermute | solution.py:434
  152.9 1.6 combine_near.1
  154.6 13.9 %expert_weights.1 = (bf16[1,2,704,2048]{3,2,1,0:T(8,128)(2,1)}, bf16[1,704,2048]{2,1,0:T(8,128)(2,1)}) custom-call(s32[4]{0:T(128)} %copy-done.11, bf16[240,1024]{1,0:T(8,128)(2,1)} %copy-done, bf16[240,1024]{1,0:T(8,128)(2,1)} %collective-permute-done.3.refs_1_, bf16[240,1024]{1,0:T(8,128)(2,1)} %collective-permute-done.4.refs_2_, ...), custom_call_target="tpu_custom_call" | custom-call | flops 1024 | bytes 1024 | tf_op jit(solution)/shard_map/expert_weights/pallas_call | solution.py:43
  168.5 6.0 %collective-permute-done.40 = bf16[144,1024]{1,0:T(8,128)(2,1)S(1)} collective-permute-done((bf16[144,1024]{1,0:T(8,128)(2,1)}, bf16[144,1024]{1,0:T(8,128)(2,1)S(1)}, u32[]{:S(2)}, u32[]{:S(2)}) %collective-permute-start.40) | collective-permute-done | bytes 294944 | tf_op jit(solution)/shard_map/ppermute | solution.py:427
  174.5 1.2 add_bitcast_fusion
  175.7 1.9 %add_convert_fusion.4 = bf16[128,1024]{1,0:T(8,128)(2,1)} fusion(bf16[128,1024]{1,0:T(8,128)(2,1)S(1)} %copy-done.24, bf16[144,1024]{1,0:T(8,128)(2,1)S(1)} %collective-permute-done.40, bf16[144,1024]{1,0:T(8,128)(2,1)S(1)} %collective-permute-done.39, bf16[144,1024]{1,0:T(8,128)(2,1)} %collective-permute-done.38, bf16[144,1024]{1,0:T(8,128)(2,1)S(1)} %get-tuple-element.170), kind=kLoop, calls=%fused_computation.5 | loop fusion | flops 1310720 | bytes 1572864 | tf_op jit(solution)/shard_map/convert_element_type | solution.py:635
  177.6 1.5 convert_reduce_fusion
  (143 shorter events, 13.6 us)
Async XLA Ops:
  0.6 12.3 %collective-permute-start = (bf16[128,1024]{1,0:T(8,128)(2,1)}, bf16[128,1024]{1,0:T(8,128)(2,1)S(1)}, u32[]{:S(2)}, u32[]{:S(2)}) collective-permute-start(bf16[128,1024]{1,0:T(8,128)(2,1)} %refs_0_.1), channel_id=1, source_target_pairs={{0,8},{2,10},{4,12},{6,14},{8,16},{10,18},{12,20},{14,22},{16,24},... | collective-permute-start | bytes 786440 | tf_op jit(solution)/shard_map/ppermute | solution.py:427
  2.0 22.5 %collective-permute-start.1 = (bf16[128,1024]{1,0:T(8,128)(2,1)}, bf16[128,1024]{1,0:T(8,128)(2,1)S(1)}, u32[]{:S(2)}, u32[]{:S(2)}) collective-permute-start(bf16[128,1024]{1,0:T(8,128)(2,1)} %refs_0_.1), channel_id=1, source_target_pairs={{0,16},{2,18},{4,20},{6,22},{8,24},{10,26},{12,28},{14,30},{16,0},... | collective-permute-start | bytes 786440 | tf_op jit(solution)/shard_map/ppermute | solution.py:427
  3.1 24.2 %collective-permute-start.2 = (bf16[128,1024]{1,0:T(8,128)(2,1)}, bf16[128,1024]{1,0:T(8,128)(2,1)S(1)}, u32[]{:S(2)}, u32[]{:S(2)}) collective-permute-start(bf16[128,1024]{1,0:T(8,128)(2,1)} %refs_0_.1), channel_id=1, source_target_pairs={{0,24},{2,26},{4,28},{6,30},{8,0},{10,2},{12,4},{14,6},{16,8},{18,... | collective-permute-start | bytes 786440 | tf_op jit(solution)/shard_map/ppermute | solution.py:427
  5.9 47.5 %copy-start.11 = (s32[4]{0:T(128)}, s32[4]{0:T(128)S(1)}, u32[]{:S(2)}) copy-start(s32[4]{0:T(128)S(1)} %pad_add_fusion.info) | copy-start | bytes 52
  8.0 24.0 %copy-start.6 = (bf16[128,1024]{1,0:T(8,128)(2,1)S(1)}, bf16[128,1024]{1,0:T(8,128)(2,1)}, u32[]{:S(2)}) copy-start(bf16[128,1024]{1,0:T(8,128)(2,1)} %refs_0_.1) | copy-start | bytes 786436
  8.6 19.4 %all-to-all-start = ((f32[4,16,128]{2,1,0:T(8,128)}), f32[4,16,128]{2,1,0:T(8,128)S(1)}, u32[]{:S(2)}, u32[]{:S(2)}) async-start(f32[4,16,128]{2,1,0:T(8,128)} %broadcast_in_dim.4), calls=%async_computation | async-start | bytes 65536 | tf_op jit(solution)/shard_map/all_to_all | solution.py:456
  28.0 25.4 %all-to-all-start.1 = ((bf16[4,128,1024]{2,1,0:T(8,128)(2,1)}), bf16[4,128,1024]{2,1,0:T(8,128)(2,1)S(1)}, u32[]{:S(2)}, u32[]{:S(2)}) async-start(bf16[4,128,1024]{2,1,0:T(8,128)(2,1)} %broadcast_in_dim.5), calls=%async_computation.1 | async-start | bytes 2097152 | tf_op jit(solution)/shard_map/all_to_all | solution.py:456
  37.3 28.7 %copy-start = (bf16[240,1024]{1,0:T(8,128)(2,1)}, bf16[240,1024]{1,0:T(8,128)(2,1)S(1)}, u32[]{:S(2)}) copy-start(bf16[240,1024]{1,0:T(8,128)(2,1)S(1)} %get-tuple-element.109.refs_0_) | copy-start | bytes 1474564
  37.3 18.9 %collective-permute-start.5 = (bf16[240,1024]{1,0:T(8,128)(2,1)}, bf16[240,1024]{1,0:T(8,128)(2,1)}, u32[]{:S(2)}, u32[]{:S(2)}) collective-permute-start(bf16[240,1024]{1,0:T(8,128)(2,1)} %get-tuple-element.97), channel_id=1, source_target_pairs={{0,6},{2,4},{4,2},{6,0},{8,14},{10,12},{12,10},{14,8},{16,22},{18,... | collective-permute-start | bytes 1474568 | tf_op jit(solution)/shard_map/ppermute | solution.py:434
  39.5 22.7 %collective-permute-start.4 = (bf16[240,1024]{1,0:T(8,128)(2,1)}, bf16[240,1024]{1,0:T(8,128)(2,1)}, u32[]{:S(2)}, u32[]{:S(2)}) collective-permute-start(bf16[240,1024]{1,0:T(8,128)(2,1)} %get-tuple-element.96), channel_id=1, source_target_pairs={{0,4},{2,6},{4,0},{6,2},{8,12},{10,14},{12,8},{14,10},{16,20},{18,... | collective-permute-start | bytes 1474568 | tf_op jit(solution)/shard_map/ppermute | solution.py:434
  39.7 23.0 %collective-permute-start.3 = (bf16[240,1024]{1,0:T(8,128)(2,1)}, bf16[240,1024]{1,0:T(8,128)(2,1)}, u32[]{:S(2)}, u32[]{:S(2)}) collective-permute-start(bf16[240,1024]{1,0:T(8,128)(2,1)} %get-tuple-element.95), channel_id=1, source_target_pairs={{0,2},{2,0},{4,6},{6,4},{8,10},{10,8},{12,14},{14,12},{16,18},{18,... | collective-permute-start | bytes 1474568 | tf_op jit(solution)/shard_map/ppermute | solution.py:434
  56.2 34.7 %copy-start.1 = (bf16[224,1024]{1,0:T(8,128)(2,1)}, bf16[224,1024]{1,0:T(8,128)(2,1)S(1)}, u32[]{:S(2)}) copy-start(bf16[224,1024]{1,0:T(8,128)(2,1)S(1)} %get-tuple-element.122.refs_0_.refs_8_) | copy-start | bytes 1376260
  56.2 8.5 %collective-permute-start.9 = (bf16[240,1024]{1,0:T(8,128)(2,1)}, bf16[240,1024]{1,0:T(8,128)(2,1)}, u32[]{:S(2)}, u32[]{:S(2)}) collective-permute-start(bf16[240,1024]{1,0:T(8,128)(2,1)} %collective-permute-done.5.refs_3_), channel_id=1, source_target_pairs={{0,1},{1,0},{2,3},{3,2},{4,5},{5,4},{6,7},{7,6},{8,9},{9,8},{10,11... | collective-permute-start | bytes 1474568 | tf_op jit(solution)/shard_map/ppermute | solution.py:442
  62.2 3.4 %collective-permute-start.8 = (bf16[240,1024]{1,0:T(8,128)(2,1)}, bf16[240,1024]{1,0:T(8,128)(2,1)}, u32[]{:S(2)}, u32[]{:S(2)}) collective-permute-start(bf16[240,1024]{1,0:T(8,128)(2,1)} %collective-permute-done.4.refs_2_), channel_id=1, source_target_pairs={{0,1},{1,0},{2,3},{3,2},{4,5},{5,4},{6,7},{7,6},{8,9},{9,8},{10,11... | collective-permute-start | bytes 1474568 | tf_op jit(solution)/shard_map/ppermute | solution.py:442
  62.7 3.2 %collective-permute-start.7 = (bf16[240,1024]{1,0:T(8,128)(2,1)}, bf16[240,1024]{1,0:T(8,128)(2,1)}, u32[]{:S(2)}, u32[]{:S(2)}) collective-permute-start(bf16[240,1024]{1,0:T(8,128)(2,1)} %collective-permute-done.3.refs_1_), channel_id=1, source_target_pairs={{0,1},{1,0},{2,3},{3,2},{4,5},{5,4},{6,7},{7,6},{8,9},{9,8},{10,11... | collective-permute-start | bytes 1474568 | tf_op jit(solution)/shard_map/ppermute | solution.py:442
  62.8 3.1 %collective-permute-start.6 = (bf16[240,1024]{1,0:T(8,128)(2,1)S(1)}, bf16[240,1024]{1,0:T(8,128)(2,1)}, u32[]{:S(2)}, u32[]{:S(2)}) collective-permute-start(bf16[240,1024]{1,0:T(8,128)(2,1)S(1)} %get-tuple-element.109.refs_0_), channel_id=1, source_target_pairs={{0,1},{1,0},{2,3},{3,2},{4,5},{5,4},{6,7},{7,6},{8,9},{9,8},{10,11... | collective-permute-start | bytes 1474568 | tf_op jit(solution)/shard_map/ppermute | solution.py:442
  63.2 19.8 %collective-permute-start.19 = (bf16[224,1024]{1,0:T(8,128)(2,1)}, bf16[224,1024]{1,0:T(8,128)(2,1)}, u32[]{:S(2)}, u32[]{:S(2)}) collective-permute-start(bf16[224,1024]{1,0:T(8,128)(2,1)} %get-tuple-element.107), channel_id=1, source_target_pairs={{0,6},{2,4},{4,2},{6,0},{8,14},{10,12},{12,10},{14,8},{16,22},{18,... | collective-permute-start | bytes 1376264 | tf_op jit(solution)/shard_map/ppermute | solution.py:434
  64.7 22.1 %collective-permute-start.18 = (bf16[224,1024]{1,0:T(8,128)(2,1)}, bf16[224,1024]{1,0:T(8,128)(2,1)}, u32[]{:S(2)}, u32[]{:S(2)}) collective-permute-start(bf16[224,1024]{1,0:T(8,128)(2,1)} %get-tuple-element.106), channel_id=1, source_target_pairs={{0,4},{2,6},{4,0},{6,2},{8,12},{10,14},{12,8},{14,10},{16,20},{18,... | collective-permute-start | bytes 1376264 | tf_op jit(solution)/shard_map/ppermute | solution.py:434
  65.6 21.6 %collective-permute-start.17 = (bf16[224,1024]{1,0:T(8,128)(2,1)}, bf16[224,1024]{1,0:T(8,128)(2,1)}, u32[]{:S(2)}, u32[]{:S(2)}) collective-permute-start(bf16[224,1024]{1,0:T(8,128)(2,1)} %get-tuple-element.105), channel_id=1, source_target_pairs={{0,2},{2,0},{4,6},{6,4},{8,10},{10,8},{12,14},{14,12},{16,18},{18,... | collective-permute-start | bytes 1376264 | tf_op jit(solution)/shard_map/ppermute | solution.py:434
  82.0 5.3 %collective-permute-start.15 = (bf16[224,1024]{1,0:T(8,128)(2,1)}, bf16[224,1024]{1,0:T(8,128)(2,1)S(1)}, u32[]{:S(2)}, u32[]{:S(2)}) collective-permute-start(bf16[224,1024]{1,0:T(8,128)(2,1)} %get-tuple-element.120), channel_id=1, source_target_pairs={{0,1},{1,0},{2,3},{3,2},{4,5},{5,4},{6,7},{7,6},{8,9},{9,8},{10,11... | collective-permute-start | bytes 1376264 | tf_op jit(solution)/shard_map/ppermute | solution.py:442
  83.0 6.8 %collective-permute-start.13 = (bf16[224,1024]{1,0:T(8,128)(2,1)}, bf16[224,1024]{1,0:T(8,128)(2,1)S(1)}, u32[]{:S(2)}, u32[]{:S(2)}) collective-permute-start(bf16[224,1024]{1,0:T(8,128)(2,1)} %get-tuple-element.118), channel_id=1, source_target_pairs={{0,1},{1,0},{2,3},{3,2},{4,5},{5,4},{6,7},{7,6},{8,9},{9,8},{10,11... | collective-permute-start | bytes 1376264 | tf_op jit(solution)/shard_map/ppermute | solution.py:442
  83.0 7.8 %collective-permute-start.11 = (bf16[224,1024]{1,0:T(8,128)(2,1)}, bf16[224,1024]{1,0:T(8,128)(2,1)S(1)}, u32[]{:S(2)}, u32[]{:S(2)}) collective-permute-start(bf16[224,1024]{1,0:T(8,128)(2,1)} %get-tuple-element.116), channel_id=1, source_target_pairs={{0,1},{1,0},{2,3},{3,2},{4,5},{5,4},{6,7},{7,6},{8,9},{9,8},{10,11... | collective-permute-start | bytes 1376264 | tf_op jit(solution)/shard_map/ppermute | solution.py:442
  86.8 5.4 %collective-permute-start.10 = (bf16[224,1024]{1,0:T(8,128)(2,1)}, bf16[224,1024]{1,0:T(8,128)(2,1)S(1)}, u32[]{:S(2)}, u32[]{:S(2)}) collective-permute-start(bf16[224,1024]{1,0:T(8,128)(2,1)} %get-tuple-element.114), channel_id=1, source_target_pairs={{0,1},{1,0},{2,3},{3,2},{4,5},{5,4},{6,7},{7,6},{8,9},{9,8},{10,11... | collective-permute-start | bytes 1376264 | tf_op jit(solution)/shard_map/ppermute | solution.py:442
  87.2 6.4 %collective-permute-start.23 = (bf16[224,1024]{1,0:T(8,128)(2,1)}, bf16[224,1024]{1,0:T(8,128)(2,1)S(1)}, u32[]{:S(2)}, u32[]{:S(2)}) collective-permute-start(bf16[224,1024]{1,0:T(8,128)(2,1)} %collective-permute-done.19.refs_3_.refs_11_), channel_id=1, source_target_pairs={{0,1},{1,0},{2,3},{3,2},{4,5},{5,4},{6,7},{7,6},{8,9},{9,8},{10,11... | collective-permute-start | bytes 1376264 | tf_op jit(solution)/shard_map/ppermute | solution.py:442
  87.3 7.3 %collective-permute-start.22 = (bf16[224,1024]{1,0:T(8,128)(2,1)}, bf16[224,1024]{1,0:T(8,128)(2,1)S(1)}, u32[]{:S(2)}, u32[]{:S(2)}) collective-permute-start(bf16[224,1024]{1,0:T(8,128)(2,1)} %collective-permute-done.18.refs_2_.refs_10_), channel_id=1, source_target_pairs={{0,1},{1,0},{2,3},{3,2},{4,5},{5,4},{6,7},{7,6},{8,9},{9,8},{10,11... | collective-permute-start | bytes 1376264 | tf_op jit(solution)/shard_map/ppermute | solution.py:442
  89.8 5.3 %collective-permute-start.21 = (bf16[224,1024]{1,0:T(8,128)(2,1)}, bf16[224,1024]{1,0:T(8,128)(2,1)S(1)}, u32[]{:S(2)}, u32[]{:S(2)}) collective-permute-start(bf16[224,1024]{1,0:T(8,128)(2,1)} %collective-permute-done.17.refs_1_.refs_9_), channel_id=1, source_target_pairs={{0,1},{1,0},{2,3},{3,2},{4,5},{5,4},{6,7},{7,6},{8,9},{9,8},{10,11... | collective-permute-start | bytes 1376264 | tf_op jit(solution)/shard_map/ppermute | solution.py:442
  90.8 4.2 %collective-permute-start.20 = (bf16[224,1024]{1,0:T(8,128)(2,1)S(1)}, bf16[224,1024]{1,0:T(8,128)(2,1)S(1)}, u32[]{:S(2)}, u32[]{:S(2)}) collective-permute-start(bf16[224,1024]{1,0:T(8,128)(2,1)S(1)} %get-tuple-element.122.refs_0_.refs_8_), channel_id=1, source_target_pairs={{0,1},{1,0},{2,3},{3,2},{4,5},{5,4},{6,7},{7,6},{8,9},{9,8},{10,11... | collective-permute-start | bytes 1376264 | tf_op jit(solution)/shard_map/ppermute | solution.py:442
  92.2 22.0 %collective-permute-start.16 = (bf16[224,1024]{1,0:T(8,128)(2,1)}, bf16[224,1024]{1,0:T(8,128)(2,1)}, u32[]{:S(2)}, u32[]{:S(2)}) collective-permute-start(bf16[224,1024]{1,0:T(8,128)(2,1)} %add_convert_fusion), channel_id=1, source_target_pairs={{0,6},{2,4},{4,2},{6,0},{8,14},{10,12},{12,10},{14,8},{16,22},{18,... | collective-permute-start | bytes 1376264 | tf_op jit(solution)/shard_map/ppermute | solution.py:434
  93.7 22.1 %collective-permute-start.14 = (bf16[224,1024]{1,0:T(8,128)(2,1)}, bf16[224,1024]{1,0:T(8,128)(2,1)}, u32[]{:S(2)}, u32[]{:S(2)}) collective-permute-start(bf16[224,1024]{1,0:T(8,128)(2,1)} %add_convert_fusion.1), channel_id=1, source_target_pairs={{0,4},{2,6},{4,0},{6,2},{8,12},{10,14},{12,8},{14,10},{16,20},{18,... | collective-permute-start | bytes 1376264 | tf_op jit(solution)/shard_map/ppermute | solution.py:434
  94.6 21.1 %collective-permute-start.12 = (bf16[224,1024]{1,0:T(8,128)(2,1)}, bf16[224,1024]{1,0:T(8,128)(2,1)}, u32[]{:S(2)}, u32[]{:S(2)}) collective-permute-start(bf16[224,1024]{1,0:T(8,128)(2,1)} %add_convert_fusion.2), channel_id=1, source_target_pairs={{0,2},{2,0},{4,6},{6,4},{8,10},{10,8},{12,14},{14,12},{16,18},{18,... | collective-permute-start | bytes 1376264 | tf_op jit(solution)/shard_map/ppermute | solution.py:434
  115.7 10.4 %collective-permute-start.25 = (bf16[128,1024]{1,0:T(8,128)(2,1)}, bf16[128,1024]{1,0:T(8,128)(2,1)}, u32[]{:S(2)}, u32[]{:S(2)}) collective-permute-start(bf16[128,1024]{1,0:T(8,128)(2,1)} %get-tuple-element.139), channel_id=1, source_target_pairs={{0,1},{1,0},{2,3},{3,2},{4,5},{5,4},{6,7},{7,6},{8,9},{9,8},{10,11... | collective-permute-start | bytes 786440 | tf_op jit(solution)/shard_map/ppermute | solution.py:442
  116.3 12.4 %collective-permute-start.33 = (bf16[128,1024]{1,0:T(8,128)(2,1)}, bf16[128,1024]{1,0:T(8,128)(2,1)S(1)}, u32[]{:S(2)}, u32[]{:S(2)}) collective-permute-start(bf16[128,1024]{1,0:T(8,128)(2,1)} %get-tuple-element.166), channel_id=1, source_target_pairs={{0,1},{1,0},{2,3},{3,2},{4,5},{5,4},{6,7},{7,6},{8,9},{9,8},{10,11... | collective-permute-start | bytes 786440 | tf_op jit(solution)/shard_map/ppermute | solution.py:442
  120.3 57.3 %all-to-all-start.2 = ((bf16[4,128,1024]{2,1,0:T(8,128)(2,1)}), bf16[4,128,1024]{2,1,0:T(8,128)(2,1)}, u32[]{:S(2)}, u32[]{:S(2)}) async-start(bf16[4,128,1024]{2,1,0:T(8,128)(2,1)} %combine.1), calls=%async_computation.2 | async-start | bytes 2097152 | tf_op jit(solution)/shard_map/all_to_all | solution.py:456
  125.0 4.8 %collective-permute-start.31 = (bf16[128,1024]{1,0:T(8,128)(2,1)S(1)}, bf16[128,1024]{1,0:T(8,128)(2,1)S(1)}, u32[]{:S(2)}, u32[]{:S(2)}) collective-permute-start(bf16[128,1024]{1,0:T(8,128)(2,1)S(1)} %copy-done.31), channel_id=1, source_target_pairs={{0,1},{1,0},{2,3},{3,2},{4,5},{5,4},{6,7},{7,6},{8,9},{9,8},{10,11... | collective-permute-start | bytes 786440 | tf_op jit(solution)/shard_map/ppermute | solution.py:442
  126.1 11.8 %collective-permute-start.24 = (bf16[128,1024]{1,0:T(8,128)(2,1)S(1)}, bf16[128,1024]{1,0:T(8,128)(2,1)S(1)}, u32[]{:S(2)}, u32[]{:S(2)}) collective-permute-start(bf16[128,1024]{1,0:T(8,128)(2,1)S(1)} %copy-done.30), channel_id=1, source_target_pairs={{0,1},{1,0},{2,3},{3,2},{4,5},{5,4},{6,7},{7,6},{8,9},{9,8},{10,11... | collective-permute-start | bytes 786440 | tf_op jit(solution)/shard_map/ppermute | solution.py:442
  127.2 8.5 %collective-permute-start.26 = (bf16[128,1024]{1,0:T(8,128)(2,1)S(1)}, bf16[128,1024]{1,0:T(8,128)(2,1)S(1)}, u32[]{:S(2)}, u32[]{:S(2)}) collective-permute-start(bf16[128,1024]{1,0:T(8,128)(2,1)S(1)} %add_convert_fusion.7), channel_id=1, source_target_pairs={{0,6},{2,4},{4,2},{6,0},{8,14},{10,12},{12,10},{14,8},{16,22},{18,... | collective-permute-start | bytes 786440 | tf_op jit(solution)/shard_map/ppermute | solution.py:434
  128.8 13.7 %collective-permute-start.34 = (bf16[128,1024]{1,0:T(8,128)(2,1)S(1)}, bf16[128,1024]{1,0:T(8,128)(2,1)S(1)}, u32[]{:S(2)}, u32[]{:S(2)}) collective-permute-start(bf16[128,1024]{1,0:T(8,128)(2,1)S(1)} %add_convert_fusion.5), channel_id=1, source_target_pairs={{0,4},{2,6},{4,0},{6,2},{8,12},{10,14},{12,8},{14,10},{16,20},{18,... | collective-permute-start | bytes 786440 | tf_op jit(solution)/shard_map/ppermute | solution.py:434
  129.9 12.6 %collective-permute-start.32 = (bf16[128,1024]{1,0:T(8,128)(2,1)S(1)}, bf16[128,1024]{1,0:T(8,128)(2,1)S(1)}, u32[]{:S(2)}, u32[]{:S(2)}) collective-permute-start(bf16[128,1024]{1,0:T(8,128)(2,1)S(1)} %add_convert_fusion.6), channel_id=1, source_target_pairs={{0,2},{2,0},{4,6},{6,4},{8,10},{10,8},{12,14},{14,12},{16,18},{18,... | collective-permute-start | bytes 786440 | tf_op jit(solution)/shard_map/ppermute | solution.py:434
  135.7 3.3 %collective-permute-start.30 = (bf16[112,1024]{1,0:T(8,128)(2,1)S(1)}, bf16[112,1024]{1,0:T(8,128)(2,1)S(1)}, u32[]{:S(2)}, u32[]{:S(2)}) collective-permute-start(bf16[112,1024]{1,0:T(8,128)(2,1)S(1)} %copy-done.35), channel_id=1, source_target_pairs={{0,1},{1,0},{2,3},{3,2},{4,5},{5,4},{6,7},{7,6},{8,9},{9,8},{10,11... | collective-permute-start | bytes 688136 | tf_op jit(solution)/shard_map/ppermute | solution.py:442
  137.9 1.6 collective-permute-start.29
  138.0 2.9 %collective-permute-start.28 = (bf16[112,1024]{1,0:T(8,128)(2,1)S(1)}, bf16[112,1024]{1,0:T(8,128)(2,1)S(1)}, u32[]{:S(2)}, u32[]{:S(2)}) collective-permute-start(bf16[112,1024]{1,0:T(8,128)(2,1)S(1)} %copy-done.33), channel_id=1, source_target_pairs={{0,1},{1,0},{2,3},{3,2},{4,5},{5,4},{6,7},{7,6},{8,9},{9,8},{10,11... | collective-permute-start | bytes 688136 | tf_op jit(solution)/shard_map/ppermute | solution.py:442
  139.0 3.1 %collective-permute-start.27 = (bf16[112,1024]{1,0:T(8,128)(2,1)S(1)}, bf16[112,1024]{1,0:T(8,128)(2,1)S(1)}, u32[]{:S(2)}, u32[]{:S(2)}) collective-permute-start(bf16[112,1024]{1,0:T(8,128)(2,1)S(1)} %copy-done.32), channel_id=1, source_target_pairs={{0,1},{1,0},{2,3},{3,2},{4,5},{5,4},{6,7},{7,6},{8,9},{9,8},{10,11... | collective-permute-start | bytes 688136 | tf_op jit(solution)/shard_map/ppermute | solution.py:442
  139.5 9.0 %collective-permute-start.37 = (bf16[112,1024]{1,0:T(8,128)(2,1)S(1)}, bf16[112,1024]{1,0:T(8,128)(2,1)S(1)}, u32[]{:S(2)}, u32[]{:S(2)}) collective-permute-start(bf16[112,1024]{1,0:T(8,128)(2,1)S(1)} %add_convert_fusion.9), channel_id=1, source_target_pairs={{0,6},{2,4},{4,2},{6,0},{8,14},{10,12},{12,10},{14,8},{16,22},{18,... | collective-permute-start | bytes 688136 | tf_op jit(solution)/shard_map/ppermute | solution.py:434
  141.0 11.9 %collective-permute-start.36 = (bf16[112,1024]{1,0:T(8,128)(2,1)S(1)}, bf16[112,1024]{1,0:T(8,128)(2,1)S(1)}, u32[]{:S(2)}, u32[]{:S(2)}) collective-permute-start(bf16[112,1024]{1,0:T(8,128)(2,1)S(1)} %add_convert_fusion.10), channel_id=1, source_target_pairs={{0,4},{2,6},{4,0},{6,2},{8,12},{10,14},{12,8},{14,10},{16,20},{18,... | collective-permute-start | bytes 688136 | tf_op jit(solution)/shard_map/ppermute | solution.py:434
  142.0 10.8 %collective-permute-start.35 = (bf16[112,1024]{1,0:T(8,128)(2,1)S(1)}, bf16[112,1024]{1,0:T(8,128)(2,1)S(1)}, u32[]{:S(2)}, u32[]{:S(2)}) collective-permute-start(bf16[112,1024]{1,0:T(8,128)(2,1)S(1)} %add_convert_fusion.11), channel_id=1, source_target_pairs={{0,2},{2,0},{4,6},{6,4},{8,10},{10,8},{12,14},{14,12},{16,18},{18,... | collective-permute-start | bytes 688136 | tf_op jit(solution)/shard_map/ppermute | solution.py:434
  146.3 22.1 %collective-permute-start.39 = (bf16[144,1024]{1,0:T(8,128)(2,1)}, bf16[144,1024]{1,0:T(8,128)(2,1)S(1)}, u32[]{:S(2)}, u32[]{:S(2)}) collective-permute-start(bf16[144,1024]{1,0:T(8,128)(2,1)} %get-tuple-element.178), channel_id=1, source_target_pairs={{0,16},{2,18},{4,20},{6,22},{8,24},{10,26},{12,28},{14,30},{16,0},... | collective-permute-start | bytes 884744 | tf_op jit(solution)/shard_map/ppermute | solution.py:427
  148.5 26.0 %collective-permute-start.40 = (bf16[144,1024]{1,0:T(8,128)(2,1)}, bf16[144,1024]{1,0:T(8,128)(2,1)S(1)}, u32[]{:S(2)}, u32[]{:S(2)}) collective-permute-start(bf16[144,1024]{1,0:T(8,128)(2,1)} %get-tuple-element.179), channel_id=1, source_target_pairs={{0,8},{2,10},{4,12},{6,14},{8,16},{10,18},{12,20},{14,22},{16,24},... | collective-permute-start | bytes 884744 | tf_op jit(solution)/shard_map/ppermute | solution.py:427
  154.5 20.0 %collective-permute-start.38 = (bf16[144,1024]{1,0:T(8,128)(2,1)S(1)}, bf16[144,1024]{1,0:T(8,128)(2,1)}, u32[]{:S(2)}, u32[]{:S(2)}) collective-permute-start(bf16[144,1024]{1,0:T(8,128)(2,1)S(1)} %get-tuple-element.177), channel_id=1, source_target_pairs={{0,24},{2,26},{4,28},{6,30},{8,0},{10,2},{12,4},{14,6},{16,8},{18,... | collective-permute-start | bytes 884744 | tf_op jit(solution)/shard_map/ppermute | solution.py:427
  (32 other events, 266.4 us)

commit v4 on v2

--- a/solution.py
+++ b/solution.py
@@ -10,7 +10,7 @@
 PLANE = 4
 CHUNKS = 1
 RETURNS = 2
-BLOCKS = 1
+BLOCKS = 2
 TAIL = 16
 VMEM_LIMIT = 56 * 1024 * 1024
 SMALL_LIMIT = 16 * 1024 * 1024

time: 180 us -> 179 us (level)
  Pallas kernels: 67.4 us -> 65.2 us
  waiting for transfers between devices: 47.5 us -> 49.4 us
    ppermute x15, waiting for transfers between devices: 13.5 us -> 15.7 us  [inner_send(): return lax.ppermute(value, 'expert', [(e, e ^ q) for e in range(groups)])]
    pallas_call x9, Pallas kernels: 67.4 us -> 65.2 us  [call(): pl.pallas_call(kernel, out_shape=outs, in_specs=specs, out_specs=out_spec...]
  transfers between devices with their start and end apart: 44 -> 44, of which waited for: 12 -> 12; matrix products, arithmetic and copies ran while one was open for 6% -> 6% of each run, Pallas kernels for 38% -> 37%
where the time goes in v4:
time: 179 us; the launch traced here: 176 us
  Pallas kernels  65.2 us (36%)
  waiting for transfers between devices  49.4 us (28%)
  starting transfers between devices  43.4 us (24%)
  other arithmetic  9.6 us (5%)
  local copies, waits for them, and re-layouts  6.94 us (4%)
    pallas_call x9, Pallas kernels, call(): pl.pallas_call(kernel, out_shape=outs, in_specs=specs, out_specs=out_spec...  65.2 us
    ppermute x6, waiting for transfers between devices, outer_send(): lax.ppermute(value, 'expert', [(e, (e // pn + s) % zn * pn + e % pn) for...  20.3 us
    ppermute x15, waiting for transfers between devices, inner_send(): return lax.ppermute(value, 'expert', [(e, e ^ q) for e in range(groups)])  15.7 us
    ppermute x15, starting transfers between devices, inner_send(): return lax.ppermute(value, 'expert', [(e, e ^ q) for e in range(groups)])  13.7 us
    all_to_all x3, starting transfers between devices, outer_exchange(): lax.all_to_all(value, 'expert', split_axis=0, concat_axis=0, axis_index_g...  13 us
    all_to_all x3, waiting for transfers between devices, outer_exchange(): lax.all_to_all(value, 'expert', split_axis=0, concat_axis=0, axis_index_g...  12.8 us
    ppermute x20, starting transfers between devices, tensor_send(): return lax.ppermute(value, 'tensor', [(c, (c + j) % nt) for c in range(nt)])  10.7 us
    ppermute x6, starting transfers between devices, outer_send(): lax.ppermute(value, 'expert', [(e, (e // pn + s) % zn * pn + e % pn) for...  6.04 us
  transfers between devices with their start and end apart: 44, of which 12 were waited for; matrix products, arithmetic and copies ran while one was open for 6% of the time, Pallas kernels for 37%

profile of v4, /device:TPU:9, one launch (start us, length us, event | category | flops | bytes accessed | tf_op | source)
XLA Modules:
  0.0 175.5 jit_solution(5337685254500771380)
XLA Ops:
  0.6 1.3 collective-permute-start
  2.0 1.1 collective-permute-start.1
  3.1 1.4 collective-permute-start.2
  5.9 2.0 %broadcast_in_dim.5 = bf16[4,128,1024]{2,1,0:T(8,128)(2,1)} broadcast(bf16[128,1024]{1,0:T(8,128)(2,1)} %param.11), dimensions={1,2} | broadcast | bytes 1310720 | tf_op jit(solution)/shard_map/broadcast_in_dim | solution.py:464
  8.6 4.3 %all-to-all-start = ((f32[4,16,128]{2,1,0:T(8,128)}), f32[4,16,128]{2,1,0:T(8,128)S(1)}, u32[]{:S(2)}, u32[]{:S(2)}) async-start(f32[4,16,128]{2,1,0:T(8,128)} %broadcast_in_dim.4), calls=%async_computation | async-start | bytes 65536 | tf_op jit(solution)/shard_map/all_to_all | solution.py:454
  12.9 11.6 %collective-permute-done.1.refs_2_ = bf16[128,1024]{1,0:T(8,128)(2,1)S(1)} collective-permute-done((bf16[128,1024]{1,0:T(8,128)(2,1)}, bf16[128,1024]{1,0:T(8,128)(2,1)S(1)}, u32[]{:S(2)}, u32[]{:S(2)}) %collective-permute-start.1) | collective-permute-done | bytes 262176 | tf_op jit(solution)/shard_map/ppermute | solution.py:425
  24.5 2.8 %collective-permute-done.2.refs_3_ = bf16[128,1024]{1,0:T(8,128)(2,1)S(1)} collective-permute-done((bf16[128,1024]{1,0:T(8,128)(2,1)}, bf16[128,1024]{1,0:T(8,128)(2,1)S(1)}, u32[]{:S(2)}, u32[]{:S(2)}) %collective-permute-start.2) | collective-permute-done | bytes 262176 | tf_op jit(solution)/shard_map/ppermute | solution.py:425
  28.0 4.0 %all-to-all-start.1 = ((bf16[4,128,1024]{2,1,0:T(8,128)(2,1)}), bf16[4,128,1024]{2,1,0:T(8,128)(2,1)S(1)}, u32[]{:S(2)}, u32[]{:S(2)}) async-start(bf16[4,128,1024]{2,1,0:T(8,128)(2,1)} %broadcast_in_dim.5), calls=%async_computation.1 | async-start | bytes 2097152 | tf_op jit(solution)/shard_map/all_to_all | solution.py:454
  32.0 0.9 copy-done.4
  32.9 3.3 %pack_gates.1 = (bf16[240,1024]{1,0:T(8,128)(2,1)S(1)}, bf16[240,1024]{1,0:T(8,128)(2,1)}, bf16[240,1024]{1,0:T(8,128)(2,1)}, bf16[240,1024]{1,0:T(8,128)(2,1)}, bf16[896,512]{1,0:T(8,128)(2,1)S(1)}) custom-call(s32[4]{0:T(128)S(1)} %pad_add_fusion.info, f32[4,16,128]{2,1,0:T(8,128)S(1)} %all-to-all-done.meta, bf16[128,1024]{1,0:T(8,128)(2,1)S(1)} %copy-done.2, ...), custom_call_target="tpu_custom_call" | custom-call | flops 1024 | bytes 1024 | tf_op jit(solution)/shard_map/pack_gates/pallas_call | solution.py:43
  36.3 2.2 %collective-permute-start.5 = (bf16[240,1024]{1,0:T(8,128)(2,1)}, bf16[240,1024]{1,0:T(8,128)(2,1)}, u32[]{:S(2)}, u32[]{:S(2)}) collective-permute-start(bf16[240,1024]{1,0:T(8,128)(2,1)} %get-tuple-element.97), channel_id=1, source_target_pairs={{0,6},{2,4},{4,2},{6,0},{8,14},{10,12},{12,10},{14,8},{16,22},{18,... | collective-permute-start | bytes 1474568 | tf_op jit(solution)/shard_map/ppermute | solution.py:432
  39.0 2.2 %route.1 = (bf16[256,448]{1,0:T(8,128)(2,1)S(1)}, bf16[256,448]{1,0:T(8,128)(2,1)S(1)}) custom-call(s32[4]{0:T(128)S(1)} %pad_add_fusion.info, f32[4,16,128]{2,1,0:T(8,128)S(1)} %all-to-all-done.meta), custom_call_target="tpu_custom_call" | custom-call | flops 1024 | bytes 1024 | tf_op jit(solution)/shard_map/route/pallas_call | solution.py:43
  41.2 12.8 %all-to-all-done.1.source = bf16[4,128,1024]{2,1,0:T(8,128)(2,1)S(1)} async-done(((bf16[4,128,1024]{2,1,0:T(8,128)(2,1)}), bf16[4,128,1024]{2,1,0:T(8,128)(2,1)S(1)}, u32[]{:S(2)}, u32[]{:S(2)}) %all-to-all-start.1) | async-done | bytes 1048608 | tf_op jit(solution)/shard_map/all_to_all | solution.py:454
  54.0 2.0 %pack.1 = (bf16[224,1024]{1,0:T(8,128)(2,1)S(1)}, bf16[224,1024]{1,0:T(8,128)(2,1)S(1)}, bf16[224,1024]{1,0:T(8,128)(2,1)S(1)}, bf16[224,1024]{1,0:T(8,128)(2,1)S(1)}) custom-call(s32[4]{0:T(128)S(1)} %pad_add_fusion.info, bf16[896,512]{1,0:T(8,128)(2,1)S(1)} %get-tuple-element.101.sel, bf16[4,128,1024]{2,1,0:T(8,128)(2,1)S(1)} %all-to-all-done.1.source), custom_call_target="tpu_custom_call" | custom-call | flops 1024 | bytes 1024 | tf_op jit(solution)/shard_map/pack/pallas_call | solution.py:43
  56.0 1.7 collective-permute-start.9
  57.8 3.5 %collective-permute-done.4.refs_2_ = bf16[240,1024]{1,0:T(8,128)(2,1)} collective-permute-done((bf16[240,1024]{1,0:T(8,128)(2,1)}, bf16[240,1024]{1,0:T(8,128)(2,1)}, u32[]{:S(2)}, u32[]{:S(2)}) %collective-permute-start.4) | collective-permute-done | bytes 491552 | tf_op jit(solution)/shard_map/ppermute | solution.py:432
  62.3 1.5 collective-permute-start.19
  63.7 0.9 collective-permute-start.18
  65.7 0.8 copy-done.10
  66.6 16.0 %expert_forward.1 = (bf16[224,1024]{1,0:T(8,128)(2,1)}, bf16[224,1024]{1,0:T(8,128)(2,1)}, bf16[224,1024]{1,0:T(8,128)(2,1)}, bf16[224,1024]{1,0:T(8,128)(2,1)},...) custom-call(s32[4]{0:T(128)} %copy-done.5, ...), custom_call_target="tpu_custom_call" | custom-call | flops 1024 | bytes 1024 | tf_op jit(solution)/shard_map/expert_forward/pallas_call | solution.py:43
  82.6 1.0 collective-permute-start.15
  84.1 1.4 collective-permute-done.18.refs_2_.refs_10_
  86.5 1.2 add_convert_fusion
  87.9 1.0 add_convert_fusion.1
  89.3 0.9 add_convert_fusion.2
  90.3 1.5 collective-permute-start.16
  91.8 0.9 collective-permute-start.14
  94.1 18.2 %expert_backward.1 = (bf16[112,1024]{1,0:T(8,128)(2,1)}, bf16[112,1024]{1,0:T(8,128)(2,1)}, bf16[112,1024]{1,0:T(8,128)(2,1)}, bf16[112,1024]{1,0:T(8,128)(2,1)}...) custom-call(s32[4]{0:T(128)} %copy-done.5, ...), custom_call_target="tpu_custom_call" | custom-call | flops 1024 | bytes 1024 | tf_op jit(solution)/shard_map/expert_backward/pallas_call | solution.py:43
  112.3 1.2 collective-permute-done.14.refs_4_
  114.1 4.9 %combine.1 = bf16[4,128,1024]{2,1,0:T(8,128)(2,1)} custom-call(s32[4]{0:T(128)S(1)} %copy-done.6, bf16[256,448]{1,0:T(8,128)(2,1)S(1)} %get-tuple-element.99.refs_0_.chosen, bf16[256,448]{1,0:T(8,128)(2,1)S(1)} %get-tuple-element.100.refs_1_.chosen, bf16[224,1024]{1,0:T(8,128)(2,1)S(1)} %add_convert_fusion.3.refs_2_, ...), custom_call_target="tpu_custom_call" | custom-call | flops 1024 | bytes 1024 | tf_op jit(solution)/shard_map/combine/pallas_call | solution.py:43
  119.0 4.7 %all-to-all-start.2 = ((bf16[4,128,1024]{2,1,0:T(8,128)(2,1)}), bf16[4,128,1024]{2,1,0:T(8,128)(2,1)S(1)}, u32[]{:S(2)}, u32[]{:S(2)}) async-start(bf16[4,128,1024]{2,1,0:T(8,128)(2,1)} %combine.1), calls=%async_computation.2 | async-start | bytes 2097152 | tf_op jit(solution)/shard_map/all_to_all | solution.py:454
  123.6 1.1 collective-permute-start.31
  124.8 1.0 add_convert_fusion.7
  125.9 1.4 collective-permute-start.26
  127.3 1.0 add_convert_fusion.5
  128.3 1.0 collective-permute-start.34
  129.8 4.5 %collective-permute-done.26.refs_3_ = bf16[128,1024]{1,0:T(8,128)(2,1)S(1)} collective-permute-done((bf16[128,1024]{1,0:T(8,128)(2,1)S(1)}, bf16[128,1024]{1,0:T(8,128)(2,1)S(1)}, u32[]{:S(2)}, u32[]{:S(2)}) %collective-permute-start.26) | collective-permute-done | bytes 262176 | tf_op jit(solution)/shard_map/ppermute | solution.py:432
  134.3 2.2 %collective-permute-start.30 = (bf16[112,1024]{1,0:T(8,128)(2,1)S(1)}, bf16[112,1024]{1,0:T(8,128)(2,1)S(1)}, u32[]{:S(2)}, u32[]{:S(2)}) collective-permute-start(bf16[112,1024]{1,0:T(8,128)(2,1)S(1)} %copy-done.34), channel_id=1, source_target_pairs={{0,1},{1,0},{2,3},{3,2},{4,5},{5,4},{6,7},{7,6},{8,9},{9,8},{10,11... | collective-permute-start | bytes 688136 | tf_op jit(solution)/shard_map/ppermute | solution.py:440
  138.1 1.4 collective-permute-start.37
  139.6 1.0 collective-permute-start.36
  141.1 3.0 %combine_far.1 = (bf16[144,1024]{1,0:T(8,128)(2,1)S(1)}, bf16[144,1024]{1,0:T(8,128)(2,1)S(1)}, bf16[16,512]{1,0:T(8,128)(2,1)S(1)}) custom-call(s32[4]{0:T(128)S(1)} %copy-done.6, f32[4,16,128]{2,1,0:T(8,128)S(1)} %all-to-all-done.meta, bf16[896,512]{1,0:T(8,128)(2,1)S(1)} %get-tuple-element.101.sel, ...), custom_call_target="tpu_custom_call" | custom-call | flops 1024 | bytes 1024 | tf_op jit(solution)/shard_map/combine_far/pallas_call | solution.py:43
  144.1 2.1 %collective-permute-start.39 = (bf16[144,1024]{1,0:T(8,128)(2,1)S(1)}, bf16[144,1024]{1,0:T(8,128)(2,1)S(1)}, u32[]{:S(2)}, u32[]{:S(2)}) collective-permute-start(bf16[144,1024]{1,0:T(8,128)(2,1)S(1)} %get-tuple-element.178), channel_id=1, source_target_pairs={{0,16},{2,18},{4,20},{6,22},{8,24},{10,26},{12,28},{14,30},{16,0},... | collective-permute-start | bytes 884744 | tf_op jit(solution)/shard_map/ppermute | solution.py:425
  146.3 5.2 %collective-permute-done.36.refs_2_ = bf16[112,1024]{1,0:T(8,128)(2,1)S(1)} collective-permute-done((bf16[112,1024]{1,0:T(8,128)(2,1)S(1)}, bf16[112,1024]{1,0:T(8,128)(2,1)S(1)}, u32[]{:S(2)}, u32[]{:S(2)}) %collective-permute-start.36) | collective-permute-done | bytes 229408 | tf_op jit(solution)/shard_map/ppermute | solution.py:432
  151.5 1.6 combine_near.1
  153.2 13.9 %expert_weights.1 = (bf16[1,2,704,2048]{3,2,1,0:T(8,128)(2,1)}, bf16[1,704,2048]{2,1,0:T(8,128)(2,1)}) custom-call(s32[4]{0:T(128)} %copy-done.5, bf16[240,1024]{1,0:T(8,128)(2,1)} %copy-done, bf16[240,1024]{1,0:T(8,128)(2,1)} %collective-permute-done.3.refs_1_, bf16[240,1024]{1,0:T(8,128)(2,1)} %collective-permute-done.4.refs_2_, ...), custom_call_target="tpu_custom_call" | custom-call | flops 1024 | bytes 1024 | tf_op jit(solution)/shard_map/expert_weights/pallas_call | solution.py:43
  167.1 4.9 %collective-permute-done.40 = bf16[144,1024]{1,0:T(8,128)(2,1)S(1)} collective-permute-done((bf16[144,1024]{1,0:T(8,128)(2,1)S(1)}, bf16[144,1024]{1,0:T(8,128)(2,1)S(1)}, u32[]{:S(2)}, u32[]{:S(2)}) %collective-permute-start.40) | collective-permute-done | bytes 294944 | tf_op jit(solution)/shard_map/ppermute | solution.py:425
  172.0 1.0 collective-permute-done.38
  173.6 0.9 add_convert_fusion.4
  (141 shorter events, 13.8 us)
Async XLA Ops:
  0.6 12.3 %collective-permute-start = (bf16[128,1024]{1,0:T(8,128)(2,1)}, bf16[128,1024]{1,0:T(8,128)(2,1)S(1)}, u32[]{:S(2)}, u32[]{:S(2)}) collective-permute-start(bf16[128,1024]{1,0:T(8,128)(2,1)} %refs_0_.1), channel_id=1, source_target_pairs={{0,8},{2,10},{4,12},{6,14},{8,16},{10,18},{12,20},{14,22},{16,24},... | collective-permute-start | bytes 786440 | tf_op jit(solution)/shard_map/ppermute | solution.py:425
  2.0 22.5 %collective-permute-start.1 = (bf16[128,1024]{1,0:T(8,128)(2,1)}, bf16[128,1024]{1,0:T(8,128)(2,1)S(1)}, u32[]{:S(2)}, u32[]{:S(2)}) collective-permute-start(bf16[128,1024]{1,0:T(8,128)(2,1)} %refs_0_.1), channel_id=1, source_target_pairs={{0,16},{2,18},{4,20},{6,22},{8,24},{10,26},{12,28},{14,30},{16,0},... | collective-permute-start | bytes 786440 | tf_op jit(solution)/shard_map/ppermute | solution.py:425
  3.1 24.2 %collective-permute-start.2 = (bf16[128,1024]{1,0:T(8,128)(2,1)}, bf16[128,1024]{1,0:T(8,128)(2,1)S(1)}, u32[]{:S(2)}, u32[]{:S(2)}) collective-permute-start(bf16[128,1024]{1,0:T(8,128)(2,1)} %refs_0_.1), channel_id=1, source_target_pairs={{0,24},{2,26},{4,28},{6,30},{8,0},{10,2},{12,4},{14,6},{16,8},{18,... | collective-permute-start | bytes 786440 | tf_op jit(solution)/shard_map/ppermute | solution.py:425
  5.9 48.1 %copy-start.5 = (s32[4]{0:T(128)}, s32[4]{0:T(128)S(1)}, u32[]{:S(2)}) copy-start(s32[4]{0:T(128)S(1)} %pad_add_fusion.info) | copy-start | bytes 52
  8.0 24.0 %copy-start.2 = (bf16[128,1024]{1,0:T(8,128)(2,1)S(1)}, bf16[128,1024]{1,0:T(8,128)(2,1)}, u32[]{:S(2)}) copy-start(bf16[128,1024]{1,0:T(8,128)(2,1)} %refs_0_.1) | copy-start | bytes 786436
  8.6 19.4 %all-to-all-start = ((f32[4,16,128]{2,1,0:T(8,128)}), f32[4,16,128]{2,1,0:T(8,128)S(1)}, u32[]{:S(2)}, u32[]{:S(2)}) async-start(f32[4,16,128]{2,1,0:T(8,128)} %broadcast_in_dim.4), calls=%async_computation | async-start | bytes 65536 | tf_op jit(solution)/shard_map/all_to_all | solution.py:454
  28.0 26.0 %all-to-all-start.1 = ((bf16[4,128,1024]{2,1,0:T(8,128)(2,1)}), bf16[4,128,1024]{2,1,0:T(8,128)(2,1)S(1)}, u32[]{:S(2)}, u32[]{:S(2)}) async-start(bf16[4,128,1024]{2,1,0:T(8,128)(2,1)} %broadcast_in_dim.5), calls=%async_computation.1 | async-start | bytes 2097152 | tf_op jit(solution)/shard_map/all_to_all | solution.py:454
  36.3 28.7 %copy-start = (bf16[240,1024]{1,0:T(8,128)(2,1)}, bf16[240,1024]{1,0:T(8,128)(2,1)S(1)}, u32[]{:S(2)}) copy-start(bf16[240,1024]{1,0:T(8,128)(2,1)S(1)} %get-tuple-element.109.refs_0_) | copy-start | bytes 1474564
  36.3 19.7 %collective-permute-start.5 = (bf16[240,1024]{1,0:T(8,128)(2,1)}, bf16[240,1024]{1,0:T(8,128)(2,1)}, u32[]{:S(2)}, u32[]{:S(2)}) collective-permute-start(bf16[240,1024]{1,0:T(8,128)(2,1)} %get-tuple-element.97), channel_id=1, source_target_pairs={{0,6},{2,4},{4,2},{6,0},{8,14},{10,12},{12,10},{14,8},{16,22},{18,... | collective-permute-start | bytes 1474568 | tf_op jit(solution)/shard_map/ppermute | solution.py:432
  38.5 22.7 %collective-permute-start.4 = (bf16[240,1024]{1,0:T(8,128)(2,1)}, bf16[240,1024]{1,0:T(8,128)(2,1)}, u32[]{:S(2)}, u32[]{:S(2)}) collective-permute-start(bf16[240,1024]{1,0:T(8,128)(2,1)} %get-tuple-element.96), channel_id=1, source_target_pairs={{0,4},{2,6},{4,0},{6,2},{8,12},{10,14},{12,8},{14,10},{16,20},{18,... | collective-permute-start | bytes 1474568 | tf_op jit(solution)/shard_map/ppermute | solution.py:432
  38.8 23.0 %collective-permute-start.3 = (bf16[240,1024]{1,0:T(8,128)(2,1)}, bf16[240,1024]{1,0:T(8,128)(2,1)}, u32[]{:S(2)}, u32[]{:S(2)}) collective-permute-start(bf16[240,1024]{1,0:T(8,128)(2,1)} %get-tuple-element.95), channel_id=1, source_target_pairs={{0,2},{2,0},{4,6},{6,4},{8,10},{10,8},{12,14},{14,12},{16,18},{18,... | collective-permute-start | bytes 1474568 | tf_op jit(solution)/shard_map/ppermute | solution.py:432
  56.0 32.8 %copy-start.1 = (bf16[224,1024]{1,0:T(8,128)(2,1)}, bf16[224,1024]{1,0:T(8,128)(2,1)S(1)}, u32[]{:S(2)}) copy-start(bf16[224,1024]{1,0:T(8,128)(2,1)S(1)} %get-tuple-element.122.refs_0_.refs_8_) | copy-start | bytes 1376260
  56.0 7.7 %collective-permute-start.9 = (bf16[240,1024]{1,0:T(8,128)(2,1)}, bf16[240,1024]{1,0:T(8,128)(2,1)S(1)}, u32[]{:S(2)}, u32[]{:S(2)}) collective-permute-start(bf16[240,1024]{1,0:T(8,128)(2,1)} %collective-permute-done.5.refs_3_), channel_id=1, source_target_pairs={{0,1},{1,0},{2,3},{3,2},{4,5},{5,4},{6,7},{7,6},{8,9},{9,8},{10,11... | collective-permute-start | bytes 1474568 | tf_op jit(solution)/shard_map/ppermute | solution.py:440
  61.3 3.4 %collective-permute-start.8 = (bf16[240,1024]{1,0:T(8,128)(2,1)}, bf16[240,1024]{1,0:T(8,128)(2,1)S(1)}, u32[]{:S(2)}, u32[]{:S(2)}) collective-permute-start(bf16[240,1024]{1,0:T(8,128)(2,1)} %collective-permute-done.4.refs_2_), channel_id=1, source_target_pairs={{0,1},{1,0},{2,3},{3,2},{4,5},{5,4},{6,7},{7,6},{8,9},{9,8},{10,11... | collective-permute-start | bytes 1474568 | tf_op jit(solution)/shard_map/ppermute | solution.py:440
  61.7 3.2 %collective-permute-start.7 = (bf16[240,1024]{1,0:T(8,128)(2,1)}, bf16[240,1024]{1,0:T(8,128)(2,1)S(1)}, u32[]{:S(2)}, u32[]{:S(2)}) collective-permute-start(bf16[240,1024]{1,0:T(8,128)(2,1)} %collective-permute-done.3.refs_1_), channel_id=1, source_target_pairs={{0,1},{1,0},{2,3},{3,2},{4,5},{5,4},{6,7},{7,6},{8,9},{9,8},{10,11... | collective-permute-start | bytes 1474568 | tf_op jit(solution)/shard_map/ppermute | solution.py:440
  61.8 3.1 %collective-permute-start.6 = (bf16[240,1024]{1,0:T(8,128)(2,1)S(1)}, bf16[240,1024]{1,0:T(8,128)(2,1)S(1)}, u32[]{:S(2)}, u32[]{:S(2)}) collective-permute-start(bf16[240,1024]{1,0:T(8,128)(2,1)S(1)} %get-tuple-element.109.refs_0_), channel_id=1, source_target_pairs={{0,1},{1,0},{2,3},{3,2},{4,5},{5,4},{6,7},{7,6},{8,9},{9,8},{10,11... | collective-permute-start | bytes 1474568 | tf_op jit(solution)/shard_map/ppermute | solution.py:440
  62.3 21.4 %collective-permute-start.19 = (bf16[224,1024]{1,0:T(8,128)(2,1)S(1)}, bf16[224,1024]{1,0:T(8,128)(2,1)S(1)}, u32[]{:S(2)}, u32[]{:S(2)}) collective-permute-start(bf16[224,1024]{1,0:T(8,128)(2,1)S(1)} %get-tuple-element.107), channel_id=1, source_target_pairs={{0,6},{2,4},{4,2},{6,0},{8,14},{10,12},{12,10},{14,8},{16,22},{18,... | collective-permute-start | bytes 1376264 | tf_op jit(solution)/shard_map/ppermute | solution.py:432
  63.7 21.7 %collective-permute-start.18 = (bf16[224,1024]{1,0:T(8,128)(2,1)S(1)}, bf16[224,1024]{1,0:T(8,128)(2,1)S(1)}, u32[]{:S(2)}, u32[]{:S(2)}) collective-permute-start(bf16[224,1024]{1,0:T(8,128)(2,1)S(1)} %get-tuple-element.106), channel_id=1, source_target_pairs={{0,4},{2,6},{4,0},{6,2},{8,12},{10,14},{12,8},{14,10},{16,20},{18,... | collective-permute-start | bytes 1376264 | tf_op jit(solution)/shard_map/ppermute | solution.py:432
  64.7 21.3 %collective-permute-start.17 = (bf16[224,1024]{1,0:T(8,128)(2,1)S(1)}, bf16[224,1024]{1,0:T(8,128)(2,1)S(1)}, u32[]{:S(2)}, u32[]{:S(2)}) collective-permute-start(bf16[224,1024]{1,0:T(8,128)(2,1)S(1)} %get-tuple-element.105), channel_id=1, source_target_pairs={{0,2},{2,0},{4,6},{6,4},{8,10},{10,8},{12,14},{14,12},{16,18},{18,... | collective-permute-start | bytes 1376264 | tf_op jit(solution)/shard_map/ppermute | solution.py:432
  82.6 3.4 %collective-permute-start.15 = (bf16[224,1024]{1,0:T(8,128)(2,1)}, bf16[224,1024]{1,0:T(8,128)(2,1)S(1)}, u32[]{:S(2)}, u32[]{:S(2)}) collective-permute-start(bf16[224,1024]{1,0:T(8,128)(2,1)} %get-tuple-element.120), channel_id=1, source_target_pairs={{0,1},{1,0},{2,3},{3,2},{4,5},{5,4},{6,7},{7,6},{8,9},{9,8},{10,11... | collective-permute-start | bytes 1376264 | tf_op jit(solution)/shard_map/ppermute | solution.py:440
  83.6 4.1 %collective-permute-start.13 = (bf16[224,1024]{1,0:T(8,128)(2,1)}, bf16[224,1024]{1,0:T(8,128)(2,1)S(1)}, u32[]{:S(2)}, u32[]{:S(2)}) collective-permute-start(bf16[224,1024]{1,0:T(8,128)(2,1)} %get-tuple-element.118), channel_id=1, source_target_pairs={{0,1},{1,0},{2,3},{3,2},{4,5},{5,4},{6,7},{7,6},{8,9},{9,8},{10,11... | collective-permute-start | bytes 1376264 | tf_op jit(solution)/shard_map/ppermute | solution.py:440
  83.7 5.1 %collective-permute-start.11 = (bf16[224,1024]{1,0:T(8,128)(2,1)}, bf16[224,1024]{1,0:T(8,128)(2,1)S(1)}, u32[]{:S(2)}, u32[]{:S(2)}) collective-permute-start(bf16[224,1024]{1,0:T(8,128)(2,1)} %get-tuple-element.116), channel_id=1, source_target_pairs={{0,1},{1,0},{2,3},{3,2},{4,5},{5,4},{6,7},{7,6},{8,9},{9,8},{10,11... | collective-permute-start | bytes 1376264 | tf_op jit(solution)/shard_map/ppermute | solution.py:440
  85.5 4.8 %collective-permute-start.10 = (bf16[224,1024]{1,0:T(8,128)(2,1)}, bf16[224,1024]{1,0:T(8,128)(2,1)S(1)}, u32[]{:S(2)}, u32[]{:S(2)}) collective-permute-start(bf16[224,1024]{1,0:T(8,128)(2,1)} %get-tuple-element.114), channel_id=1, source_target_pairs={{0,1},{1,0},{2,3},{3,2},{4,5},{5,4},{6,7},{7,6},{8,9},{9,8},{10,11... | collective-permute-start | bytes 1376264 | tf_op jit(solution)/shard_map/ppermute | solution.py:440
  85.9 5.8 %collective-permute-start.23 = (bf16[224,1024]{1,0:T(8,128)(2,1)S(1)}, bf16[224,1024]{1,0:T(8,128)(2,1)S(1)}, u32[]{:S(2)}, u32[]{:S(2)}) collective-permute-start(bf16[224,1024]{1,0:T(8,128)(2,1)S(1)} %collective-permute-done.19.refs_3_.refs_11_), channel_id=1, source_target_pairs={{0,1},{1,0},{2,3},{3,2},{4,5},{5,4},{6,7},{7,6},{8,9},{9,8},{10,11... | collective-permute-start | bytes 1376264 | tf_op jit(solution)/shard_map/ppermute | solution.py:440
  86.0 6.7 %collective-permute-start.22 = (bf16[224,1024]{1,0:T(8,128)(2,1)S(1)}, bf16[224,1024]{1,0:T(8,128)(2,1)S(1)}, u32[]{:S(2)}, u32[]{:S(2)}) collective-permute-start(bf16[224,1024]{1,0:T(8,128)(2,1)S(1)} %collective-permute-done.18.refs_2_.refs_10_), channel_id=1, source_target_pairs={{0,1},{1,0},{2,3},{3,2},{4,5},{5,4},{6,7},{7,6},{8,9},{9,8},{10,11... | collective-permute-start | bytes 1376264 | tf_op jit(solution)/shard_map/ppermute | solution.py:440
  87.7 5.4 %collective-permute-start.21 = (bf16[224,1024]{1,0:T(8,128)(2,1)S(1)}, bf16[224,1024]{1,0:T(8,128)(2,1)S(1)}, u32[]{:S(2)}, u32[]{:S(2)}) collective-permute-start(bf16[224,1024]{1,0:T(8,128)(2,1)S(1)} %collective-permute-done.17.refs_1_.refs_9_), channel_id=1, source_target_pairs={{0,1},{1,0},{2,3},{3,2},{4,5},{5,4},{6,7},{7,6},{8,9},{9,8},{10,11... | collective-permute-start | bytes 1376264 | tf_op jit(solution)/shard_map/ppermute | solution.py:440
  88.8 4.3 %collective-permute-start.20 = (bf16[224,1024]{1,0:T(8,128)(2,1)S(1)}, bf16[224,1024]{1,0:T(8,128)(2,1)S(1)}, u32[]{:S(2)}, u32[]{:S(2)}) collective-permute-start(bf16[224,1024]{1,0:T(8,128)(2,1)S(1)} %get-tuple-element.122.refs_0_.refs_8_), channel_id=1, source_target_pairs={{0,1},{1,0},{2,3},{3,2},{4,5},{5,4},{6,7},{7,6},{8,9},{9,8},{10,11... | collective-permute-start | bytes 1376264 | tf_op jit(solution)/shard_map/ppermute | solution.py:440
  90.3 22.0 %collective-permute-start.16 = (bf16[224,1024]{1,0:T(8,128)(2,1)S(1)}, bf16[224,1024]{1,0:T(8,128)(2,1)S(1)}, u32[]{:S(2)}, u32[]{:S(2)}) collective-permute-start(bf16[224,1024]{1,0:T(8,128)(2,1)S(1)} %add_convert_fusion), channel_id=1, source_target_pairs={{0,6},{2,4},{4,2},{6,0},{8,14},{10,12},{12,10},{14,8},{16,22},{18,... | collective-permute-start | bytes 1376264 | tf_op jit(solution)/shard_map/ppermute | solution.py:432
  91.8 21.7 %collective-permute-start.14 = (bf16[224,1024]{1,0:T(8,128)(2,1)}, bf16[224,1024]{1,0:T(8,128)(2,1)S(1)}, u32[]{:S(2)}, u32[]{:S(2)}) collective-permute-start(bf16[224,1024]{1,0:T(8,128)(2,1)} %add_convert_fusion.1), channel_id=1, source_target_pairs={{0,4},{2,6},{4,0},{6,2},{8,12},{10,14},{12,8},{14,10},{16,20},{18,... | collective-permute-start | bytes 1376264 | tf_op jit(solution)/shard_map/ppermute | solution.py:432
  92.7 20.8 %collective-permute-start.12 = (bf16[224,1024]{1,0:T(8,128)(2,1)}, bf16[224,1024]{1,0:T(8,128)(2,1)S(1)}, u32[]{:S(2)}, u32[]{:S(2)}) collective-permute-start(bf16[224,1024]{1,0:T(8,128)(2,1)} %add_convert_fusion.2), channel_id=1, source_target_pairs={{0,2},{2,0},{4,6},{6,4},{8,10},{10,8},{12,14},{14,12},{16,18},{18,... | collective-permute-start | bytes 1376264 | tf_op jit(solution)/shard_map/ppermute | solution.py:432
  113.5 11.3 %collective-permute-start.25 = (bf16[128,1024]{1,0:T(8,128)(2,1)}, bf16[128,1024]{1,0:T(8,128)(2,1)}, u32[]{:S(2)}, u32[]{:S(2)}) collective-permute-start(bf16[128,1024]{1,0:T(8,128)(2,1)} %get-tuple-element.139), channel_id=1, source_target_pairs={{0,1},{1,0},{2,3},{3,2},{4,5},{5,4},{6,7},{7,6},{8,9},{9,8},{10,11... | collective-permute-start | bytes 786440 | tf_op jit(solution)/shard_map/ppermute | solution.py:440
  114.0 13.2 %collective-permute-start.33 = (bf16[128,1024]{1,0:T(8,128)(2,1)}, bf16[128,1024]{1,0:T(8,128)(2,1)}, u32[]{:S(2)}, u32[]{:S(2)}) collective-permute-start(bf16[128,1024]{1,0:T(8,128)(2,1)} %get-tuple-element.166), channel_id=1, source_target_pairs={{0,1},{1,0},{2,3},{3,2},{4,5},{5,4},{6,7},{7,6},{8,9},{9,8},{10,11... | collective-permute-start | bytes 786440 | tf_op jit(solution)/shard_map/ppermute | solution.py:440
  119.0 55.6 %all-to-all-start.2 = ((bf16[4,128,1024]{2,1,0:T(8,128)(2,1)}), bf16[4,128,1024]{2,1,0:T(8,128)(2,1)S(1)}, u32[]{:S(2)}, u32[]{:S(2)}) async-start(bf16[4,128,1024]{2,1,0:T(8,128)(2,1)} %combine.1), calls=%async_computation.2 | async-start | bytes 2097152 | tf_op jit(solution)/shard_map/all_to_all | solution.py:454
  123.6 5.7 %collective-permute-start.31 = (bf16[128,1024]{1,0:T(8,128)(2,1)}, bf16[128,1024]{1,0:T(8,128)(2,1)S(1)}, u32[]{:S(2)}, u32[]{:S(2)}) collective-permute-start(bf16[128,1024]{1,0:T(8,128)(2,1)} %get-tuple-element.160), channel_id=1, source_target_pairs={{0,1},{1,0},{2,3},{3,2},{4,5},{5,4},{6,7},{7,6},{8,9},{9,8},{10,11... | collective-permute-start | bytes 786440 | tf_op jit(solution)/shard_map/ppermute | solution.py:440
  124.7 11.8 %collective-permute-start.24 = (bf16[128,1024]{1,0:T(8,128)(2,1)}, bf16[128,1024]{1,0:T(8,128)(2,1)S(1)}, u32[]{:S(2)}, u32[]{:S(2)}) collective-permute-start(bf16[128,1024]{1,0:T(8,128)(2,1)} %get-tuple-element.133), channel_id=1, source_target_pairs={{0,1},{1,0},{2,3},{3,2},{4,5},{5,4},{6,7},{7,6},{8,9},{9,8},{10,11... | collective-permute-start | bytes 786440 | tf_op jit(solution)/shard_map/ppermute | solution.py:440
  125.9 8.5 %collective-permute-start.26 = (bf16[128,1024]{1,0:T(8,128)(2,1)S(1)}, bf16[128,1024]{1,0:T(8,128)(2,1)S(1)}, u32[]{:S(2)}, u32[]{:S(2)}) collective-permute-start(bf16[128,1024]{1,0:T(8,128)(2,1)S(1)} %add_convert_fusion.7), channel_id=1, source_target_pairs={{0,6},{2,4},{4,2},{6,0},{8,14},{10,12},{12,10},{14,8},{16,22},{18,... | collective-permute-start | bytes 786440 | tf_op jit(solution)/shard_map/ppermute | solution.py:432
  128.3 12.8 %collective-permute-start.34 = (bf16[128,1024]{1,0:T(8,128)(2,1)S(1)}, bf16[128,1024]{1,0:T(8,128)(2,1)S(1)}, u32[]{:S(2)}, u32[]{:S(2)}) collective-permute-start(bf16[128,1024]{1,0:T(8,128)(2,1)S(1)} %add_convert_fusion.5), channel_id=1, source_target_pairs={{0,4},{2,6},{4,0},{6,2},{8,12},{10,14},{12,8},{14,10},{16,20},{18,... | collective-permute-start | bytes 786440 | tf_op jit(solution)/shard_map/ppermute | solution.py:432
  129.4 11.7 %collective-permute-start.32 = (bf16[128,1024]{1,0:T(8,128)(2,1)S(1)}, bf16[128,1024]{1,0:T(8,128)(2,1)S(1)}, u32[]{:S(2)}, u32[]{:S(2)}) collective-permute-start(bf16[128,1024]{1,0:T(8,128)(2,1)S(1)} %add_convert_fusion.6), channel_id=1, source_target_pairs={{0,2},{2,0},{4,6},{6,4},{8,10},{10,8},{12,14},{14,12},{16,18},{18,... | collective-permute-start | bytes 786440 | tf_op jit(solution)/shard_map/ppermute | solution.py:432
  134.3 3.3 %collective-permute-start.30 = (bf16[112,1024]{1,0:T(8,128)(2,1)S(1)}, bf16[112,1024]{1,0:T(8,128)(2,1)S(1)}, u32[]{:S(2)}, u32[]{:S(2)}) collective-permute-start(bf16[112,1024]{1,0:T(8,128)(2,1)S(1)} %copy-done.34), channel_id=1, source_target_pairs={{0,1},{1,0},{2,3},{3,2},{4,5},{5,4},{6,7},{7,6},{8,9},{9,8},{10,11... | collective-permute-start | bytes 688136 | tf_op jit(solution)/shard_map/ppermute | solution.py:440
  136.6 1.6 collective-permute-start.29
  136.6 2.9 %collective-permute-start.28 = (bf16[112,1024]{1,0:T(8,128)(2,1)S(1)}, bf16[112,1024]{1,0:T(8,128)(2,1)S(1)}, u32[]{:S(2)}, u32[]{:S(2)}) collective-permute-start(bf16[112,1024]{1,0:T(8,128)(2,1)S(1)} %copy-done.32), channel_id=1, source_target_pairs={{0,1},{1,0},{2,3},{3,2},{4,5},{5,4},{6,7},{7,6},{8,9},{9,8},{10,11... | collective-permute-start | bytes 688136 | tf_op jit(solution)/shard_map/ppermute | solution.py:440
  137.6 3.0 %collective-permute-start.27 = (bf16[112,1024]{1,0:T(8,128)(2,1)S(1)}, bf16[112,1024]{1,0:T(8,128)(2,1)S(1)}, u32[]{:S(2)}, u32[]{:S(2)}) collective-permute-start(bf16[112,1024]{1,0:T(8,128)(2,1)S(1)} %copy-done.31), channel_id=1, source_target_pairs={{0,1},{1,0},{2,3},{3,2},{4,5},{5,4},{6,7},{7,6},{8,9},{9,8},{10,11... | collective-permute-start | bytes 688136 | tf_op jit(solution)/shard_map/ppermute | solution.py:440
  138.1 8.2 %collective-permute-start.37 = (bf16[112,1024]{1,0:T(8,128)(2,1)S(1)}, bf16[112,1024]{1,0:T(8,128)(2,1)S(1)}, u32[]{:S(2)}, u32[]{:S(2)}) collective-permute-start(bf16[112,1024]{1,0:T(8,128)(2,1)S(1)} %add_convert_fusion.9), channel_id=1, source_target_pairs={{0,6},{2,4},{4,2},{6,0},{8,14},{10,12},{12,10},{14,8},{16,22},{18,... | collective-permute-start | bytes 688136 | tf_op jit(solution)/shard_map/ppermute | solution.py:432
  139.6 11.9 %collective-permute-start.36 = (bf16[112,1024]{1,0:T(8,128)(2,1)S(1)}, bf16[112,1024]{1,0:T(8,128)(2,1)S(1)}, u32[]{:S(2)}, u32[]{:S(2)}) collective-permute-start(bf16[112,1024]{1,0:T(8,128)(2,1)S(1)} %add_convert_fusion.10), channel_id=1, source_target_pairs={{0,4},{2,6},{4,0},{6,2},{8,12},{10,14},{12,8},{14,10},{16,20},{18,... | collective-permute-start | bytes 688136 | tf_op jit(solution)/shard_map/ppermute | solution.py:432
  140.6 10.8 %collective-permute-start.35 = (bf16[112,1024]{1,0:T(8,128)(2,1)S(1)}, bf16[112,1024]{1,0:T(8,128)(2,1)S(1)}, u32[]{:S(2)}, u32[]{:S(2)}) collective-permute-start(bf16[112,1024]{1,0:T(8,128)(2,1)S(1)} %add_convert_fusion.11), channel_id=1, source_target_pairs={{0,2},{2,0},{4,6},{6,4},{8,10},{10,8},{12,14},{14,12},{16,18},{18,... | collective-permute-start | bytes 688136 | tf_op jit(solution)/shard_map/ppermute | solution.py:432
  144.1 22.9 %collective-permute-start.39 = (bf16[144,1024]{1,0:T(8,128)(2,1)S(1)}, bf16[144,1024]{1,0:T(8,128)(2,1)S(1)}, u32[]{:S(2)}, u32[]{:S(2)}) collective-permute-start(bf16[144,1024]{1,0:T(8,128)(2,1)S(1)} %get-tuple-element.178), channel_id=1, source_target_pairs={{0,16},{2,18},{4,20},{6,22},{8,24},{10,26},{12,28},{14,30},{16,0},... | collective-permute-start | bytes 884744 | tf_op jit(solution)/shard_map/ppermute | solution.py:425
  146.3 25.7 %collective-permute-start.40 = (bf16[144,1024]{1,0:T(8,128)(2,1)S(1)}, bf16[144,1024]{1,0:T(8,128)(2,1)S(1)}, u32[]{:S(2)}, u32[]{:S(2)}) collective-permute-start(bf16[144,1024]{1,0:T(8,128)(2,1)S(1)} %get-tuple-element.179), channel_id=1, source_target_pairs={{0,8},{2,10},{4,12},{6,14},{8,16},{10,18},{12,20},{14,22},{16,24},... | collective-permute-start | bytes 884744 | tf_op jit(solution)/shard_map/ppermute | solution.py:425
  153.1 19.9 %collective-permute-start.38 = (bf16[144,1024]{1,0:T(8,128)(2,1)S(1)}, bf16[144,1024]{1,0:T(8,128)(2,1)S(1)}, u32[]{:S(2)}, u32[]{:S(2)}) collective-permute-start(bf16[144,1024]{1,0:T(8,128)(2,1)S(1)} %get-tuple-element.177), channel_id=1, source_target_pairs={{0,24},{2,26},{4,28},{6,30},{8,0},{10,2},{12,4},{14,6},{16,8},{18,... | collective-permute-start | bytes 884744 | tf_op jit(solution)/shard_map/ppermute | solution.py:425
  (31 other events, 201.6 us)

commit v5 on v4

--- a/solution.py
+++ b/solution.py
@@ -10,7 +10,7 @@
 PLANE = 4
 CHUNKS = 1
 RETURNS = 2
-BLOCKS = 2
+BLOCKS = 4
 TAIL = 16
 VMEM_LIMIT = 56 * 1024 * 1024
 SMALL_LIMIT = 16 * 1024 * 1024

time: 179 us -> 183 us (1.022)
  the two profiles are of different devices: /device:TPU:9 before, /device:TPU:0 now
where the time goes in v5:
time: 183 us; the launch traced here: 179 us
  Pallas kernels  66.4 us (36%)
  starting transfers between devices  49.5 us (27%)
  waiting for transfers between devices  45 us (25%)
  other arithmetic  9.81 us (5%)
  local copies, waits for them, and re-layouts  6.94 us (4%)
    pallas_call x9, Pallas kernels, call(): pl.pallas_call(kernel, out_shape=outs, in_specs=specs, out_specs=out_spec...  66.4 us
    all_to_all x3, waiting for transfers between devices, outer_exchange(): lax.all_to_all(value, 'expert', split_axis=0, concat_axis=0, axis_index_g...  21.1 us
    ppermute x15, starting transfers between devices, inner_send(): return lax.ppermute(value, 'expert', [(e, e ^ q) for e in range(groups)])  17.8 us
    ppermute x6, starting transfers between devices, outer_send(): lax.ppermute(value, 'expert', [(e, (e // pn + s) % zn * pn + e % pn) for...  15.3 us
    ppermute x6, waiting for transfers between devices, outer_send(): lax.ppermute(value, 'expert', [(e, (e // pn + s) % zn * pn + e % pn) for...  12.7 us
    all_to_all x3, starting transfers between devices, outer_exchange(): lax.all_to_all(value, 'expert', split_axis=0, concat_axis=0, axis_index_g...  11.9 us
    ppermute x15, waiting for transfers between devices, inner_send(): return lax.ppermute(value, 'expert', [(e, e ^ q) for e in range(groups)])  10.2 us
    convert_element_type x12, other arithmetic, core_sum(): sums.append(total.astype(BF16))  5.9 us
  transfers between devices with their start and end apart: 44, of which 13 were waited for; matrix products, arithmetic and copies ran while one was open for 6% of the time, Pallas kernels for 37%

profile of v5, /device:TPU:0, one launch (start us, length us, event | category | flops | bytes accessed | tf_op | source)
XLA Modules:
  0.0 179.2 jit_solution(10635008843904939896)
XLA Ops:
  0.6 3.1 %collective-permute-start = (bf16[128,1024]{1,0:T(8,128)(2,1)}, bf16[128,1024]{1,0:T(8,128)(2,1)S(1)}, u32[]{:S(2)}, u32[]{:S(2)}) collective-permute-start(bf16[128,1024]{1,0:T(8,128)(2,1)} %refs_0_.1), channel_id=1, source_target_pairs={{0,8},{2,10},{4,12},{6,14},{8,16},{10,18},{12,20},{14,22},{16,24},... | collective-permute-start | bytes 786440 | tf_op jit(solution)/shard_map/ppermute | solution.py:425
  3.7 2.6 %collective-permute-start.1 = (bf16[128,1024]{1,0:T(8,128)(2,1)}, bf16[128,1024]{1,0:T(8,128)(2,1)S(1)}, u32[]{:S(2)}, u32[]{:S(2)}) collective-permute-start(bf16[128,1024]{1,0:T(8,128)(2,1)} %refs_0_.1), channel_id=1, source_target_pairs={{0,16},{2,18},{4,20},{6,22},{8,24},{10,26},{12,28},{14,30},{16,0},... | collective-permute-start | bytes 786440 | tf_op jit(solution)/shard_map/ppermute | solution.py:425
  6.3 1.3 collective-permute-start.2
  9.1 2.0 %broadcast_in_dim.5 = bf16[4,128,1024]{2,1,0:T(8,128)(2,1)} broadcast(bf16[128,1024]{1,0:T(8,128)(2,1)} %param.11), dimensions={1,2} | broadcast | bytes 1310720 | tf_op jit(solution)/shard_map/broadcast_in_dim | solution.py:464
  11.8 3.3 %all-to-all-start = ((f32[4,16,128]{2,1,0:T(8,128)}), f32[4,16,128]{2,1,0:T(8,128)S(1)}, u32[]{:S(2)}, u32[]{:S(2)}) async-start(f32[4,16,128]{2,1,0:T(8,128)} %broadcast_in_dim.4), calls=%async_computation | async-start | bytes 65536 | tf_op jit(solution)/shard_map/all_to_all | solution.py:454
  15.1 8.8 %collective-permute-done.1.refs_2_ = bf16[128,1024]{1,0:T(8,128)(2,1)S(1)} collective-permute-done((bf16[128,1024]{1,0:T(8,128)(2,1)}, bf16[128,1024]{1,0:T(8,128)(2,1)S(1)}, u32[]{:S(2)}, u32[]{:S(2)}) %collective-permute-start.1) | collective-permute-done | bytes 262176 | tf_op jit(solution)/shard_map/ppermute | solution.py:425
  23.9 0.7 copy-done.3
  24.6 5.3 %all-to-all-done.meta = f32[4,16,128]{2,1,0:T(8,128)S(1)} async-done(((f32[4,16,128]{2,1,0:T(8,128)}), f32[4,16,128]{2,1,0:T(8,128)S(1)}, u32[]{:S(2)}, u32[]{:S(2)}) %all-to-all-start) | async-done | bytes 32800 | tf_op jit(solution)/shard_map/all_to_all | solution.py:454
  29.9 3.5 %all-to-all-start.1 = ((bf16[4,128,1024]{2,1,0:T(8,128)(2,1)}), bf16[4,128,1024]{2,1,0:T(8,128)(2,1)S(1)}, u32[]{:S(2)}, u32[]{:S(2)}) async-start(bf16[4,128,1024]{2,1,0:T(8,128)(2,1)} %broadcast_in_dim.5), calls=%async_computation.1 | async-start | bytes 2097152 | tf_op jit(solution)/shard_map/all_to_all | solution.py:454
  33.4 0.9 copy-done.4
  34.4 3.3 %pack_gates.1 = (bf16[240,1024]{1,0:T(8,128)(2,1)S(1)}, bf16[240,1024]{1,0:T(8,128)(2,1)}, bf16[240,1024]{1,0:T(8,128)(2,1)}, bf16[240,1024]{1,0:T(8,128)(2,1)}, bf16[896,512]{1,0:T(8,128)(2,1)S(1)}) custom-call(s32[4]{0:T(128)S(1)} %pad_add_fusion.info, f32[4,16,128]{2,1,0:T(8,128)S(1)} %all-to-all-done.meta, bf16[128,1024]{1,0:T(8,128)(2,1)S(1)} %copy-done.2, ...), custom_call_target="tpu_custom_call" | custom-call | flops 1024 | bytes 1024 | tf_op jit(solution)/shard_map/pack_gates/pallas_call | solution.py:43
  37.7 2.5 %collective-permute-start.5 = (bf16[240,1024]{1,0:T(8,128)(2,1)}, bf16[240,1024]{1,0:T(8,128)(2,1)}, u32[]{:S(2)}, u32[]{:S(2)}) collective-permute-start(bf16[240,1024]{1,0:T(8,128)(2,1)} %get-tuple-element.97), channel_id=1, source_target_pairs={{0,6},{2,4},{4,2},{6,0},{8,14},{10,12},{12,10},{14,8},{16,22},{18,... | collective-permute-start | bytes 1474568 | tf_op jit(solution)/shard_map/ppermute | solution.py:432
  41.3 2.2 %route.1 = (bf16[256,448]{1,0:T(8,128)(2,1)S(1)}, bf16[256,448]{1,0:T(8,128)(2,1)S(1)}) custom-call(s32[4]{0:T(128)S(1)} %pad_add_fusion.info, f32[4,16,128]{2,1,0:T(8,128)S(1)} %all-to-all-done.meta), custom_call_target="tpu_custom_call" | custom-call | flops 1024 | bytes 1024 | tf_op jit(solution)/shard_map/route/pallas_call | solution.py:43
  43.5 15.8 %all-to-all-done.1.source = bf16[4,128,1024]{2,1,0:T(8,128)(2,1)S(1)} async-done(((bf16[4,128,1024]{2,1,0:T(8,128)(2,1)}), bf16[4,128,1024]{2,1,0:T(8,128)(2,1)S(1)}, u32[]{:S(2)}, u32[]{:S(2)}) %all-to-all-start.1) | async-done | bytes 1048608 | tf_op jit(solution)/shard_map/all_to_all | solution.py:454
  59.3 2.0 %pack.1 = (bf16[224,1024]{1,0:T(8,128)(2,1)S(1)}, bf16[224,1024]{1,0:T(8,128)(2,1)S(1)}, bf16[224,1024]{1,0:T(8,128)(2,1)S(1)}, bf16[224,1024]{1,0:T(8,128)(2,1)S(1)}) custom-call(s32[4]{0:T(128)S(1)} %pad_add_fusion.info, bf16[896,512]{1,0:T(8,128)(2,1)S(1)} %get-tuple-element.101.sel, bf16[4,128,1024]{2,1,0:T(8,128)(2,1)S(1)} %all-to-all-done.1.source), custom_call_target="tpu_custom_call" | custom-call | flops 1024 | bytes 1024 | tf_op jit(solution)/shard_map/pack/pallas_call | solution.py:43
  61.4 1.0 collective-permute-done.4.refs_2_
  63.0 1.8 %collective-permute-start.19 = (bf16[224,1024]{1,0:T(8,128)(2,1)S(1)}, bf16[224,1024]{1,0:T(8,128)(2,1)S(1)}, u32[]{:S(2)}, u32[]{:S(2)}) collective-permute-start(bf16[224,1024]{1,0:T(8,128)(2,1)S(1)} %get-tuple-element.107), channel_id=1, source_target_pairs={{0,6},{2,4},{4,2},{6,0},{8,14},{10,12},{12,10},{14,8},{16,22},{18,... | collective-permute-start | bytes 1376264 | tf_op jit(solution)/shard_map/ppermute | solution.py:432
  64.8 1.1 collective-permute-start.18
  67.3 0.8 copy-done.10
  68.2 16.5 %expert_forward.1 = (bf16[224,1024]{1,0:T(8,128)(2,1)}, bf16[224,1024]{1,0:T(8,128)(2,1)}, bf16[224,1024]{1,0:T(8,128)(2,1)}, bf16[224,1024]{1,0:T(8,128)(2,1)},...) custom-call(s32[4]{0:T(128)} %copy-done.5, ...), custom_call_target="tpu_custom_call" | custom-call | flops 1024 | bytes 1024 | tf_op jit(solution)/shard_map/expert_forward/pallas_call | solution.py:43
  85.3 1.3 collective-permute-done.18.refs_2_.refs_10_
  87.2 1.2 add_convert_fusion
  88.9 1.0 add_convert_fusion.1
  90.1 1.2 add_convert_fusion.2
  91.2 1.7 collective-permute-start.16
  93.0 1.2 collective-permute-start.14
  95.0 0.7 copy-done.16
  95.8 19.1 %expert_backward.1 = (bf16[112,1024]{1,0:T(8,128)(2,1)}, bf16[112,1024]{1,0:T(8,128)(2,1)}, bf16[112,1024]{1,0:T(8,128)(2,1)}, bf16[112,1024]{1,0:T(8,128)(2,1)}...) custom-call(s32[4]{0:T(128)} %copy-done.5, ...), custom_call_target="tpu_custom_call" | custom-call | flops 1024 | bytes 1024 | tf_op jit(solution)/shard_map/expert_backward/pallas_call | solution.py:43
  115.5 4.9 %combine.1 = bf16[4,128,1024]{2,1,0:T(8,128)(2,1)} custom-call(s32[4]{0:T(128)S(1)} %copy-done.6, bf16[256,448]{1,0:T(8,128)(2,1)S(1)} %get-tuple-element.99.refs_0_.chosen, bf16[256,448]{1,0:T(8,128)(2,1)S(1)} %get-tuple-element.100.refs_1_.chosen, bf16[224,1024]{1,0:T(8,128)(2,1)S(1)} %add_convert_fusion.3.refs_2_, ...), custom_call_target="tpu_custom_call" | custom-call | flops 1024 | bytes 1024 | tf_op jit(solution)/shard_map/combine/pallas_call | solution.py:43
  120.4 5.2 %all-to-all-start.2 = ((bf16[4,128,1024]{2,1,0:T(8,128)(2,1)}), bf16[4,128,1024]{2,1,0:T(8,128)(2,1)S(1)}, u32[]{:S(2)}, u32[]{:S(2)}) async-start(bf16[4,128,1024]{2,1,0:T(8,128)(2,1)} %combine.1), calls=%async_computation.2 | async-start | bytes 2097152 | tf_op jit(solution)/shard_map/all_to_all | solution.py:454
  126.2 1.0 add_convert_fusion.7
  127.3 1.8 collective-permute-start.26
  129.1 1.0 add_convert_fusion.5
  130.1 1.3 collective-permute-start.34
  132.1 5.4 %collective-permute-done.26.refs_3_ = bf16[128,1024]{1,0:T(8,128)(2,1)S(1)} collective-permute-done((bf16[128,1024]{1,0:T(8,128)(2,1)S(1)}, bf16[128,1024]{1,0:T(8,128)(2,1)S(1)}, u32[]{:S(2)}, u32[]{:S(2)}) %collective-permute-start.26) | collective-permute-done | bytes 262176 | tf_op jit(solution)/shard_map/ppermute | solution.py:432
  138.2 0.7 collective-permute-done.30
  139.3 1.7 collective-permute-start.37
  141.1 1.3 collective-permute-start.36
  143.1 3.0 %combine_far.1 = (bf16[144,1024]{1,0:T(8,128)(2,1)S(1)}, bf16[144,1024]{1,0:T(8,128)(2,1)S(1)}, bf16[16,512]{1,0:T(8,128)(2,1)S(1)}) custom-call(s32[4]{0:T(128)S(1)} %copy-done.6, f32[4,16,128]{2,1,0:T(8,128)S(1)} %all-to-all-done.meta, bf16[896,512]{1,0:T(8,128)(2,1)S(1)} %get-tuple-element.101.sel, ...), custom_call_target="tpu_custom_call" | custom-call | flops 1024 | bytes 1024 | tf_op jit(solution)/shard_map/combine_far/pallas_call | solution.py:43
  146.1 3.0 %collective-permute-start.39 = (bf16[144,1024]{1,0:T(8,128)(2,1)S(1)}, bf16[144,1024]{1,0:T(8,128)(2,1)S(1)}, u32[]{:S(2)}, u32[]{:S(2)}) collective-permute-start(bf16[144,1024]{1,0:T(8,128)(2,1)S(1)} %get-tuple-element.178), channel_id=1, source_target_pairs={{0,16},{2,18},{4,20},{6,22},{8,24},{10,26},{12,28},{14,30},{16,0},... | collective-permute-start | bytes 884744 | tf_op jit(solution)/shard_map/ppermute | solution.py:425
  149.1 1.5 collective-permute-start.40
  150.6 2.3 %collective-permute-done.36.refs_2_ = bf16[112,1024]{1,0:T(8,128)(2,1)S(1)} collective-permute-done((bf16[112,1024]{1,0:T(8,128)(2,1)S(1)}, bf16[112,1024]{1,0:T(8,128)(2,1)S(1)}, u32[]{:S(2)}, u32[]{:S(2)}) %collective-permute-start.36) | collective-permute-done | bytes 229408 | tf_op jit(solution)/shard_map/ppermute | solution.py:432
  153.0 1.6 combine_near.1
  154.6 3.9 %collective-permute-start.38 = (bf16[144,1024]{1,0:T(8,128)(2,1)S(1)}, bf16[144,1024]{1,0:T(8,128)(2,1)S(1)}, u32[]{:S(2)}, u32[]{:S(2)}) collective-permute-start(bf16[144,1024]{1,0:T(8,128)(2,1)S(1)} %get-tuple-element.177), channel_id=1, source_target_pairs={{0,24},{2,26},{4,28},{6,30},{8,0},{10,2},{12,4},{14,6},{16,8},{18,... | collective-permute-start | bytes 884744 | tf_op jit(solution)/shard_map/ppermute | solution.py:425
  158.5 13.9 %expert_weights.1 = (bf16[1,2,704,2048]{3,2,1,0:T(8,128)(2,1)}, bf16[1,704,2048]{2,1,0:T(8,128)(2,1)}) custom-call(s32[4]{0:T(128)} %copy-done.5, bf16[240,1024]{1,0:T(8,128)(2,1)} %copy-done, bf16[240,1024]{1,0:T(8,128)(2,1)} %collective-permute-done.3.refs_1_, bf16[240,1024]{1,0:T(8,128)(2,1)} %collective-permute-done.4.refs_2_, ...), custom_call_target="tpu_custom_call" | custom-call | flops 1024 | bytes 1024 | tf_op jit(solution)/shard_map/expert_weights/pallas_call | solution.py:43
  172.4 3.9 %collective-permute-done.38 = bf16[144,1024]{1,0:T(8,128)(2,1)S(1)} collective-permute-done((bf16[144,1024]{1,0:T(8,128)(2,1)S(1)}, bf16[144,1024]{1,0:T(8,128)(2,1)S(1)}, u32[]{:S(2)}, u32[]{:S(2)}) %collective-permute-start.38) | collective-permute-done | bytes 294944 | tf_op jit(solution)/shard_map/ppermute | solution.py:425
  176.9 0.9 add_convert_fusion.4
  178.0 0.8 subtract_convert_fusion
  (141 shorter events, 12.5 us)
Async XLA Ops:
  0.6 14.4 %collective-permute-start = (bf16[128,1024]{1,0:T(8,128)(2,1)}, bf16[128,1024]{1,0:T(8,128)(2,1)S(1)}, u32[]{:S(2)}, u32[]{:S(2)}) collective-permute-start(bf16[128,1024]{1,0:T(8,128)(2,1)} %refs_0_.1), channel_id=1, source_target_pairs={{0,8},{2,10},{4,12},{6,14},{8,16},{10,18},{12,20},{14,22},{16,24},... | collective-permute-start | bytes 786440 | tf_op jit(solution)/shard_map/ppermute | solution.py:425
  3.7 20.1 %collective-permute-start.1 = (bf16[128,1024]{1,0:T(8,128)(2,1)}, bf16[128,1024]{1,0:T(8,128)(2,1)S(1)}, u32[]{:S(2)}, u32[]{:S(2)}) collective-permute-start(bf16[128,1024]{1,0:T(8,128)(2,1)} %refs_0_.1), channel_id=1, source_target_pairs={{0,16},{2,18},{4,20},{6,22},{8,24},{10,26},{12,28},{14,30},{16,0},... | collective-permute-start | bytes 786440 | tf_op jit(solution)/shard_map/ppermute | solution.py:425
  6.3 17.6 %collective-permute-start.2 = (bf16[128,1024]{1,0:T(8,128)(2,1)}, bf16[128,1024]{1,0:T(8,128)(2,1)S(1)}, u32[]{:S(2)}, u32[]{:S(2)}) collective-permute-start(bf16[128,1024]{1,0:T(8,128)(2,1)} %refs_0_.1), channel_id=1, source_target_pairs={{0,24},{2,26},{4,28},{6,30},{8,0},{10,2},{12,4},{14,6},{16,8},{18,... | collective-permute-start | bytes 786440 | tf_op jit(solution)/shard_map/ppermute | solution.py:425
  9.1 50.2 %copy-start.5 = (s32[4]{0:T(128)}, s32[4]{0:T(128)S(1)}, u32[]{:S(2)}) copy-start(s32[4]{0:T(128)S(1)} %pad_add_fusion.info) | copy-start | bytes 52
  11.2 22.3 %copy-start.2 = (bf16[128,1024]{1,0:T(8,128)(2,1)S(1)}, bf16[128,1024]{1,0:T(8,128)(2,1)}, u32[]{:S(2)}) copy-start(bf16[128,1024]{1,0:T(8,128)(2,1)} %refs_0_.1) | copy-start | bytes 786436
  11.8 18.1 %all-to-all-start = ((f32[4,16,128]{2,1,0:T(8,128)}), f32[4,16,128]{2,1,0:T(8,128)S(1)}, u32[]{:S(2)}, u32[]{:S(2)}) async-start(f32[4,16,128]{2,1,0:T(8,128)} %broadcast_in_dim.4), calls=%async_computation | async-start | bytes 65536 | tf_op jit(solution)/shard_map/all_to_all | solution.py:454
  29.9 29.4 %all-to-all-start.1 = ((bf16[4,128,1024]{2,1,0:T(8,128)(2,1)}), bf16[4,128,1024]{2,1,0:T(8,128)(2,1)S(1)}, u32[]{:S(2)}, u32[]{:S(2)}) async-start(bf16[4,128,1024]{2,1,0:T(8,128)(2,1)} %broadcast_in_dim.5), calls=%async_computation.1 | async-start | bytes 2097152 | tf_op jit(solution)/shard_map/all_to_all | solution.py:454
  37.7 28.8 %copy-start = (bf16[240,1024]{1,0:T(8,128)(2,1)}, bf16[240,1024]{1,0:T(8,128)(2,1)S(1)}, u32[]{:S(2)}) copy-start(bf16[240,1024]{1,0:T(8,128)(2,1)S(1)} %get-tuple-element.109.refs_0_) | copy-start | bytes 1474564
  37.7 23.6 %collective-permute-start.5 = (bf16[240,1024]{1,0:T(8,128)(2,1)}, bf16[240,1024]{1,0:T(8,128)(2,1)}, u32[]{:S(2)}, u32[]{:S(2)}) collective-permute-start(bf16[240,1024]{1,0:T(8,128)(2,1)} %get-tuple-element.97), channel_id=1, source_target_pairs={{0,6},{2,4},{4,2},{6,0},{8,14},{10,12},{12,10},{14,8},{16,22},{18,... | collective-permute-start | bytes 1474568 | tf_op jit(solution)/shard_map/ppermute | solution.py:432
  40.2 22.1 %collective-permute-start.4 = (bf16[240,1024]{1,0:T(8,128)(2,1)}, bf16[240,1024]{1,0:T(8,128)(2,1)}, u32[]{:S(2)}, u32[]{:S(2)}) collective-permute-start(bf16[240,1024]{1,0:T(8,128)(2,1)} %get-tuple-element.96), channel_id=1, source_target_pairs={{0,4},{2,6},{4,0},{6,2},{8,12},{10,14},{12,8},{14,10},{16,20},{18,... | collective-permute-start | bytes 1474568 | tf_op jit(solution)/shard_map/ppermute | solution.py:432
  40.8 21.7 %collective-permute-start.3 = (bf16[240,1024]{1,0:T(8,128)(2,1)}, bf16[240,1024]{1,0:T(8,128)(2,1)}, u32[]{:S(2)}, u32[]{:S(2)}) collective-permute-start(bf16[240,1024]{1,0:T(8,128)(2,1)} %get-tuple-element.95), channel_id=1, source_target_pairs={{0,2},{2,0},{4,6},{6,4},{8,10},{10,8},{12,14},{14,12},{16,18},{18,... | collective-permute-start | bytes 1474568 | tf_op jit(solution)/shard_map/ppermute | solution.py:432
  61.3 28.6 %copy-start.1 = (bf16[224,1024]{1,0:T(8,128)(2,1)}, bf16[224,1024]{1,0:T(8,128)(2,1)S(1)}, u32[]{:S(2)}) copy-start(bf16[224,1024]{1,0:T(8,128)(2,1)S(1)} %get-tuple-element.122.refs_0_.refs_8_) | copy-start | bytes 1376260
  61.3 3.5 %collective-permute-start.9 = (bf16[240,1024]{1,0:T(8,128)(2,1)}, bf16[240,1024]{1,0:T(8,128)(2,1)S(1)}, u32[]{:S(2)}, u32[]{:S(2)}) collective-permute-start(bf16[240,1024]{1,0:T(8,128)(2,1)} %collective-permute-done.5.refs_3_), channel_id=1, source_target_pairs={{0,1},{1,0},{2,3},{3,2},{4,5},{5,4},{6,7},{7,6},{8,9},{9,8},{10,11... | collective-permute-start | bytes 1474568 | tf_op jit(solution)/shard_map/ppermute | solution.py:440
  62.4 3.6 %collective-permute-start.8 = (bf16[240,1024]{1,0:T(8,128)(2,1)}, bf16[240,1024]{1,0:T(8,128)(2,1)S(1)}, u32[]{:S(2)}, u32[]{:S(2)}) collective-permute-start(bf16[240,1024]{1,0:T(8,128)(2,1)} %collective-permute-done.4.refs_2_), channel_id=1, source_target_pairs={{0,1},{1,0},{2,3},{3,2},{4,5},{5,4},{6,7},{7,6},{8,9},{9,8},{10,11... | collective-permute-start | bytes 1474568 | tf_op jit(solution)/shard_map/ppermute | solution.py:440
  62.5 4.0 %collective-permute-start.7 = (bf16[240,1024]{1,0:T(8,128)(2,1)}, bf16[240,1024]{1,0:T(8,128)(2,1)S(1)}, u32[]{:S(2)}, u32[]{:S(2)}) collective-permute-start(bf16[240,1024]{1,0:T(8,128)(2,1)} %collective-permute-done.3.refs_1_), channel_id=1, source_target_pairs={{0,1},{1,0},{2,3},{3,2},{4,5},{5,4},{6,7},{7,6},{8,9},{9,8},{10,11... | collective-permute-start | bytes 1474568 | tf_op jit(solution)/shard_map/ppermute | solution.py:440
  62.9 3.6 %collective-permute-start.6 = (bf16[240,1024]{1,0:T(8,128)(2,1)S(1)}, bf16[240,1024]{1,0:T(8,128)(2,1)S(1)}, u32[]{:S(2)}, u32[]{:S(2)}) collective-permute-start(bf16[240,1024]{1,0:T(8,128)(2,1)S(1)} %get-tuple-element.109.refs_0_), channel_id=1, source_target_pairs={{0,1},{1,0},{2,3},{3,2},{4,5},{5,4},{6,7},{7,6},{8,9},{9,8},{10,11... | collective-permute-start | bytes 1474568 | tf_op jit(solution)/shard_map/ppermute | solution.py:440
  63.0 22.2 %collective-permute-start.19 = (bf16[224,1024]{1,0:T(8,128)(2,1)S(1)}, bf16[224,1024]{1,0:T(8,128)(2,1)S(1)}, u32[]{:S(2)}, u32[]{:S(2)}) collective-permute-start(bf16[224,1024]{1,0:T(8,128)(2,1)S(1)} %get-tuple-element.107), channel_id=1, source_target_pairs={{0,6},{2,4},{4,2},{6,0},{8,14},{10,12},{12,10},{14,8},{16,22},{18,... | collective-permute-start | bytes 1376264 | tf_op jit(solution)/shard_map/ppermute | solution.py:432
  64.8 21.8 %collective-permute-start.18 = (bf16[224,1024]{1,0:T(8,128)(2,1)S(1)}, bf16[224,1024]{1,0:T(8,128)(2,1)S(1)}, u32[]{:S(2)}, u32[]{:S(2)}) collective-permute-start(bf16[224,1024]{1,0:T(8,128)(2,1)S(1)} %get-tuple-element.106), channel_id=1, source_target_pairs={{0,4},{2,6},{4,0},{6,2},{8,12},{10,14},{12,8},{14,10},{16,20},{18,... | collective-permute-start | bytes 1376264 | tf_op jit(solution)/shard_map/ppermute | solution.py:432
  66.0 20.7 %collective-permute-start.17 = (bf16[224,1024]{1,0:T(8,128)(2,1)S(1)}, bf16[224,1024]{1,0:T(8,128)(2,1)S(1)}, u32[]{:S(2)}, u32[]{:S(2)}) collective-permute-start(bf16[224,1024]{1,0:T(8,128)(2,1)S(1)} %get-tuple-element.105), channel_id=1, source_target_pairs={{0,2},{2,0},{4,6},{6,4},{8,10},{10,8},{12,14},{14,12},{16,18},{18,... | collective-permute-start | bytes 1376264 | tf_op jit(solution)/shard_map/ppermute | solution.py:432
  84.6 2.5 %collective-permute-start.15 = (bf16[224,1024]{1,0:T(8,128)(2,1)}, bf16[224,1024]{1,0:T(8,128)(2,1)S(1)}, u32[]{:S(2)}, u32[]{:S(2)}) collective-permute-start(bf16[224,1024]{1,0:T(8,128)(2,1)} %get-tuple-element.120), channel_id=1, source_target_pairs={{0,1},{1,0},{2,3},{3,2},{4,5},{5,4},{6,7},{7,6},{8,9},{9,8},{10,11... | collective-permute-start | bytes 1376264 | tf_op jit(solution)/shard_map/ppermute | solution.py:440
  84.7 3.7 %collective-permute-start.13 = (bf16[224,1024]{1,0:T(8,128)(2,1)}, bf16[224,1024]{1,0:T(8,128)(2,1)S(1)}, u32[]{:S(2)}, u32[]{:S(2)}) collective-permute-start(bf16[224,1024]{1,0:T(8,128)(2,1)} %get-tuple-element.118), channel_id=1, source_target_pairs={{0,1},{1,0},{2,3},{3,2},{4,5},{5,4},{6,7},{7,6},{8,9},{9,8},{10,11... | collective-permute-start | bytes 1376264 | tf_op jit(solution)/shard_map/ppermute | solution.py:440
  85.2 4.7 %collective-permute-start.11 = (bf16[224,1024]{1,0:T(8,128)(2,1)}, bf16[224,1024]{1,0:T(8,128)(2,1)S(1)}, u32[]{:S(2)}, u32[]{:S(2)}) collective-permute-start(bf16[224,1024]{1,0:T(8,128)(2,1)} %get-tuple-element.116), channel_id=1, source_target_pairs={{0,1},{1,0},{2,3},{3,2},{4,5},{5,4},{6,7},{7,6},{8,9},{9,8},{10,11... | collective-permute-start | bytes 1376264 | tf_op jit(solution)/shard_map/ppermute | solution.py:440
  86.6 4.6 %collective-permute-start.10 = (bf16[224,1024]{1,0:T(8,128)(2,1)}, bf16[224,1024]{1,0:T(8,128)(2,1)S(1)}, u32[]{:S(2)}, u32[]{:S(2)}) collective-permute-start(bf16[224,1024]{1,0:T(8,128)(2,1)} %get-tuple-element.114), channel_id=1, source_target_pairs={{0,1},{1,0},{2,3},{3,2},{4,5},{5,4},{6,7},{7,6},{8,9},{9,8},{10,11... | collective-permute-start | bytes 1376264 | tf_op jit(solution)/shard_map/ppermute | solution.py:440
  86.7 6.3 %collective-permute-start.23 = (bf16[224,1024]{1,0:T(8,128)(2,1)S(1)}, bf16[224,1024]{1,0:T(8,128)(2,1)S(1)}, u32[]{:S(2)}, u32[]{:S(2)}) collective-permute-start(bf16[224,1024]{1,0:T(8,128)(2,1)S(1)} %collective-permute-done.19.refs_3_.refs_11_), channel_id=1, source_target_pairs={{0,1},{1,0},{2,3},{3,2},{4,5},{5,4},{6,7},{7,6},{8,9},{9,8},{10,11... | collective-permute-start | bytes 1376264 | tf_op jit(solution)/shard_map/ppermute | solution.py:440
  87.1 7.1 %collective-permute-start.22 = (bf16[224,1024]{1,0:T(8,128)(2,1)S(1)}, bf16[224,1024]{1,0:T(8,128)(2,1)S(1)}, u32[]{:S(2)}, u32[]{:S(2)}) collective-permute-start(bf16[224,1024]{1,0:T(8,128)(2,1)S(1)} %collective-permute-done.18.refs_2_.refs_10_), channel_id=1, source_target_pairs={{0,1},{1,0},{2,3},{3,2},{4,5},{5,4},{6,7},{7,6},{8,9},{9,8},{10,11... | collective-permute-start | bytes 1376264 | tf_op jit(solution)/shard_map/ppermute | solution.py:440
  88.4 6.5 %collective-permute-start.21 = (bf16[224,1024]{1,0:T(8,128)(2,1)S(1)}, bf16[224,1024]{1,0:T(8,128)(2,1)S(1)}, u32[]{:S(2)}, u32[]{:S(2)}) collective-permute-start(bf16[224,1024]{1,0:T(8,128)(2,1)S(1)} %collective-permute-done.17.refs_1_.refs_9_), channel_id=1, source_target_pairs={{0,1},{1,0},{2,3},{3,2},{4,5},{5,4},{6,7},{7,6},{8,9},{9,8},{10,11... | collective-permute-start | bytes 1376264 | tf_op jit(solution)/shard_map/ppermute | solution.py:440
  89.9 5.0 %collective-permute-start.20 = (bf16[224,1024]{1,0:T(8,128)(2,1)S(1)}, bf16[224,1024]{1,0:T(8,128)(2,1)S(1)}, u32[]{:S(2)}, u32[]{:S(2)}) collective-permute-start(bf16[224,1024]{1,0:T(8,128)(2,1)S(1)} %get-tuple-element.122.refs_0_.refs_8_), channel_id=1, source_target_pairs={{0,1},{1,0},{2,3},{3,2},{4,5},{5,4},{6,7},{7,6},{8,9},{9,8},{10,11... | collective-permute-start | bytes 1376264 | tf_op jit(solution)/shard_map/ppermute | solution.py:440
  91.2 23.7 %collective-permute-start.16 = (bf16[224,1024]{1,0:T(8,128)(2,1)S(1)}, bf16[224,1024]{1,0:T(8,128)(2,1)S(1)}, u32[]{:S(2)}, u32[]{:S(2)}) collective-permute-start(bf16[224,1024]{1,0:T(8,128)(2,1)S(1)} %add_convert_fusion), channel_id=1, source_target_pairs={{0,6},{2,4},{4,2},{6,0},{8,14},{10,12},{12,10},{14,8},{16,22},{18,... | collective-permute-start | bytes 1376264 | tf_op jit(solution)/shard_map/ppermute | solution.py:432
  93.0 22.0 %collective-permute-start.14 = (bf16[224,1024]{1,0:T(8,128)(2,1)}, bf16[224,1024]{1,0:T(8,128)(2,1)S(1)}, u32[]{:S(2)}, u32[]{:S(2)}) collective-permute-start(bf16[224,1024]{1,0:T(8,128)(2,1)} %add_convert_fusion.1), channel_id=1, source_target_pairs={{0,4},{2,6},{4,0},{6,2},{8,12},{10,14},{12,8},{14,10},{16,20},{18,... | collective-permute-start | bytes 1376264 | tf_op jit(solution)/shard_map/ppermute | solution.py:432
  94.2 20.8 %collective-permute-start.12 = (bf16[224,1024]{1,0:T(8,128)(2,1)}, bf16[224,1024]{1,0:T(8,128)(2,1)S(1)}, u32[]{:S(2)}, u32[]{:S(2)}) collective-permute-start(bf16[224,1024]{1,0:T(8,128)(2,1)} %add_convert_fusion.2), channel_id=1, source_target_pairs={{0,2},{2,0},{4,6},{6,4},{8,10},{10,8},{12,14},{14,12},{16,18},{18,... | collective-permute-start | bytes 1376264 | tf_op jit(solution)/shard_map/ppermute | solution.py:432
  115.0 11.3 %collective-permute-start.25 = (bf16[128,1024]{1,0:T(8,128)(2,1)}, bf16[128,1024]{1,0:T(8,128)(2,1)}, u32[]{:S(2)}, u32[]{:S(2)}) collective-permute-start(bf16[128,1024]{1,0:T(8,128)(2,1)} %get-tuple-element.139), channel_id=1, source_target_pairs={{0,1},{1,0},{2,3},{3,2},{4,5},{5,4},{6,7},{7,6},{8,9},{9,8},{10,11... | collective-permute-start | bytes 786440 | tf_op jit(solution)/shard_map/ppermute | solution.py:440
  115.0 14.0 %collective-permute-start.33 = (bf16[128,1024]{1,0:T(8,128)(2,1)}, bf16[128,1024]{1,0:T(8,128)(2,1)}, u32[]{:S(2)}, u32[]{:S(2)}) collective-permute-start(bf16[128,1024]{1,0:T(8,128)(2,1)} %get-tuple-element.166), channel_id=1, source_target_pairs={{0,1},{1,0},{2,3},{3,2},{4,5},{5,4},{6,7},{7,6},{8,9},{9,8},{10,11... | collective-permute-start | bytes 786440 | tf_op jit(solution)/shard_map/ppermute | solution.py:440
  120.4 57.4 %all-to-all-start.2 = ((bf16[4,128,1024]{2,1,0:T(8,128)(2,1)}), bf16[4,128,1024]{2,1,0:T(8,128)(2,1)S(1)}, u32[]{:S(2)}, u32[]{:S(2)}) async-start(bf16[4,128,1024]{2,1,0:T(8,128)(2,1)} %combine.1), calls=%async_computation.2 | async-start | bytes 2097152 | tf_op jit(solution)/shard_map/all_to_all | solution.py:454
  125.6 5.8 %collective-permute-start.31 = (bf16[128,1024]{1,0:T(8,128)(2,1)}, bf16[128,1024]{1,0:T(8,128)(2,1)S(1)}, u32[]{:S(2)}, u32[]{:S(2)}) collective-permute-start(bf16[128,1024]{1,0:T(8,128)(2,1)} %get-tuple-element.160), channel_id=1, source_target_pairs={{0,1},{1,0},{2,3},{3,2},{4,5},{5,4},{6,7},{7,6},{8,9},{9,8},{10,11... | collective-permute-start | bytes 786440 | tf_op jit(solution)/shard_map/ppermute | solution.py:440
  125.7 11.8 %collective-permute-start.24 = (bf16[128,1024]{1,0:T(8,128)(2,1)}, bf16[128,1024]{1,0:T(8,128)(2,1)S(1)}, u32[]{:S(2)}, u32[]{:S(2)}) collective-permute-start(bf16[128,1024]{1,0:T(8,128)(2,1)} %get-tuple-element.133), channel_id=1, source_target_pairs={{0,1},{1,0},{2,3},{3,2},{4,5},{5,4},{6,7},{7,6},{8,9},{9,8},{10,11... | collective-permute-start | bytes 786440 | tf_op jit(solution)/shard_map/ppermute | solution.py:440
  127.3 10.2 %collective-permute-start.26 = (bf16[128,1024]{1,0:T(8,128)(2,1)S(1)}, bf16[128,1024]{1,0:T(8,128)(2,1)S(1)}, u32[]{:S(2)}, u32[]{:S(2)}) collective-permute-start(bf16[128,1024]{1,0:T(8,128)(2,1)S(1)} %add_convert_fusion.7), channel_id=1, source_target_pairs={{0,6},{2,4},{4,2},{6,0},{8,14},{10,12},{12,10},{14,8},{16,22},{18,... | collective-permute-start | bytes 786440 | tf_op jit(solution)/shard_map/ppermute | solution.py:432
  130.1 13.0 %collective-permute-start.34 = (bf16[128,1024]{1,0:T(8,128)(2,1)S(1)}, bf16[128,1024]{1,0:T(8,128)(2,1)S(1)}, u32[]{:S(2)}, u32[]{:S(2)}) collective-permute-start(bf16[128,1024]{1,0:T(8,128)(2,1)S(1)} %add_convert_fusion.5), channel_id=1, source_target_pairs={{0,4},{2,6},{4,0},{6,2},{8,12},{10,14},{12,8},{14,10},{16,20},{18,... | collective-permute-start | bytes 786440 | tf_op jit(solution)/shard_map/ppermute | solution.py:432
  131.5 11.7 %collective-permute-start.32 = (bf16[128,1024]{1,0:T(8,128)(2,1)S(1)}, bf16[128,1024]{1,0:T(8,128)(2,1)S(1)}, u32[]{:S(2)}, u32[]{:S(2)}) collective-permute-start(bf16[128,1024]{1,0:T(8,128)(2,1)S(1)} %add_convert_fusion.6), channel_id=1, source_target_pairs={{0,2},{2,0},{4,6},{6,4},{8,10},{10,8},{12,14},{14,12},{16,18},{18,... | collective-permute-start | bytes 786440 | tf_op jit(solution)/shard_map/ppermute | solution.py:432
  137.5 1.5 collective-permute-start.30
  137.6 1.7 collective-permute-start.29
  138.1 2.9 %collective-permute-start.28 = (bf16[112,1024]{1,0:T(8,128)(2,1)S(1)}, bf16[112,1024]{1,0:T(8,128)(2,1)S(1)}, u32[]{:S(2)}, u32[]{:S(2)}) collective-permute-start(bf16[112,1024]{1,0:T(8,128)(2,1)S(1)} %copy-done.32), channel_id=1, source_target_pairs={{0,1},{1,0},{2,3},{3,2},{4,5},{5,4},{6,7},{7,6},{8,9},{9,8},{10,11... | collective-permute-start | bytes 688136 | tf_op jit(solution)/shard_map/ppermute | solution.py:440
  138.9 3.5 %collective-permute-start.27 = (bf16[112,1024]{1,0:T(8,128)(2,1)S(1)}, bf16[112,1024]{1,0:T(8,128)(2,1)S(1)}, u32[]{:S(2)}, u32[]{:S(2)}) collective-permute-start(bf16[112,1024]{1,0:T(8,128)(2,1)S(1)} %copy-done.31), channel_id=1, source_target_pairs={{0,1},{1,0},{2,3},{3,2},{4,5},{5,4},{6,7},{7,6},{8,9},{9,8},{10,11... | collective-permute-start | bytes 688136 | tf_op jit(solution)/shard_map/ppermute | solution.py:440
  139.3 11.3 %collective-permute-start.37 = (bf16[112,1024]{1,0:T(8,128)(2,1)S(1)}, bf16[112,1024]{1,0:T(8,128)(2,1)S(1)}, u32[]{:S(2)}, u32[]{:S(2)}) collective-permute-start(bf16[112,1024]{1,0:T(8,128)(2,1)S(1)} %add_convert_fusion.9), channel_id=1, source_target_pairs={{0,6},{2,4},{4,2},{6,0},{8,14},{10,12},{12,10},{14,8},{16,22},{18,... | collective-permute-start | bytes 688136 | tf_op jit(solution)/shard_map/ppermute | solution.py:432
  141.1 11.9 %collective-permute-start.36 = (bf16[112,1024]{1,0:T(8,128)(2,1)S(1)}, bf16[112,1024]{1,0:T(8,128)(2,1)S(1)}, u32[]{:S(2)}, u32[]{:S(2)}) collective-permute-start(bf16[112,1024]{1,0:T(8,128)(2,1)S(1)} %add_convert_fusion.10), channel_id=1, source_target_pairs={{0,4},{2,6},{4,0},{6,2},{8,12},{10,14},{12,8},{14,10},{16,20},{18,... | collective-permute-start | bytes 688136 | tf_op jit(solution)/shard_map/ppermute | solution.py:432
  142.4 10.6 %collective-permute-start.35 = (bf16[112,1024]{1,0:T(8,128)(2,1)S(1)}, bf16[112,1024]{1,0:T(8,128)(2,1)S(1)}, u32[]{:S(2)}, u32[]{:S(2)}) collective-permute-start(bf16[112,1024]{1,0:T(8,128)(2,1)S(1)} %add_convert_fusion.11), channel_id=1, source_target_pairs={{0,2},{2,0},{4,6},{6,4},{8,10},{10,8},{12,14},{14,12},{16,18},{18,... | collective-permute-start | bytes 688136 | tf_op jit(solution)/shard_map/ppermute | solution.py:432
  146.1 26.2 %collective-permute-start.39 = (bf16[144,1024]{1,0:T(8,128)(2,1)S(1)}, bf16[144,1024]{1,0:T(8,128)(2,1)S(1)}, u32[]{:S(2)}, u32[]{:S(2)}) collective-permute-start(bf16[144,1024]{1,0:T(8,128)(2,1)S(1)} %get-tuple-element.178), channel_id=1, source_target_pairs={{0,16},{2,18},{4,20},{6,22},{8,24},{10,26},{12,28},{14,30},{16,0},... | collective-permute-start | bytes 884744 | tf_op jit(solution)/shard_map/ppermute | solution.py:425
  149.1 23.3 %collective-permute-start.40 = (bf16[144,1024]{1,0:T(8,128)(2,1)S(1)}, bf16[144,1024]{1,0:T(8,128)(2,1)S(1)}, u32[]{:S(2)}, u32[]{:S(2)}) collective-permute-start(bf16[144,1024]{1,0:T(8,128)(2,1)S(1)} %get-tuple-element.179), channel_id=1, source_target_pairs={{0,8},{2,10},{4,12},{6,14},{8,16},{10,18},{12,20},{14,22},{16,24},... | collective-permute-start | bytes 884744 | tf_op jit(solution)/shard_map/ppermute | solution.py:425
  154.6 21.7 %collective-permute-start.38 = (bf16[144,1024]{1,0:T(8,128)(2,1)S(1)}, bf16[144,1024]{1,0:T(8,128)(2,1)S(1)}, u32[]{:S(2)}, u32[]{:S(2)}) collective-permute-start(bf16[144,1024]{1,0:T(8,128)(2,1)S(1)} %get-tuple-element.177), channel_id=1, source_target_pairs={{0,24},{2,26},{4,28},{6,30},{8,0},{10,2},{12,4},{14,6},{16,8},{18,... | collective-permute-start | bytes 884744 | tf_op jit(solution)/shard_map/ppermute | solution.py:425
  (31 other events, 199.1 us)
